TPU v7x, 32 devices: a whole 2x2x4 slice. The times are simulated.
32 devices in a mesh: panel: 8 (over z, x), slab: 4 (over y, core).
Axes of the slice: x: 2, y: 2, z: 4, core: 2. Of those that a mesh axis runs over, the one named last changes fastest.
Arguments:
- charges: bfloat16 [262144], P(('panel', 'slab')), may hold values from -6 to 6
- target: float32 [262144], P(('panel', 'slab')), may hold values from -6 to 6
- stencil: bfloat16 [4096, 64, 256], P(('panel', 'slab')), may hold values from -0.375 to 0.375
- near_matrix: bfloat16 [4096, 4, 4096], P(('panel', 'slab')), may hold values from -0.375 to 0.375
- green: float32 [4096, 4096], P(None, ('panel', 'slab')), may hold values from 0.5 to 8
- block_dest: int32 [4096, 1], P(('panel', 'slab')), may hold values from 0 to 31; in each aligned block of 128 rows (0 to 127, 128 to 255, ...) at most 8 rows name the same one
- block_tile: int32 [4096], P(('panel', 'slab')), may hold values from 0 to 2047
- near_offset: int32 [4096, 4], P(('panel', 'slab')), may hold values from -8 to 8
Outputs:
- potentials: float32 [262144], P(('panel', 'slab'))
- gradient: float32 [262144], P(('panel', 'slab'))
Inputs may be any that keep to these rules, and one draw needn't show every extreme that they name: `block_dest`: in the 128 blocks of one device no owner is named more than 8 times; in some device's blocks one owner is named exactly 8 times.
All inputs are finite; a program needn't handle non-finite values.
Results may differ from a plain program's by a relative error of at most 0.0025.
The roundings to bfloat16 on the way count: a program that leaves them out, or rounds other values in their place, can miss the bound.
Values may be sent and summed in bfloat16 or wider, within the bound.
No kernel may reach another device: no remote copies, remote signals or barrier semaphores. Data moves between devices by JAX's collectives and lax.ppermute only.
A program may use at most 128 MiB of HBM per device.

v0:
```python
import math

import jax
import jax.numpy as jnp
from jax import lax
from jax.sharding import PartitionSpec as P

GRID = 4096
TILE = 16
REACH = 8


HIGHEST = lax.Precision.HIGHEST


def extended_2(cells, sides, width):
    for axis, dim in sides:
        count = lax.axis_size(axis)
        ends = count - 1
        head = lax.slice_in_dim(cells, 0, width, axis=dim)
        tail = lax.slice_in_dim(cells, cells.shape[dim] - width, cells.shape[dim], axis=dim)
        cells = jnp.concatenate(
            [
                lax.ppermute(tail, axis, [(i, (i + 1) % count) for i in range(ends)]),
                cells,
                lax.ppermute(head, axis, [((i + 1) % count, i) for i in range(ends)]),
            ],
            axis=dim,
        )
    return cells


def tables(size_in, size_out, modulus, direction):
    row_index = lax.broadcasted_iota(jnp.int32, (size_in, size_out), 0)
    col_index = lax.broadcasted_iota(jnp.int32, (size_in, size_out), 1)
    phase_angle = (
        direction * 2.0 * math.pi / modulus * (row_index * col_index % modulus).astype(jnp.float32)
    )
    return (jnp.cos(phase_angle), jnp.sin(phase_angle))


def rotate(stacked, formula, cosine, sine):
    with_cos = jnp.einsum(formula, stacked, cosine, precision=HIGHEST)
    with_sin = jnp.einsum(formula, stacked, sine, precision=HIGHEST)
    return jnp.stack([with_cos[0] - with_sin[1], with_sin[0] + with_cos[1]])


def twiddle(stacked, cosine, sine):
    return jnp.stack(
        [stacked[0] * cosine - stacked[1] * sine, stacked[0] * sine + stacked[1] * cosine]
    )


def convolve(grid_cells, green_local, devices, regroup):
    row_count = grid_cells.shape[0]
    width = GRID // devices
    shaped = grid_cells.reshape(row_count, width, devices)
    inner_cos, inner_sin = tables(width, width, width, -1.0)
    outer_cos, outer_sin = tables(devices, devices, devices, -1.0)
    local_cos, local_sin = tables(row_count, row_count, row_count, -1.0)
    twist_cos, twist_sin = tables(width, devices, GRID, -1.0)
    spin_cos, spin_sin = tables(row_count, devices, GRID, -1.0)
    partial_value = jnp.stack(
        [
            jnp.einsum("rab,ak->rkb", shaped, inner_cos, precision=HIGHEST),
            jnp.einsum("rab,ak->rkb", shaped, inner_sin, precision=HIGHEST),
        ]
    )
    partial_value = twiddle(partial_value, twist_cos[None], twist_sin[None])
    spectrum = rotate(partial_value, "zrab,bk->zrka", outer_cos, outer_sin)
    spectrum = regroup(spectrum)
    spectrum = rotate(spectrum, "zrsc,sk->zrkc", outer_cos, outer_sin)
    spectrum = twiddle(spectrum, spin_cos[:, :, None], spin_sin[:, :, None])
    spectrum = rotate(spectrum, "zrkc,rm->zmkc", local_cos, local_sin)
    spectrum = spectrum * green_local.reshape(row_count, devices, width)[None]
    spectrum = rotate(spectrum, "zmkc,mq->zqkc", local_cos, -local_sin)
    spectrum = twiddle(spectrum, spin_cos[:, :, None], -spin_sin[:, :, None])
    spectrum = rotate(spectrum, "zqkc,ks->zqsc", outer_cos, -outer_sin)
    spectrum = regroup(spectrum)
    spectrum = rotate(spectrum, "zrka,kq->zrqa", outer_cos, -outer_sin)
    spectrum = twiddle(spectrum, twist_cos.T[None], -twist_sin.T[None])
    real_out = jnp.einsum("rqk,kp->rpq", spectrum[0], inner_cos, precision=HIGHEST)
    real_out = real_out + jnp.einsum("rqk,kp->rpq", spectrum[1], inner_sin, precision=HIGHEST)
    return real_out.reshape(row_count, GRID) * (1.0 / (GRID * GRID))


def local(charges, target, stencil, near_matrix, green, block_dest, block_tile, near_offset):
    devices = lax.axis_size(("panel", "slab"))
    blocks = stencil.shape[0]
    block_size = stencil.shape[1]
    cell_count = stencil.shape[2]
    pair_count = near_offset.shape[1]
    capacity = 2 * blocks // devices
    row_count = GRID // devices
    tile_rows = row_count // TILE
    tile_cols = GRID // TILE
    tile_total = tile_rows * tile_cols
    destination = block_dest[:, 0]
    one_hot = (destination[:, None] == jnp.arange(devices, dtype=jnp.int32)[None, :]).astype(
        jnp.int32
    )
    earlier = jnp.cumsum(one_hot, axis=0) - one_hot
    slot_index = destination * capacity + jnp.sum(earlier * one_hot, axis=1)
    tile_ids = (
        jnp.full((devices * capacity,), -1.0, jnp.float32)
        .at[slot_index]
        .set(block_tile.astype(jnp.float32))
    )

    def regroup(stacked):
        return lax.all_to_all(stacked, ("panel", "slab"), split_axis=2, concat_axis=2, tiled=True)

    def far_field(values):
        tile_values = jnp.einsum("bp,bpt->bt", values, stencil, preferred_element_type=jnp.float32)
        outgoing = (
            jnp.zeros((devices * capacity, cell_count), jnp.float32).at[slot_index].set(tile_values)
        )
        arrived, arrived_ids = (
            lax.all_to_all(
                outgoing.reshape(devices, capacity, cell_count),
                ("panel", "slab"),
                split_axis=0,
                concat_axis=0,
                tiled=True,
            ),
            lax.all_to_all(
                tile_ids.reshape(devices, capacity),
                ("panel", "slab"),
                split_axis=0,
                concat_axis=0,
                tiled=True,
            ),
        )
        where_ids = arrived_ids.reshape(-1)
        owned_tile = jnp.where(where_ids < 0.0, tile_total, where_ids.astype(jnp.int32))
        tile_sums = (
            jnp.zeros((tile_total, cell_count), jnp.float32)
            .at[owned_tile]
            .add(arrived.reshape(-1, cell_count), mode="drop")
        )
        grid_cells = (
            tile_sums.reshape(tile_rows, tile_cols, TILE, TILE)
            .transpose(0, 2, 1, 3)
            .reshape(row_count, GRID)
        )
        field = convolve(grid_cells, green, devices, regroup)
        back_tiles = field.reshape(tile_rows, TILE, tile_cols, TILE).transpose(0, 2, 1, 3)
        back_tiles = back_tiles.reshape(tile_total, cell_count).astype(jnp.bfloat16)
        returning = jnp.take(back_tiles, jnp.minimum(owned_tile, tile_total - 1), axis=0)
        returned = lax.all_to_all(
            returning.reshape(devices, capacity, cell_count),
            ("panel", "slab"),
            split_axis=0,
            concat_axis=0,
            tiled=True,
        )
        own_tiles = returned.reshape(devices * capacity, cell_count)[slot_index]
        return jnp.einsum("bpt,bt->bp", stencil, own_tiles, preferred_element_type=jnp.float32)

    couple = near_matrix.reshape(blocks, pair_count, block_size, block_size)
    positions = jnp.arange(blocks, dtype=jnp.int32)[:, None] + REACH + near_offset
    charge_blocks = charges.reshape(blocks, block_size)
    extended = extended_2(charge_blocks, ((("panel", "slab"), 0),), REACH)
    potentials = far_field(charge_blocks) + jnp.einsum(
        "bkps,bks->bp", couple, extended[positions], preferred_element_type=jnp.float32
    )
    residual = (potentials - target.reshape(blocks, block_size)).astype(jnp.bfloat16)
    terms = jnp.einsum("bkps,bp->bks", couple, residual, preferred_element_type=jnp.float32)
    extended = jnp.zeros((blocks + 2 * REACH, block_size), jnp.float32)
    extended = extended.at[positions.reshape(-1)].add(terms.reshape(-1, block_size))
    rims = jnp.concatenate([extended[:REACH], extended[blocks + REACH :]], axis=0)
    neighbour = extended_2(rims, ((("panel", "slab"), 0),), REACH)
    own_part = extended[REACH : blocks + REACH]
    own_part = own_part.at[:REACH].add(neighbour[:REACH])
    gradient = far_field(residual) + own_part.at[blocks - REACH :].add(neighbour[3 * REACH :])
    return (potentials.reshape(-1), gradient.reshape(-1))


def solution(mesh):
    return jax.shard_map(
        local,
        mesh=mesh,
        in_specs=(
            P(("panel", "slab")),
            P(("panel", "slab")),
            P(("panel", "slab"), None, None),
            P(("panel", "slab"), None, None),
            P(None, ("panel", "slab")),
            P(("panel", "slab"), None),
            P(("panel", "slab")),
            P(("panel", "slab"), None),
        ),
        out_specs=(P(("panel", "slab")), P(("panel", "slab"))),
        check_vma=False,
    )
```

profile of v0, /device:TPU:0, one launch (start us, length us, event | category | flops | bytes accessed | tf_op | source)
XLA Modules:
  0.0 824.9 jit_solution(16676152683994728272)
XLA Ops:
  5.3 7.3 all-to-all-start
  24.1 10.3 %all-to-all-done.1 = f32[32,8,256]{2,1,0:T(8,128)S(1)} async-done(((f32[32,8,256]{2,1,0:T(8,128)}), f32[32,8,256]{2,1,0:T(8,128)S(1)}, u32[]{:S(2)}, u32[]{:S(2)}) %all-to-all-start.1) | async-done | bytes 262176 | tf_op jit(solution)/shard_map/all_to_all | solution.py:119
  41.4 13.5 %copy.152 = f32[8,16,256,16]{1,0,3,2:T(8,128)} copy(f32[8,16,256,16]{2,0,3,1:T(8,128)S(1)} %bitcast.294) | data formatting | bytes 4194304 | tf_op jit(solution)/shard_map/transpose | solution.py:143
  54.9 11.4 %reshape_reshape.6 = f32[128,128,32]{0,2,1:T(8,128)} reshape(f32[8,16,256,16]{1,0,3,2:T(8,128)} %copy.152) | data formatting | bytes 4194304 | tf_op jit(solution)/shard_map/reshape;reshape | solution.py:57
  104.4 91.3 %all-to-all-done.2 = f32[2,128,32,128]{3,1,0,2:T(8,128)} async-done(((f32[2,128,32,128]{3,1,0,2:T(8,128)}), f32[2,128,32,128]{3,1,0,2:T(8,128)}, u32[]{:S(2)}, u32[]{:S(2)}) %all-to-all-start.2) | async-done | bytes 4194336 | tf_op jit(solution)/shard_map/all_to_all | solution.py:111
  195.7 8.2 fusion.36
  203.9 8.3 %fusion.39 = f32[2,128,32,128]{3,2,1,0:T(8,128)S(1)} fusion(f32[2,128,32,128]{3,1,0,2:T(8,128)} %all-to-all-done.2), kind=kOutput, calls=%fused_computation.64 | convolution fusion | flops 402667520 | bytes 8388608 | tf_op jit(solution)/shard_map/zrsc,sk->zrkc/dot_general | solution.py:44
  267.6 7.9 copy.177
  275.5 13.0 %copy.218 = bf16[128,4,64,64]{3,2,1,0:T(8,128)(2,1)} copy(bf16[128,4,64,64]{0,3,2,1:T(8,128)(2,1)} %bitcast.293) | data formatting | bytes 8388608 | tf_op jit(solution)/shard_map/reshape | solution.py:160
  291.2 66.5 %all-to-all-done.3 = f32[2,128,32,128]{3,1,0,2:T(8,128)} async-done(((f32[2,128,32,128]{3,1,0,2:T(8,128)}), f32[2,128,32,128]{3,1,0,2:T(8,128)}, u32[]{:S(2)}, u32[]{:S(2)}) %all-to-all-start.3) | async-done | bytes 4194336 | tf_op jit(solution)/shard_map/all_to_all | solution.py:111
  357.7 8.2 fusion.48
  365.9 8.5 %fusion.51 = f32[2,128,32,128]{3,2,1,0:T(8,128)S(1)} fusion(f32[2,128,32,128]{3,1,0,2:T(8,128)} %all-to-all-done.3), kind=kOutput, calls=%fused_computation.68 | convolution fusion | flops 402668544 | bytes 8388608 | tf_op jit(solution)/shard_map/zrka,kq->zrqa/dot_general | solution.py:44
  382.6 7.4 convert_element_type.225
  390.0 10.6 %copy.174 = bf16[8,256,16,16]{1,0,3,2:T(8,128)(2,1)S(1)} copy(bf16[8,256,16,16]{2,0,3,1:T(8,128)(2,1)} %bitcast.287) | data formatting | bytes 2097152 | tf_op jit(solution)/shard_map/convert_element_type | solution.py:148
  426.3 13.7 %all_to_all.50 = f32[32,8,256]{2,1,0:T(8,128)S(1)} all-to-all(f32[32,8,256]{2,1,0:T(8,128)S(1)} %bitcast.307), channel_id=1, replica_groups=mesh['panel'=8,'slab'=4] {'panel','slab'}, dimensions={0} | all-to-all | bytes 524288 | tf_op jit(solution)/shard_map/all_to_all | solution.py:119
  450.5 14.3 %copy.179 = f32[8,16,256,16]{1,0,3,2:T(8,128)} copy(f32[8,16,256,16]{2,0,3,1:T(8,128)} %bitcast.295) | data formatting | bytes 4194304 | tf_op jit(solution)/shard_map/transpose | solution.py:143
  464.9 11.4 %reshape_reshape.7 = f32[128,128,32]{0,2,1:T(8,128)} reshape(f32[8,16,256,16]{1,0,3,2:T(8,128)} %copy.179) | data formatting | bytes 4194304 | tf_op jit(solution)/shard_map/reshape;reshape | solution.py:57
  508.1 96.0 %all_to_all.51 = f32[2,128,32,128]{3,1,0,2:T(8,128)S(1)} all-to-all(f32[2,128,32,128]{3,1,0,2:T(8,128)S(1)} %copy.184), channel_id=1, replica_groups=mesh['panel'=8,'slab'=4] {'panel','slab'}, dimensions={2} | all-to-all | bytes 8388608 | tf_op jit(solution)/shard_map/all_to_all | solution.py:111
  677.5 83.0 %all-to-all-done.7 = f32[2,128,32,128]{3,1,0,2:T(8,128)} async-done(((f32[2,128,32,128]{3,1,0,2:T(8,128)}), f32[2,128,32,128]{3,1,0,2:T(8,128)}, u32[]{:S(2)}, u32[]{:S(2)}) %all-to-all-start.7) | async-done | bytes 4194336 | tf_op jit(solution)/shard_map/all_to_all | solution.py:111
  760.5 8.2 fusion.66
  768.7 8.5 %fusion.69 = f32[2,128,32,128]{3,2,1,0:T(8,128)S(1)} fusion(f32[2,128,32,128]{3,1,0,2:T(8,128)} %all-to-all-done.7), kind=kOutput, calls=%fused_computation.74 | convolution fusion | flops 402668544 | bytes 8388608 | tf_op jit(solution)/shard_map/zrka,kq->zrqa/dot_general | solution.py:44
  785.3 7.4 convert_element_type.231
  792.8 10.6 %copy.197 = bf16[8,256,16,16]{1,0,3,2:T(8,128)(2,1)S(1)} copy(bf16[8,256,16,16]{2,0,3,1:T(8,128)(2,1)} %bitcast.288) | data formatting | bytes 2097152 | tf_op jit(solution)/shard_map/convert_element_type | solution.py:148
  811.6 8.2 all-to-all-done.8
  (174 shorter events, 289.3 us)
Async XLA Ops:
  3.0 264.4 %copy-start.11 = (s32[128]{0:T(128)}, s32[128]{0:T(128)S(1)}, u32[]{:S(2)}) copy-start(s32[128]{0:T(128)S(1)} %fusion.234) | copy-start | bytes 1540
  5.3 14.4 %all-to-all-start = ((f32[32,1,8]{2,1,0:T(1,128)}), f32[32,1,8]{2,1,0:T(1,128)S(1)}, u32[]{:S(2)}, u32[]{:S(2)}) async-start(f32[32,1,8]{2,1,0:T(1,128)} %bitcast.3), calls=%async_computation | async-start | bytes 32768 | tf_op jit(solution)/shard_map/all_to_all | solution.py:126
  19.7 14.7 %all-to-all-start.1 = ((f32[32,8,256]{2,1,0:T(8,128)}), f32[32,8,256]{2,1,0:T(8,128)S(1)}, u32[]{:S(2)}, u32[]{:S(2)}) async-start(f32[32,8,256]{2,1,0:T(8,128)} %bitcast.13), calls=%async_computation.1 | async-start | bytes 524288 | tf_op jit(solution)/shard_map/all_to_all | solution.py:119
  24.1 14.8 %copy-start.10 = (s32[256,1]{0,1:T(1,128)}, s32[256,1]{0,1:T(1,128)S(1)}, u32[]{:S(2)}) copy-start(s32[256,1]{0,1:T(1,128)S(1)} %compare_select_fusion.2) | copy-start | bytes 3076
  81.3 5.9 copy-start
  97.2 98.5 %all-to-all-start.2 = ((f32[2,128,32,128]{3,1,0,2:T(8,128)}), f32[2,128,32,128]{3,1,0,2:T(8,128)}, u32[]{:S(2)}, u32[]{:S(2)}) async-start(f32[2,128,32,128]{3,1,0,2:T(8,128)} %copy.157), calls=%async_computation.2 | async-start | bytes 8388608 | tf_op jit(solution)/shard_map/all_to_all | solution.py:111
  257.6 5.8 copy-start.7
  257.6 9.5 %copy-start.9 = (s32[128,4]{0,1:T(4,128)S(1)}, s32[128,4]{0,1:T(4,128)}, u32[]{:S(2)}) copy-start(s32[128,4]{0,1:T(4,128)} %param.21) | copy-start | bytes 6148
  257.6 100.1 %all-to-all-start.3 = ((f32[2,128,32,128]{3,1,0,2:T(8,128)}), f32[2,128,32,128]{3,1,0,2:T(8,128)}, u32[]{:S(2)}, u32[]{:S(2)}) async-start(f32[2,128,32,128]{3,1,0,2:T(8,128)} %copy.168), calls=%async_computation.3 | async-start | bytes 8388608 | tf_op jit(solution)/shard_map/all_to_all | solution.py:111
  263.5 25.7 %collective-permute-start = (bf16[8,64]{1,0:T(8,128)(2,1)S(1)}, bf16[8,64]{1,0:T(8,128)(2,1)S(1)}, u32[]{:S(2)}, u32[]{:S(2)}) collective-permute-start(bf16[8,64]{1,0:T(8,128)(2,1)S(1)} %slice.245), channel_id=1, source_target_pairs={{0,1},{1,2},{2,3},{3,4},{4,5},{5,6},{6,7},{7,8},{8,9},{9,10},{10,1... | collective-permute-start | bytes 3080 | tf_op jit(solution)/shard_map/ppermute | solution.py:24
  265.8 23.4 %collective-permute-start.1 = (bf16[8,64]{1,0:T(8,128)(2,1)S(1)}, bf16[8,64]{1,0:T(8,128)(2,1)S(1)}, u32[]{:S(2)}, u32[]{:S(2)}) collective-permute-start(bf16[8,64]{1,0:T(8,128)(2,1)S(1)} %slice.247), channel_id=1, source_target_pairs={{1,0},{2,1},{3,2},{4,3},{5,4},{6,5},{7,6},{8,7},{9,8},{10,9},{11,1... | collective-permute-start | bytes 3080 | tf_op jit(solution)/shard_map/ppermute | solution.py:26
  275.5 13.0 %copy-start.8 = (f32[8192]{0:T(1024)S(1)}, f32[8192]{0:T(1024)}, u32[]{:S(2)}) copy-start(f32[8192]{0:T(1024)} %param.15) | copy-start | bytes 98308
  405.4 14.7 %all-to-all-start.4 = ((bf16[32,8,256]{2,1,0:T(8,128)(2,1)}), bf16[32,8,256]{2,1,0:T(8,128)(2,1)S(1)}, u32[]{:S(2)}, u32[]{:S(2)}) async-start(bf16[32,8,256]{2,1,0:T(8,128)(2,1)} %select_bitcast_fusion.1), calls=%async_computation.4 | async-start | bytes 262144 | tf_op jit(solution)/shard_map/all_to_all | solution.py:150
  420.9 3.5 copy-start.6
  420.9 3.6 copy-start.3
  479.3 3.9 copy-start.2
  494.0 6.1 copy-start.1
  662.1 98.4 %all-to-all-start.7 = ((f32[2,128,32,128]{3,1,0,2:T(8,128)}), f32[2,128,32,128]{3,1,0,2:T(8,128)}, u32[]{:S(2)}, u32[]{:S(2)}) async-start(f32[2,128,32,128]{3,1,0,2:T(8,128)} %copy.191), calls=%async_computation.7 | async-start | bytes 8388608 | tf_op jit(solution)/shard_map/all_to_all | solution.py:111
  673.2 95.5 %copy-start.4 = (f32[144,64]{1,0:T(8,128)}, f32[144,64]{1,0:T(8,128)S(1)}, u32[]{:S(2)}) copy-start(f32[144,64]{1,0:T(8,128)S(1)} %scatter_custom_fusion.5) | copy-start | bytes 110596
  673.2 138.3 %collective-permute-start.2 = (f32[8,64]{1,0:T(8,128)S(1)}, f32[8,64]{1,0:T(8,128)S(1)}, u32[]{:S(2)}, u32[]{:S(2)}) collective-permute-start(f32[8,64]{1,0:T(8,128)S(1)} %get-tuple-element.62), channel_id=1, source_target_pairs={{0,1},{1,2},{2,3},{3,4},{4,5},{5,6},{6,7},{7,8},{8,9},{9,10},{10,1... | collective-permute-start | bytes 6152 | tf_op jit(solution)/shard_map/ppermute | solution.py:24
  675.5 136.1 %collective-permute-start.3 = (f32[8,64]{1,0:T(8,128)S(1)}, f32[8,64]{1,0:T(8,128)S(1)}, u32[]{:S(2)}, u32[]{:S(2)}) collective-permute-start(f32[8,64]{1,0:T(8,128)S(1)} %get-tuple-element.61), channel_id=1, source_target_pairs={{1,0},{2,1},{3,2},{4,3},{5,4},{6,5},{7,6},{8,7},{9,8},{10,9},{11,1... | collective-permute-start | bytes 6152 | tf_op jit(solution)/shard_map/ppermute | solution.py:26
  803.7 7.9 copy-start.5
  803.7 7.9 slice-start
  806.2 13.6 %all-to-all-start.8 = ((bf16[32,8,256]{2,1,0:T(8,128)(2,1)}), bf16[32,8,256]{2,1,0:T(8,128)(2,1)S(1)}, u32[]{:S(2)}, u32[]{:S(2)}) async-start(bf16[32,8,256]{2,1,0:T(8,128)(2,1)} %select_bitcast_fusion), calls=%async_computation.8 | async-start | bytes 262144 | tf_op jit(solution)/shard_map/all_to_all | solution.py:150
where the time goes:
time: 831 us; the launch traced here: 825 us
  waiting for transfers between devices  264 us (32%)
  matrix products  187 us (23%)
  local copies, waits for them, and re-layouts  184 us (22%)
  blocking collectives  110 us (13%)
  starting transfers between devices  44.1 us (5%)
  other arithmetic  35.1 us (4%)
    all_to_all x3, waiting for transfers between devices, regroup(): lax.all_to_all(stacked, ('panel', 'slab'), split_axis=2, concat_axis=2, t...  241 us
    all_to_all x1, blocking collectives, regroup(): lax.all_to_all(stacked, ('panel', 'slab'), split_axis=2, concat_axis=2, t...  96 us
    dot_general x12, matrix products, rotate(): with_sin = jnp.einsum(formula, stacked, sine, precision=HIGHEST)  73.4 us
    dot_general x12, matrix products, rotate(): with_cos = jnp.einsum(formula, stacked, cosine, precision=HIGHEST)  68 us
    convert_element_type x8, local copies, waits for them, and re-layouts, far_field(): back_tiles = back_tiles.reshape(tile_total, cell_count).astype(jnp.bfloat16)  39.5 us
    transpose x2, local copies, waits for them, and re-layouts, far_field(): grid_cells = tile_sums.reshape(tile_rows, tile_cols, TILE, TILE).transpos...  27.8 us
    another operation x4, local copies, waits for them, and re-layouts, convolve(): shaped = grid_cells.reshape(row_count, width, devices)  27.8 us
  transfers between devices with their start and end apart: 11, of which 7 were waited for; matrix products, arithmetic and copies ran while one was open for 11% of the time, Pallas kernels for 0%

commit v1 on v0

v1 whole, which is shorter than its diff:
```python
import functools
import math

import jax
import jax.numpy as jnp
import numpy as np
from jax import lax
from jax.experimental import pallas as pl
from jax.experimental.pallas import tpu as pltpu
from jax.sharding import PartitionSpec as P

REACH = 8
AXES = ("panel", "slab")
BF16 = jnp.bfloat16
F32 = jnp.float32
VMEM_BYTES = 40 * 1024 * 1024
STEP = 16


def extended_2(cells, sides, width):
    for axis, dim in sides:
        count = lax.axis_size(axis)
        ends = count - 1
        head = lax.slice_in_dim(cells, 0, width, axis=dim)
        tail = lax.slice_in_dim(cells, cells.shape[dim] - width, cells.shape[dim], axis=dim)
        cells = jnp.concatenate(
            [
                lax.ppermute(tail, axis, [(i, (i + 1) % count) for i in range(ends)]),
                cells,
                lax.ppermute(head, axis, [((i + 1) % count, i) for i in range(ends)]),
            ],
            axis=dim,
        )
    return cells


def split(table):
    high = table.astype(jnp.bfloat16)
    return np.stack([high, (table - high.astype(np.float64)).astype(jnp.bfloat16)])


class Plan:
    def __init__(self, grid, tile, devices):
        self.grid, self.tile, self.devices = grid, tile, devices
        self.tile_cols = grid // tile
        self.rows = grid // devices
        self.width = grid // devices
        self.half = self.width // 2
        self.per_mu = devices // tile
        self.kappas = self.tile_cols // 2
        self.group = max(1, min(tile, 2 * 128 // self.rows))

    def place(self, position, mu):
        part, j = divmod(position, self.width)
        device = self.per_mu * mu + part
        if j < self.half:
            return device, j, 1.0
        return self.devices - 1 - device, j - self.half, -1.0

    def kappa(self):
        out = []
        for position in range(self.kappas):
            part, j = divmod(position, self.width)
            if j >= self.half:
                j = self.half + (self.half - (j - self.half)) % self.half
            out.append(self.width * part + j)
        return np.array(out)

    def forward_table(self):
        angle = 2 * np.pi * np.outer(self.kappa(), np.arange(self.tile_cols)) / self.tile_cols
        sine = -np.sin(angle)
        sine[0] = (-1.0) ** np.arange(self.tile_cols)
        return split(np.concatenate([np.cos(angle), sine]))

    def inverse_table(self):
        angle = 2 * np.pi * np.outer(np.arange(self.tile_cols), self.kappa()) / self.tile_cols
        cosine, sine = 2 * np.cos(angle), -2 * np.sin(angle)
        cosine[:, 0] = 1.0
        sine[:, 0] = (-1.0) ** np.arange(self.tile_cols)
        return split(np.concatenate([cosine, sine], axis=1))

    def column_twiddles(self):
        angle = 2 * np.pi * np.outer(np.arange(self.tile), self.kappa()) / self.grid
        full = np.broadcast_to(angle[:, :, None], (self.tile, self.kappas, self.rows))
        return np.cos(full).astype(np.float32), np.sin(full).astype(np.float32)

    def edge_tables(self):
        n, m = self.tile, self.tile // 2
        cells = np.arange(n)
        forward, inverse = np.zeros((2 * n, 2 * n)), np.zeros((2 * n, 2 * n))
        forward[0, :n], forward[n, :n] = 1.0, (-1.0) ** cells
        inverse[:n, 0], inverse[:n, n] = 1.0, (-1.0) ** cells
        for mu in range(1, m):
            angle = 2 * np.pi * cells * mu / n
            forward[mu, :n], forward[n + mu, :n] = np.cos(angle), -np.sin(angle)
            inverse[:n, mu], inverse[:n, n + mu] = 2 * np.cos(angle), -2 * np.sin(angle)
        for nu in range(m):
            angle = 2 * np.pi * cells * (1 + 2 * nu) / (2 * n)
            forward[m + nu, n:], forward[n + m + nu, n:] = np.cos(angle), -np.sin(angle)
            inverse[n:, m + nu], inverse[n:, n + m + nu] = 2 * np.cos(angle), -2 * np.sin(angle)
        return forward.astype(np.float32), inverse.astype(np.float32)

    def spread_table(self):
        n, tile_rows = self.tile, self.rows // self.tile
        eye = np.eye(n)
        table = np.einsum("ai,cj,t->acjti", eye, eye, np.ones(tile_rows))
        return table.reshape(n * n, n * self.rows).astype(jnp.bfloat16)

    def row_tables(self):
        n = self.rows
        angle = 2 * np.pi * (np.outer(np.arange(n), np.arange(n)) % n) / n
        both = split(np.concatenate([np.cos(angle), np.sin(angle)], axis=1))
        angle = 2 * np.pi * np.outer(np.arange(self.devices), np.arange(n)) / self.grid
        angle = angle.reshape(self.devices, 1, n)
        return both, np.cos(angle).astype(np.float32), np.sin(angle).astype(np.float32)

    def mirror_tables(self):
        pick = np.zeros((self.half + STEP, self.width))
        pick[self.half, 0] = 1.0
        for i in range(self.half):
            pick[i, self.width - i if i else self.half] = 1.0
        n = self.rows
        first, rest = np.zeros((n, n)), np.zeros((n, n))
        for i in range(n):
            first[(n - i) % n, i] = 1.0
            rest[n - 1 - i, i] = 1.0
        return pick.astype(jnp.bfloat16), np.stack([first, rest]).astype(jnp.bfloat16)


def transform(points, sign):
    count = len(points)
    if count == 1:
        return points
    even, odd = transform(points[0::2], sign), transform(points[1::2], sign)
    low, high = [], []
    for k in range(count // 2):
        (er, ei), (re, im) = even[k], odd[k]
        if 4 * k == count:
            re, im = (-im, re) if sign > 0 else (im, -re)
        elif 8 * k == count or 8 * k == 3 * count:
            root = math.sqrt(0.5)
            if 8 * k == count:
                re, im = (re - sign * im) * root, (im + sign * re) * root
            else:
                re, im = (-re - sign * im) * root, (sign * re - im) * root
        elif k:
            c, s = math.cos(2 * math.pi * k / count), sign * math.sin(2 * math.pi * k / count)
            re, im = re * c - im * s, im * c + re * s
        low.append((er + re, ei + im))
        high.append((er - re, ei - im))
    return low + high


def dot(a, b):
    return jnp.dot(a, b, preferred_element_type=F32)


def slot_tiles(marks, plan):
    number = marks.astype(jnp.int32) - 1
    shift = plan.tile_cols.bit_length() - 1
    return number & (plan.tile_cols - 1), number >> shift


def slot_mask(tile_row, plan):
    mine = tile_row[:, : plan.rows]
    lane = lax.broadcasted_iota(jnp.int32, mine.shape, 1) // plan.tile
    mask = (mine == lane).astype(F32)
    return jnp.concatenate([mask] * plan.group, axis=1) > 0.5


def forward_rows(plan, values, marks, spread, table, cosine, sine, edge, out, work):
    tile, rows, group, half = plan.tile, plan.rows, plan.group, plan.half
    slots = values.shape[0]
    marks_in = marks[...]
    _, tile_row = slot_tiles(marks_in, plan)
    mask = slot_mask(tile_row, plan)
    tile_col, _ = slot_tiles(marks_in.T[0:1, :], plan)
    place = lax.broadcasted_iota(jnp.int32, (plan.tile_cols, slots), 0)
    chosen = (place == tile_col).astype(F32).astype(BF16)
    weights = dot(table[0], chosen).astype(BF16)
    weights_low = dot(table[1], chosen).astype(BF16)
    exact = values[...]
    high = exact.astype(BF16)
    low = (exact - high.astype(F32)).astype(BF16)
    span = group * rows
    for chunk in range(tile // group):
        lanes = spread[:, chunk * span : (chunk + 1) * span]
        high_part = jnp.where(mask, dot(high, lanes), 0.0).astype(BF16)
        low_part = jnp.where(mask, dot(low, lanes), 0.0).astype(BF16)
        work[chunk] = (
            dot(weights, high_part) + dot(weights, low_part) + dot(weights_low, high_part)
        )

    def piece(cell, start, size):
        at = (cell % group) * rows
        return work[cell // group, start : start + size, at : at + rows]

    ends = [piece(cell, 0, 8)[0:1] for cell in range(tile)]
    ends += [piece(cell, plan.kappas, 8)[0:1] for cell in range(tile)]
    shared = jnp.dot(
        edge[...],
        jnp.concatenate(ends, axis=0),
        precision=lax.Precision.HIGHEST,
        preferred_element_type=F32,
    )
    first = lax.broadcasted_iota(jnp.int32, (STEP, rows), 0) == 0
    for start in range(0, plan.kappas, STEP):
        points = []
        for cell in range(tile):
            re, im = piece(cell, start, STEP), piece(cell, plan.kappas + start, STEP)
            if cell:
                c, s = cosine[cell, start : start + STEP], sine[cell, start : start + STEP]
                re, im = re * c + im * s, im * c - re * s
            points.append((re, im))
        for mu, (re, im) in enumerate(transform(points, -1)):
            if start == 0:
                re = jnp.where(first, shared[mu : mu + 1], re)
                im = jnp.where(first, shared[tile + mu : tile + mu + 1], im)
            device, row, sign = plan.place(start, mu)
            out[device, row : row + STEP] = re.astype(BF16)
            out[device, half + row : half + row + STEP] = (im * sign).astype(BF16)


def inverse_rows(plan, spectrum, marks, spread, table, cosine, sine, edge, out, work):
    tile, rows, group, half = plan.tile, plan.rows, plan.group, plan.half
    slots = marks.shape[0]
    tile_col, tile_row = slot_tiles(marks[...], plan)
    mask = slot_mask(tile_row, plan)
    place = lax.broadcasted_iota(jnp.int32, (slots, plan.tile_cols), 1)
    chosen = (place == tile_col[:, 0:1]).astype(F32).astype(BF16)
    weights = dot(chosen, table[0]).astype(BF16)
    weights_low = dot(chosen, table[1]).astype(BF16)
    ends = [spectrum[plan.per_mu * mu, 0:STEP].astype(F32)[0:1] for mu in range(tile)]
    ends += [spectrum[plan.per_mu * mu, half : half + STEP].astype(F32)[0:1] for mu in range(tile)]
    shared = jnp.dot(
        edge[...],
        jnp.concatenate(ends, axis=0),
        precision=lax.Precision.HIGHEST,
        preferred_element_type=F32,
    )
    first = lax.broadcasted_iota(jnp.int32, (STEP, rows), 0) == 0
    for start in range(0, plan.kappas, STEP):
        points = []
        for mu in range(tile):
            device, row, sign = plan.place(start, mu)
            re = spectrum[device, row : row + STEP].astype(F32)
            im = spectrum[device, half + row : half + row + STEP].astype(F32) * sign
            points.append((re, im))
        for cell, (re, im) in enumerate(transform(points, 1)):
            if cell:
                c, s = cosine[cell, start : start + STEP], sine[cell, start : start + STEP]
                re, im = re * c - im * s, im * c + re * s
            if start == 0:
                re = jnp.where(first, shared[cell : cell + 1], re)
                im = jnp.where(first, shared[tile + cell : tile + cell + 1], im)
            at = (cell % group) * rows
            work[cell // group, start : start + STEP, at : at + rows] = re.astype(BF16)
            work[cell // group, plan.kappas + start : plan.kappas + start + STEP, at : at + rows] = (
                im.astype(BF16)
            )
    span = group * rows
    total = jnp.zeros(out.shape, F32)
    for chunk in range(tile // group):
        field = dot(weights, work[chunk]) + dot(weights_low, work[chunk])
        field = jnp.where(mask, field, 0.0).astype(BF16)
        lanes = spread[:, chunk * span : (chunk + 1) * span]
        total = total + lax.dot_general(
            field, lanes, (((1,), (1,)), ((), ())), preferred_element_type=F32
        )
    out[...] = total.astype(BF16)


def columns(plan, origin, spectrum, green, both, cosine, sine, out, work):
    devices, rows, half = plan.devices, plan.rows, plan.half
    wide = half + 8
    holds_edge = origin[0] == 1
    top = (lax.broadcasted_iota(jnp.int32, (8, rows), 0) == 0) & holds_edge

    def load(s, carry):
        work[s, 0:half] = spectrum[s, 0:half].astype(F32)
        imag = spectrum[s, half : 2 * half].astype(F32)
        work[s, wide : wide + half] = imag
        head = imag[0:8]
        work[s, wide : wide + 8] = jnp.where(top, 0.0, head)
        work[s, half:wide] = jnp.where(top, head, 0.0)
        work[s, wide + half : 2 * wide] = jnp.zeros((8, rows), F32)
        return carry

    lax.fori_loop(0, devices, load, 0)

    def first(g, carry):
        at = pl.multiple_of(g * 8, 8)
        points = [(work[s, pl.ds(at, 8)], work[s, pl.ds(wide + at, 8)]) for s in range(devices)]
        for m, (re, im) in enumerate(transform(points, -1)):
            if m:
                c, s = cosine[m], sine[m]
                re, im = re * c + im * s, im * c - re * s
            work[m, pl.ds(at, 8)] = re
            work[m, pl.ds(wide + at, 8)] = im
        return carry

    lax.fori_loop(0, wide // 8, first, 0)
    batch = 4

    def second(i, carry):
        at = pl.ds(i * batch, batch)
        flat = (batch * 2 * wide, rows)
        y = work[at].reshape(flat).astype(BF16)
        u = (dot(y, both[0]) + dot(y, both[1])).reshape(batch, 2 * wide, 2 * rows)
        g = green[at]
        re = (u[:, :wide, :rows] + u[:, wide:, rows:]) * g
        im = (u[:, wide:, :rows] - u[:, :wide, rows:]) * g
        y = jnp.concatenate([re, im], axis=1).reshape(flat).astype(BF16)
        u = (dot(y, both[0]) + dot(y, both[1])).reshape(batch, 2 * wide, 2 * rows)
        re = u[:, :wide, :rows] - u[:, wide:, rows:]
        im = u[:, wide:, :rows] + u[:, :wide, rows:]
        c, s = cosine[at], sine[at]
        work[at, 0:wide] = re * c - im * s
        work[at, wide : 2 * wide] = im * c + re * s
        return carry

    lax.fori_loop(0, devices // batch, second, 0)

    def third(g, carry):
        at = pl.multiple_of(g * 8, 8)
        points = [(work[m, pl.ds(at, 8)], work[m, pl.ds(wide + at, 8)]) for m in range(devices)]
        for s, (re, im) in enumerate(transform(points, 1)):
            work[s, pl.ds(at, 8)] = re
            work[s, pl.ds(wide + at, 8)] = im
        return carry

    lax.fori_loop(0, wide // 8, third, 0)

    def store(s, carry):
        work[s, wide : wide + 8] = jnp.where(top, work[s, half:wide], work[s, wide : wide + 8])
        out[s, 0:half] = work[s, 0:half].astype(BF16)
        out[s, half : 2 * half] = work[s, wide : wide + half].astype(BF16)
        return carry

    lax.fori_loop(0, devices, store, 0)


def mirrored_green(plan, green, pick, turn, early, late, edge, edge_turned):
    devices, rows, half = plan.devices, plan.rows, plan.half
    for m in range(devices):
        block = green[pl.ds(m, rows, stride=devices), :].astype(BF16)
        picked = lax.dot_general(
            pick[...], block, (((1,), (1,)), ((), ())), preferred_element_type=F32
        )
        turned = dot(picked.astype(BF16), turn[0 if m == 0 else 1])
        mirrored = (devices - m) % devices
        if mirrored < devices // 2:
            early[mirrored] = turned[0:half].astype(BF16)
        else:
            late[mirrored - devices // 2] = turned[0:half].astype(BF16)
        edge[m : m + 1] = picked[half : half + 1]
        edge_turned[mirrored : mirrored + 1] = turned[half : half + 1]


def own_green(plan, follows, green, own):
    devices, rows, half = plan.devices, plan.rows, plan.half
    partner = follows[0] == 1
    first = lax.broadcasted_iota(jnp.int32, (half, rows), 0) == 0
    for m in range(devices):
        turned = green[pl.ds(m, rows, stride=devices), :].T
        swap = jnp.broadcast_to(turned[half : half + 1], (half, rows))
        own[m] = jnp.where(first & partner, swap, turned[0:half])


def kernel(body, plan, out_shape, scratch, scalars, operands):
    in_specs = [pl.BlockSpec(memory_space=pltpu.SMEM)] * len(scalars)
    in_specs += [pl.BlockSpec(memory_space=pltpu.VMEM)] * len(operands)
    return pl.pallas_call(
        functools.partial(body, plan),
        out_shape=out_shape,
        in_specs=in_specs,
        out_specs=jax.tree.map(lambda _: pl.BlockSpec(memory_space=pltpu.VMEM), out_shape),
        scratch_shapes=scratch,
        compiler_params=pltpu.CompilerParams(vmem_limit_bytes=VMEM_BYTES),
    )(*scalars, *operands)


def leaving_green(plan, green):
    devices, half, rows = plan.devices, plan.half, plan.rows
    pick, turn = plan.mirror_tables()
    part = jax.ShapeDtypeStruct((devices // 2, half, rows), BF16)
    line = jax.ShapeDtypeStruct((devices, rows), F32)
    return kernel(
        mirrored_green,
        plan,
        (part, part, line, line),
        [],
        [],
        [green, jnp.asarray(pick), jnp.asarray(turn)],
    )


def staying_green(plan, green):
    devices, half, rows, per_mu = plan.devices, plan.half, plan.rows, plan.per_mu
    partner = lax.axis_index(AXES) % per_mu >= per_mu // 2
    return kernel(
        own_green,
        plan,
        jax.ShapeDtypeStruct((devices, half, rows), F32),
        [],
        [partner.astype(jnp.int32).reshape(1)],
        [green],
    )


def swap_mirrored(plan, part):
    return lax.ppermute(part, AXES, [(i, plan.devices - 1 - i) for i in range(plan.devices)])


def swap_edges(plan, edge, edge_turned):
    devices, per_mu, tile = plan.devices, plan.per_mu, plan.tile
    upper = range(tile // 2, tile)
    plain = [(devices // 2, 0)]
    plain += [(per_mu * (m - tile // 2) + per_mu // 2, per_mu * m) for m in upper]
    mirror = [(devices // 2, 0)]
    mirror += [(per_mu * (tile - 1 - m + tile // 2) + per_mu // 2, per_mu * m) for m in upper]
    for i in range(1, devices):
        low = i % per_mu
        if low < per_mu // 2 and (low or i // per_mu < tile // 2):
            mirror.append((devices - i, i))
    return lax.ppermute(edge, AXES, plain), lax.ppermute(edge_turned, AXES, mirror)


def symmetric_green(plan, own, received, edges, swapped_edges):
    devices, rows, per_mu = plan.devices, plan.rows, plan.per_mu
    tile, grid = plan.tile, plan.grid
    edge, edge_turned = edges
    edge_plain, edge_mirror = swapped_edges
    me = lax.axis_index(AXES)
    mu, part = me // per_mu, me % per_mu
    partner = part >= per_mu // 2
    shared = (part == 0) & (mu >= tile // 2)
    head = jnp.where(shared, edge_plain, edge) + jnp.where(me == 0, edge_turned, edge_mirror)
    total = own + jnp.concatenate(received, axis=0).astype(F32)
    at_top = lax.broadcasted_iota(jnp.int32, total.shape, 1) == 0
    total = jnp.where(at_top & ~partner, head[:, None, :], total)
    extra = jnp.concatenate(
        [(edge_plain + edge_mirror)[:, None, :], jnp.zeros((devices, 7, rows), F32)], axis=1
    )
    return jnp.concatenate([total, extra], axis=1) * (0.5 / (grid * grid))


def local(charges, target, stencil, near_matrix, green, block_dest, block_tile, near_offset):
    devices = lax.axis_size(AXES)
    blocks, block_size, cell_count = stencil.shape
    pair_count = near_offset.shape[1]
    capacity = 2 * blocks // devices
    slots = devices * capacity
    plan = Plan(green.shape[0], math.isqrt(cell_count), devices)
    me = lax.axis_index(AXES)
    destination = block_dest[:, 0]
    one_hot = (destination[:, None] == jnp.arange(devices, dtype=jnp.int32)[None, :]).astype(
        jnp.int32
    )
    earlier = jnp.cumsum(one_hot, axis=0) - one_hot
    slot_index = destination * capacity + jnp.sum(earlier * one_hot, axis=1)
    spread = jnp.asarray(plan.spread_table())
    forward_table = jnp.asarray(plan.forward_table())
    inverse_table = jnp.asarray(plan.inverse_table())
    cosine, sine = (jnp.asarray(t) for t in plan.column_twiddles())
    edge_forward, edge_inverse = (jnp.asarray(t) for t in plan.edge_tables())
    both, row_cos, row_sin = (jnp.asarray(t) for t in plan.row_tables())
    origin = (me == 0).astype(jnp.int32).reshape(1)
    early, late, *edges = leaving_green(plan, green)
    spectrum_shape = jax.ShapeDtypeStruct((devices, plan.width, plan.rows), BF16)
    work_shape = (plan.tile // plan.group, plan.tile_cols, plan.group * plan.rows)

    def exchange(values):
        return lax.all_to_all(values, AXES, split_axis=0, concat_axis=0, tiled=True)

    def project(values, marked):
        tile_values = jnp.einsum("bp,bpt->bt", values, stencil, preferred_element_type=F32)
        if marked:
            named = jnp.broadcast_to((block_tile + 1).astype(F32)[:, None], (blocks, 128))
            tile_values = jnp.concatenate([tile_values, named], axis=1)
        outgoing = jnp.zeros((slots, tile_values.shape[1]), F32).at[slot_index].set(tile_values)
        return outgoing.reshape(devices, capacity, -1)

    def to_columns(arrived, marks):
        return kernel(
            forward_rows,
            plan,
            spectrum_shape,
            [pltpu.VMEM(work_shape, F32)],
            [],
            [arrived, marks, spread, forward_table, cosine, sine, edge_forward],
        )

    def along_columns(spectrum, weights):
        return kernel(
            columns,
            plan,
            spectrum_shape,
            [pltpu.VMEM((devices, 2 * (plan.half + 8), plan.rows), F32)],
            [origin],
            [spectrum, weights, both, row_cos, row_sin],
        )

    def to_rows(spectrum, marks):
        picked = kernel(
            inverse_rows,
            plan,
            jax.ShapeDtypeStruct((slots, cell_count), BF16),
            [pltpu.VMEM(work_shape, BF16)],
            [],
            [spectrum, marks, spread, inverse_table, cosine, sine, edge_inverse],
        )
        return picked.reshape(devices, capacity, cell_count)

    def interpolate(returned):
        own_tiles = returned.reshape(slots, cell_count)[slot_index]
        return jnp.einsum("bpt,bt->bp", stencil, own_tiles, preferred_element_type=F32)

    couple = near_matrix.reshape(blocks, pair_count, block_size, block_size)
    positions = jnp.arange(blocks, dtype=jnp.int32)[:, None] + REACH + near_offset
    charge_blocks = charges.reshape(blocks, block_size)
    extended = extended_2(charge_blocks, ((AXES, 0),), REACH)
    sources = extended[positions]

    early, late, edges = lax.optimization_barrier((early, late, edges))
    early = swap_mirrored(plan, early)
    outgoing, early, late = lax.optimization_barrier((project(charge_blocks, True), early, late))
    late = swap_mirrored(plan, late)
    swapped_edges = swap_edges(plan, *edges)
    arrived = exchange(outgoing).reshape(slots, -1)
    own = staying_green(plan, green)
    arrived, own = lax.optimization_barrier((arrived, own))
    marks = arrived[:, cell_count:]
    spectrum = to_columns(arrived[:, :cell_count], marks)
    spectrum, late, swapped_edges = lax.optimization_barrier((spectrum, late, swapped_edges))
    weights = symmetric_green(plan, own, (early, late), edges, swapped_edges)
    spectrum, couple, sources = lax.optimization_barrier((exchange(spectrum), couple, sources))
    picked = to_rows(exchange(along_columns(spectrum, weights)), marks)
    far = interpolate(exchange(picked))
    near = jnp.einsum("bkps,bks->bp", couple, sources, preferred_element_type=F32)
    potentials = far + near
    residual = (potentials - target.reshape(blocks, block_size)).astype(BF16)

    arrived = exchange(project(residual, False)).reshape(slots, -1)
    spectrum = exchange(to_columns(arrived, marks))
    spectrum = exchange(along_columns(spectrum, weights))
    terms = jnp.einsum("bkps,bp->bks", couple, residual, preferred_element_type=F32)
    extended = jnp.zeros((blocks + 2 * REACH, block_size), F32)
    extended = extended.at[positions.reshape(-1)].add(terms.reshape(-1, block_size))
    rims = jnp.concatenate([extended[:REACH], extended[blocks + REACH :]], axis=0)
    neighbour = extended_2(rims, ((AXES, 0),), REACH)
    own_part = extended[REACH : blocks + REACH]
    own_part = own_part.at[:REACH].add(neighbour[:REACH])
    own_part = own_part.at[blocks - REACH :].add(neighbour[3 * REACH :])
    gradient = interpolate(exchange(to_rows(spectrum, marks))) + own_part
    return (potentials.reshape(-1), gradient.reshape(-1))


def solution(mesh):
    rows = P(AXES)
    return jax.shard_map(
        local,
        mesh=mesh,
        in_specs=(rows, rows, rows, rows, P(None, AXES), rows, rows, rows),
        out_specs=(rows, rows),
        check_vma=False,
    )
```

time: 831 us -> 272 us (0.33)
  waiting for transfers between devices: 264 us -> 30.1 us
  matrix products: 187 us -> 27.2 us
  local copies, waits for them, and re-layouts: 184 us -> 59.2 us
  blocking collectives: 110 us -> 41.9 us
  Pallas kernels: 0 us -> 36.2 us
  other arithmetic: 35.1 us -> 18 us
  starting transfers between devices: 44.1 us -> 55.9 us
    all_to_all x7 -> x6, waiting for transfers between devices: 264 us -> 30.1 us  [exchange(): return lax.all_to_all(values, AXES, split_axis=0, concat_axis=0, tiled=True)]
    dot_general x38 -> x6, matrix products: 187 us -> 27.2 us  [the longest x1 10.7 us: local(): jnp.einsum('bkps,bp->bks', couple, residual, preferred_element_type=F32)]
    all_to_all x2, blocking collectives: 110 us -> 41.9 us  [exchange(): return lax.all_to_all(values, AXES, split_axis=0, concat_axis=0, tiled=True)]
    another operation x11 -> x0, local copies, waits for them, and re-layouts: 54.8 us -> none  [the longest x4 27.8 us: convolve(): shaped = grid_cells.reshape(row_count, width, devices)]
    convert_element_type x9 -> x0, local copies, waits for them, and re-layouts: 39.6 us -> none  [the longest x8 39.5 us: far_field(): back_tiles = back_tiles.reshape(tile_total, cell_count).astype(jnp.bfloat16)]
    pallas_call x0 -> x8, Pallas kernels: none -> 36.2 us  [kernel(): pl.pallas_call(functools.partial(body, plan), out_shape=out_shape, in_spe...]
    transpose x2 -> x0, local copies, waits for them, and re-layouts: 27.8 us -> none  [far_field(): grid_cells = tile_sums.reshape(tile_rows, tile_cols, TILE, TILE).transpos...]
    optimization_barrier x0 -> x1, local copies, waits for them, and re-layouts: none -> 15.6 us  [local(): lax.optimization_barrier((exchange(spectrum), couple, sources))]
  transfers between devices with their start and end apart: 11 -> 14, of which waited for: 7 -> 5; matrix products, arithmetic and copies ran while one was open for 11% -> 28% of each run, Pallas kernels for 0% -> 3%
where the time goes in v1:
time: 272 us; the launch traced here: 270 us
  local copies, waits for them, and re-layouts  59.2 us (22%)
  starting transfers between devices  55.9 us (21%)
  blocking collectives  41.9 us (15%)
  Pallas kernels  36.2 us (13%)
  waiting for transfers between devices  30.1 us (11%)
  matrix products  27.2 us (10%)
  other arithmetic  18 us (7%)
    all_to_all x2, blocking collectives, exchange(): return lax.all_to_all(values, AXES, split_axis=0, concat_axis=0, tiled=True)  41.9 us
    pallas_call x8, Pallas kernels, kernel(): pl.pallas_call(functools.partial(body, plan), out_shape=out_shape, in_spe...  36.2 us
    all_to_all x6, starting transfers between devices, exchange(): return lax.all_to_all(values, AXES, split_axis=0, concat_axis=0, tiled=True)  33.7 us
    all_to_all x6, waiting for transfers between devices, exchange(): return lax.all_to_all(values, AXES, split_axis=0, concat_axis=0, tiled=True)  30.1 us
    unnamed x75, local copies, waits for them, and re-layouts  22.2 us
    optimization_barrier x1, local copies, waits for them, and re-layouts, local(): lax.optimization_barrier((exchange(spectrum), couple, sources))  15.6 us
    ppermute x2, starting transfers between devices, swap_mirrored(): lax.ppermute(part, AXES, [(i, plan.devices - 1 - i) for i in range(plan.d...  11.6 us
    dot_general x1, matrix products, local(): jnp.einsum('bkps,bp->bks', couple, residual, preferred_element_type=F32)  10.7 us
  transfers between devices with their start and end apart: 14, of which 5 were waited for; matrix products, arithmetic and copies ran while one was open for 28% of the time, Pallas kernels for 3%

profile of v1, /device:TPU:0, one launch (start us, length us, event | category | flops | bytes accessed | tf_op | source)
XLA Modules:
  0.0 269.6 jit_solution(3712901564027202713)
XLA Ops:
  3.8 5.7 %shard_map.203 = (bf16[16,64,128]{2,1,0:T(8,128)(2,1)}, bf16[16,64,128]{2,1,0:T(8,128)(2,1)S(1)}, f32[32,128]{1,0:T(8,128)}, f32[32,128]{1,0:T(8,128)}) custom-call(f32[4096,128]{1,0:T(8,128)S(1)} %copy-done.5, bf16[80,128]{1,0:T(8,128)(2,1)S(1)} %copy-done.26, bf16[2,128,128]{2,1,0:T(8,128)(2,1)S(1)} %copy-done.25), custom_call_target="tpu_custom_call" | custom-call | tf_op jit(solution)/shard_map/pallas_call | solution.py:373
  10.2 6.4 %collective-permute-start = (bf16[16,64,128]{2,1,0:T(8,128)(2,1)}, bf16[16,64,128]{2,1,0:T(8,128)(2,1)}, u32[]{:S(2)}, u32[]{:S(2)}) collective-permute-start(bf16[16,64,128]{2,1,0:T(8,128)(2,1)} %get-tuple-element.42), channel_id=1, source_target_pairs={{0,31},{1,30},{2,29},{3,28},{4,27},{5,26},{6,25},{7,24},{8,23},{9,... | collective-permute-start | bytes 786440 | tf_op jit(solution)/shard_map/ppermute | solution.py:412
  26.0 6.9 %all-to-all-start = ((f32[32,8,384]{2,1,0:T(8,128)}), f32[32,8,384]{2,1,0:T(8,128)}, u32[]{:S(2)}, u32[]{:S(2)}) async-start(f32[32,8,384]{2,1,0:T(8,128)} %bitcast.57), calls=%async_computation | async-start | bytes 786432 | tf_op jit(solution)/shard_map/all_to_all | solution.py:474
  32.9 5.2 %collective-permute-start.1 = (bf16[16,64,128]{2,1,0:T(8,128)(2,1)}, bf16[16,64,128]{2,1,0:T(8,128)(2,1)}, u32[]{:S(2)}, u32[]{:S(2)}) collective-permute-start(bf16[16,64,128]{2,1,0:T(8,128)(2,1)} %copy-done.27), channel_id=1, source_target_pairs={{0,31},{1,30},{2,29},{3,28},{4,27},{5,26},{6,25},{7,24},{8,23},{9,... | collective-permute-start | bytes 786440 | tf_op jit(solution)/shard_map/ppermute | solution.py:412
  44.6 7.3 %all-to-all-done = f32[32,8,384]{2,1,0:T(8,128)} async-done(((f32[32,8,384]{2,1,0:T(8,128)}), f32[32,8,384]{2,1,0:T(8,128)}, u32[]{:S(2)}, u32[]{:S(2)}) %all-to-all-start) | async-done | bytes 393248 | tf_op jit(solution)/shard_map/all_to_all | solution.py:474
  57.5 3.4 %all-to-all-start.1 = ((bf16[32,128,128]{2,1,0:T(8,128)(2,1)}), bf16[32,128,128]{2,1,0:T(8,128)(2,1)}, u32[]{:S(2)}, u32[]{:S(2)}) async-start(bf16[32,128,128]{2,1,0:T(8,128)(2,1)} %copy-done.7), calls=%async_computation.1 | async-start | bytes 2097152 | tf_op jit(solution)/shard_map/all_to_all | solution.py:474
  68.6 7.9 %copy.22 = bf16[128,4,4096]{0,2,1:T(8,128)(2,1)} copy(bf16[128,4,4096]{2,1,0:T(4,128)(2,1)} %param.27) | data formatting | bytes 8388608 | tf_op args[3]
  82.0 5.1 %all-to-all-done.1.spectrum = bf16[32,128,128]{2,1,0:T(8,128)(2,1)} async-done(((bf16[32,128,128]{2,1,0:T(8,128)(2,1)}), bf16[32,128,128]{2,1,0:T(8,128)(2,1)}, u32[]{:S(2)}, u32[]{:S(2)}) %all-to-all-start.1) | async-done | bytes 1048608 | tf_op jit(solution)/shard_map/all_to_all | solution.py:474
  88.4 9.3 %shard_map.206 = bf16[32,128,128]{2,1,0:T(8,128)(2,1)S(1)} custom-call(s32[1]{0:T(128)} %bitcast.origin, bf16[32,128,128]{2,1,0:T(8,128)(2,1)} %all-to-all-done.1.spectrum, f32[32,72,128]{2,1,0:T(8,128)S(1)} %copy-done.3, bf16[2,128,256]{2,1,0:T(8,128)(2,1)S(1)} %copy-done.14, f32[32,1,128]{2,1,0:T(1,128)S(1)} %copy-done.21, f32[32,1,128]{2,1,0:T(1,128)S(1)} %copy-done.19), custom_call_target="tpu_custom_call" | custom-call | tf_op jit(solution)/shard_map/pallas_call | solution.py:373
  98.7 8.3 %all-to-all-start.2 = ((bf16[32,128,128]{2,1,0:T(8,128)(2,1)}), bf16[32,128,128]{2,1,0:T(8,128)(2,1)}, u32[]{:S(2)}, u32[]{:S(2)}) async-start(bf16[32,128,128]{2,1,0:T(8,128)(2,1)} %copy-done.10), calls=%async_computation.2 | async-start | bytes 2097152 | tf_op jit(solution)/shard_map/all_to_all | solution.py:474
  108.4 15.6 %copy.36 = bf16[128,4,64,64]{2,3,1,0:T(8,128)(2,1)} copy(bf16[128,4,64,64]{0,3,2,1:T(8,128)(2,1)} %bitcast.55) | data formatting | bytes 8388608 | tf_op jit(solution)/shard_map/optimization_barrier | solution.py:537
  124.0 9.1 %all-to-all-done.2.spectrum = bf16[32,128,128]{2,1,0:T(8,128)(2,1)} async-done(((bf16[32,128,128]{2,1,0:T(8,128)(2,1)}), bf16[32,128,128]{2,1,0:T(8,128)(2,1)}, u32[]{:S(2)}, u32[]{:S(2)}) %all-to-all-start.2) | async-done | bytes 1048608 | tf_op jit(solution)/shard_map/all_to_all | solution.py:474
  137.0 3.8 %all-to-all-start.3 = ((bf16[32,8,256]{2,1,0:T(8,128)(2,1)}), bf16[32,8,256]{2,1,0:T(8,128)(2,1)}, u32[]{:S(2)}, u32[]{:S(2)}) async-start(bf16[32,8,256]{2,1,0:T(8,128)(2,1)} %bitcast.54), calls=%async_computation.3 | async-start | bytes 262144 | tf_op jit(solution)/shard_map/all_to_all | solution.py:474
  140.8 5.3 %fusion = f32[128,1,64,1]{2,1,3,0:T(1,128)} fusion(bf16[128,4,64,64]{2,3,1,0:T(8,128)(2,1)} %copy.36, bf16[128,4,64,1]{2,1,0,3:T(4,128)(2,1)} %bitcast.63), kind=kOutput, calls=%fused_computation.8 | convolution fusion | flops 4194304 | bytes 4292608 | tf_op jit(solution)/shard_map/bkps,bks->bp/dot_general | solution.py:540
  151.4 3.5 %fusion.12 = f32[128,1,64]{2,1,0:T(1,128)S(1)} fusion(bf16[128,64,256]{2,1,0:T(8,128)(2,1)} %param.26, bf16[128,256,1]{1,0,2:T(8,128)(2,1)} %bitcast.69), kind=kOutput, calls=%fused_computation.20 | convolution fusion | flops 4194304 | bytes 4292608 | tf_op jit(solution)/shard_map/bpt,bt->bp/dot_general | solution.py:517
  159.6 13.4 %all_to_all.40 = f32[32,8,256]{2,1,0:T(8,128)S(1)} all-to-all(f32[32,8,256]{2,1,0:T(8,128)} %bitcast.58), channel_id=1, replica_groups=mesh['panel'=8,'slab'=4] {'panel','slab'}, dimensions={0} | all-to-all | bytes 524288 | tf_op jit(solution)/shard_map/all_to_all | solution.py:474
  177.4 28.5 %all_to_all.41.spectrum = bf16[32,128,128]{2,1,0:T(8,128)(2,1)S(1)} all-to-all(bf16[32,128,128]{2,1,0:T(8,128)(2,1)S(1)} %shard_map.208), channel_id=1, replica_groups=mesh['panel'=8,'slab'=4] {'panel','slab'}, dimensions={0} | all-to-all | bytes 2097152 | tf_op jit(solution)/shard_map/all_to_all | solution.py:474
  205.9 8.1 %shard_map.209 = bf16[32,128,128]{2,1,0:T(8,128)(2,1)S(1)} custom-call(s32[1]{0:T(128)} %bitcast.origin, bf16[32,128,128]{2,1,0:T(8,128)(2,1)S(1)} %all_to_all.41.spectrum, f32[32,72,128]{2,1,0:T(8,128)S(1)} %copy-done.4, bf16[2,128,256]{2,1,0:T(8,128)(2,1)S(1)} %copy-done.15, f32[32,1,128]{2,1,0:T(1,128)S(1)} %copy-done.22, f32[32,1,128]{2,1,0:T(1,128)S(1)} %copy-done.20), custom_call_target="tpu_custom_call" | custom-call | tf_op jit(solution)/shard_map/pallas_call | solution.py:373
  215.0 4.0 %all-to-all-start.6 = ((bf16[32,128,128]{2,1,0:T(8,128)(2,1)}), bf16[32,128,128]{2,1,0:T(8,128)(2,1)}, u32[]{:S(2)}, u32[]{:S(2)}) async-start(bf16[32,128,128]{2,1,0:T(8,128)(2,1)} %copy-done.9), calls=%async_computation.6 | async-start | bytes 2097152 | tf_op jit(solution)/shard_map/all_to_all | solution.py:474
  223.2 10.7 %fusion.15 = f32[128,1,4,64]{3,1,2,0:T(1,128)} fusion(bf16[128,4,64,64]{2,3,1,0:T(8,128)(2,1)} %copy.36, bf16[128,64,1,1]{1,0,2,3:T(8,128)(2,1)} %bitcast.60), kind=kOutput, calls=%fused_computation.24 | convolution fusion | flops 4194304 | bytes 4341760 | tf_op jit(solution)/shard_map/bkps,bp->bks/dot_general | solution.py:547
  233.8 3.2 %scatter_custom_fusion.2 = f32[144,64]{1,0:T(8,128)} fusion(s32[512]{0:T(512)} %bitcast.72, f32[512,64]{1,0:T(8,128)} %bitcast.62, f32[]{:T(128)} %constant.134.clone.1), kind=kCustom, calls=%fused_computation.33 | custom fusion | flops 32768 | bytes 37376 | tf_op jit(solution)/shard_map/scatter-add | solution.py:549
  249.0 7.4 %all-to-all-start.7 = ((bf16[32,8,256]{2,1,0:T(8,128)(2,1)}), bf16[32,8,256]{2,1,0:T(8,128)(2,1)S(1)}, u32[]{:S(2)}, u32[]{:S(2)}) async-start(bf16[32,8,256]{2,1,0:T(8,128)(2,1)} %bitcast.53), calls=%async_computation.7 | async-start | bytes 262144 | tf_op jit(solution)/shard_map/all_to_all | solution.py:474
  258.9 5.7 %all-to-all-done.7 = bf16[32,8,256]{2,1,0:T(8,128)(2,1)S(1)} async-done(((bf16[32,8,256]{2,1,0:T(8,128)(2,1)}), bf16[32,8,256]{2,1,0:T(8,128)(2,1)S(1)}, u32[]{:S(2)}, u32[]{:S(2)}) %all-to-all-start.7) | async-done | bytes 131104 | tf_op jit(solution)/shard_map/all_to_all | solution.py:474
  265.6 3.4 %fusion.9 = f32[128,1,64]{2,1,0:T(1,128)S(1)} fusion(bf16[128,64,256]{2,1,0:T(8,128)(2,1)} %param.26, bf16[128,256,1]{1,0,2:T(8,128)(2,1)S(1)} %bitcast.68), kind=kOutput, calls=%fused_computation.17 | convolution fusion | flops 4194304 | bytes 4292608 | tf_op jit(solution)/shard_map/bpt,bt->bp/dot_general | solution.py:517
  (141 shorter events, 81.4 us)
Async XLA Ops:
  10.2 15.8 %collective-permute-start = (bf16[16,64,128]{2,1,0:T(8,128)(2,1)}, bf16[16,64,128]{2,1,0:T(8,128)(2,1)}, u32[]{:S(2)}, u32[]{:S(2)}) collective-permute-start(bf16[16,64,128]{2,1,0:T(8,128)(2,1)} %get-tuple-element.42), channel_id=1, source_target_pairs={{0,31},{1,30},{2,29},{3,28},{4,27},{5,26},{6,25},{7,24},{8,23},{9,... | collective-permute-start | bytes 786440 | tf_op jit(solution)/shard_map/ppermute | solution.py:412
  19.5 34.3 %copy-start = (f32[16,128,128]{2,1,0:T(8,128)S(1)}, f32[16,128,128]{2,1,0:T(8,128)}, u32[]{:S(2)}) copy-start(f32[16,128,128]{2,1,0:T(8,128)} %constant.147.clone.sine) | copy-start | bytes 3145732
  19.5 34.3 %copy-start.1 = (f32[16,128,128]{2,1,0:T(8,128)S(1)}, f32[16,128,128]{2,1,0:T(8,128)}, u32[]{:S(2)}) copy-start(f32[16,128,128]{2,1,0:T(8,128)} %constant.146.clone.cosine) | copy-start | bytes 3145732
  19.5 34.3 %copy-start.2 = (bf16[256,2048]{1,0:T(8,128)(2,1)S(1)}, bf16[256,2048]{1,0:T(8,128)(2,1)}, u32[]{:S(2)}) copy-start(bf16[256,2048]{1,0:T(8,128)(2,1)} %constant.143.clone.spread) | copy-start | bytes 3145732
  19.5 34.3 %copy-start.12 = (bf16[2,256,256]{2,1,0:T(8,128)(2,1)S(1)}, bf16[2,256,256]{2,1,0:T(8,128)(2,1)}, u32[]{:S(2)}) copy-start(bf16[2,256,256]{2,1,0:T(8,128)(2,1)} %constant.144.clone.table) | copy-start | bytes 786436
  19.5 34.3 %copy-start.23 = (f32[32,32]{1,0:T(8,128)S(1)}, f32[32,32]{1,0:T(8,128)}, u32[]{:S(2)}) copy-start(f32[32,32]{1,0:T(8,128)} %constant.148.clone.edge) | copy-start | bytes 12292
  26.0 25.9 %all-to-all-start = ((f32[32,8,384]{2,1,0:T(8,128)}), f32[32,8,384]{2,1,0:T(8,128)}, u32[]{:S(2)}, u32[]{:S(2)}) async-start(f32[32,8,384]{2,1,0:T(8,128)} %bitcast.57), calls=%async_computation | async-start | bytes 786432 | tf_op jit(solution)/shard_map/all_to_all | solution.py:474
  32.9 24.6 %collective-permute-start.1 = (bf16[16,64,128]{2,1,0:T(8,128)(2,1)}, bf16[16,64,128]{2,1,0:T(8,128)(2,1)}, u32[]{:S(2)}, u32[]{:S(2)}) collective-permute-start(bf16[16,64,128]{2,1,0:T(8,128)(2,1)} %copy-done.27), channel_id=1, source_target_pairs={{0,31},{1,30},{2,29},{3,28},{4,27},{5,26},{6,25},{7,24},{8,23},{9,... | collective-permute-start | bytes 786440 | tf_op jit(solution)/shard_map/ppermute | solution.py:412
  38.1 19.4 %collective-permute-start.2 = (f32[32,128]{1,0:T(8,128)}, f32[32,128]{1,0:T(8,128)}, u32[]{:S(2)}, u32[]{:S(2)}) collective-permute-start(f32[32,128]{1,0:T(8,128)} %get-tuple-element.47), channel_id=1, source_target_pairs={{16,0},{1,16},{3,18},{5,20},{7,22},{9,24},{11,26},{13,28},{15,30}} | collective-permute-start | bytes 49160 | tf_op jit(solution)/shard_map/ppermute | solution.py:426
  39.4 18.1 %collective-permute-start.3 = (f32[32,128]{1,0:T(8,128)}, f32[32,128]{1,0:T(8,128)}, u32[]{:S(2)}, u32[]{:S(2)}) collective-permute-start(f32[32,128]{1,0:T(8,128)} %get-tuple-element.48), channel_id=1, source_target_pairs={{16,0},{31,16},{29,18},{27,20},{25,22},{23,24},{21,26},{19,28},{17... | collective-permute-start | bytes 49160 | tf_op jit(solution)/shard_map/ppermute | solution.py:426
  57.5 29.6 %all-to-all-start.1 = ((bf16[32,128,128]{2,1,0:T(8,128)(2,1)}), bf16[32,128,128]{2,1,0:T(8,128)(2,1)}, u32[]{:S(2)}, u32[]{:S(2)}) async-start(bf16[32,128,128]{2,1,0:T(8,128)(2,1)} %copy-done.7), calls=%async_computation.1 | async-start | bytes 2097152 | tf_op jit(solution)/shard_map/all_to_all | solution.py:474
  61.7 14.7 %collective-permute-start.5 = (bf16[8,64]{1,0:T(8,128)(2,1)S(1)}, bf16[8,64]{1,0:T(8,128)(2,1)S(1)}, u32[]{:S(2)}, u32[]{:S(2)}) collective-permute-start(bf16[8,64]{1,0:T(8,128)(2,1)S(1)} %slice.87), channel_id=1, source_target_pairs={{1,0},{2,1},{3,2},{4,3},{5,4},{6,5},{7,6},{8,7},{9,8},{10,9},{11,1... | collective-permute-start | bytes 3080 | tf_op jit(solution)/shard_map/ppermute | solution.py:30
  63.1 13.4 %collective-permute-start.4 = (bf16[8,64]{1,0:T(8,128)(2,1)S(1)}, bf16[8,64]{1,0:T(8,128)(2,1)S(1)}, u32[]{:S(2)}, u32[]{:S(2)}) collective-permute-start(bf16[8,64]{1,0:T(8,128)(2,1)S(1)} %slice.85), channel_id=1, source_target_pairs={{0,1},{1,2},{2,3},{3,4},{4,5},{5,6},{6,7},{7,8},{8,9},{9,10},{10,1... | collective-permute-start | bytes 3080 | tf_op jit(solution)/shard_map/ppermute | solution.py:28
  80.8 27.0 %copy-start.36 = (s32[128]{0:T(128)S(1)}, s32[128]{0:T(128)}, u32[]{:S(2)}) copy-start(s32[128]{0:T(128)} %fusion.24) | copy-start | bytes 1540
  98.7 34.4 %all-to-all-start.2 = ((bf16[32,128,128]{2,1,0:T(8,128)(2,1)}), bf16[32,128,128]{2,1,0:T(8,128)(2,1)}, u32[]{:S(2)}, u32[]{:S(2)}) async-start(bf16[32,128,128]{2,1,0:T(8,128)(2,1)} %copy-done.10), calls=%async_computation.2 | async-start | bytes 2097152 | tf_op jit(solution)/shard_map/all_to_all | solution.py:474
  137.0 12.0 %all-to-all-start.3 = ((bf16[32,8,256]{2,1,0:T(8,128)(2,1)}), bf16[32,8,256]{2,1,0:T(8,128)(2,1)}, u32[]{:S(2)}, u32[]{:S(2)}) async-start(bf16[32,8,256]{2,1,0:T(8,128)(2,1)} %bitcast.54), calls=%async_computation.3 | async-start | bytes 262144 | tf_op jit(solution)/shard_map/all_to_all | solution.py:474
  159.6 46.3 %copy-start.4 = (f32[32,72,128]{2,1,0:T(8,128)S(1)}, f32[32,72,128]{2,1,0:T(8,128)}, u32[]{:S(2)}) copy-start(f32[32,72,128]{2,1,0:T(8,128)} %maximum_multiply_fusion.green) | copy-start | bytes 3538948
  174.7 31.2 %copy-start.15 = (bf16[2,128,256]{2,1,0:T(8,128)(2,1)S(1)}, bf16[2,128,256]{2,1,0:T(8,128)(2,1)}, u32[]{:S(2)}) copy-start(bf16[2,128,256]{2,1,0:T(8,128)(2,1)} %constant.150.clone.both) | copy-start | bytes 393220
  174.7 31.2 %copy-start.20 = (f32[32,1,128]{2,1,0:T(1,128)S(1)}, f32[32,1,128]{2,1,0:T(1,128)}, u32[]{:S(2)}) copy-start(f32[32,1,128]{2,1,0:T(1,128)} %constant.152.clone.sine) | copy-start | bytes 49156
  174.7 31.2 %copy-start.22 = (f32[32,1,128]{2,1,0:T(1,128)S(1)}, f32[32,1,128]{2,1,0:T(1,128)}, u32[]{:S(2)}) copy-start(f32[32,1,128]{2,1,0:T(1,128)} %constant.151.clone.cosine) | copy-start | bytes 49156
  215.0 30.1 %all-to-all-start.6 = ((bf16[32,128,128]{2,1,0:T(8,128)(2,1)}), bf16[32,128,128]{2,1,0:T(8,128)(2,1)}, u32[]{:S(2)}, u32[]{:S(2)}) async-start(bf16[32,128,128]{2,1,0:T(8,128)(2,1)} %copy-done.9), calls=%async_computation.6 | async-start | bytes 2097152 | tf_op jit(solution)/shard_map/all_to_all | solution.py:474
  238.4 18.0 %collective-permute-start.6 = (f32[8,64]{1,0:T(8,128)}, f32[8,64]{1,0:T(8,128)}, u32[]{:S(2)}, u32[]{:S(2)}) collective-permute-start(f32[8,64]{1,0:T(8,128)} %get-tuple-element.63), channel_id=1, source_target_pairs={{0,1},{1,2},{2,3},{3,4},{4,5},{5,6},{6,7},{7,8},{8,9},{9,10},{10,1... | collective-permute-start | bytes 6152 | tf_op jit(solution)/shard_map/ppermute | solution.py:28
  243.8 13.8 %collective-permute-start.7 = (f32[8,64]{1,0:T(8,128)}, f32[8,64]{1,0:T(8,128)}, u32[]{:S(2)}, u32[]{:S(2)}) collective-permute-start(f32[8,64]{1,0:T(8,128)} %get-tuple-element.62), channel_id=1, source_target_pairs={{1,0},{2,1},{3,2},{4,3},{5,4},{6,5},{7,6},{8,7},{9,8},{10,9},{11,1... | collective-permute-start | bytes 6152 | tf_op jit(solution)/shard_map/ppermute | solution.py:30
  249.0 15.6 %all-to-all-start.7 = ((bf16[32,8,256]{2,1,0:T(8,128)(2,1)}), bf16[32,8,256]{2,1,0:T(8,128)(2,1)S(1)}, u32[]{:S(2)}, u32[]{:S(2)}) async-start(bf16[32,8,256]{2,1,0:T(8,128)(2,1)} %bitcast.53), calls=%async_computation.7 | async-start | bytes 262144 | tf_op jit(solution)/shard_map/all_to_all | solution.py:474
  (27 other events, 150.9 us)

commit v2 on v1

v2 whole, which is shorter than its diff:
```python
import functools
import math

import jax
import jax.numpy as jnp
import numpy as np
from jax import lax
from jax.experimental import pallas as pl
from jax.experimental.pallas import tpu as pltpu
from jax.sharding import PartitionSpec as P

REACH = 8
AXES = ("panel", "slab")
BF16 = jnp.bfloat16
F32 = jnp.float32
WIDE = 56 * 1024 * 1024
NARROW = 24 * 1024 * 1024
STEP = 16


def extended_2(cells, sides, width):
    for axis, dim in sides:
        count = lax.axis_size(axis)
        ends = count - 1
        head = lax.slice_in_dim(cells, 0, width, axis=dim)
        tail = lax.slice_in_dim(cells, cells.shape[dim] - width, cells.shape[dim], axis=dim)
        cells = jnp.concatenate(
            [
                lax.ppermute(tail, axis, [(i, (i + 1) % count) for i in range(ends)]),
                cells,
                lax.ppermute(head, axis, [((i + 1) % count, i) for i in range(ends)]),
            ],
            axis=dim,
        )
    return cells


def split(table):
    high = table.astype(jnp.bfloat16)
    return np.stack([high, (table - high.astype(np.float64)).astype(jnp.bfloat16)])


class Plan:
    def __init__(self, grid, tile, devices):
        self.grid, self.tile, self.devices = grid, tile, devices
        self.tile_cols = grid // tile
        self.rows = grid // devices
        self.width = grid // devices
        self.half = self.width // 2
        self.per_mu = devices // tile
        self.kappas = self.tile_cols // 2
        self.group = max(1, min(tile, 2 * 128 // self.rows))

    def factors(self):
        outer = 1 << ((self.devices.bit_length() - 1) // 2)
        return outer, self.devices // outer

    def low_part(self, index):
        outer, inner = self.factors()
        return index // inner + outer * (index % inner)

    def place_of(self, low):
        outer, inner = self.factors()
        return (low % outer) * inner + low // outer

    def place(self, position, mu):
        part, j = divmod(position, self.width)
        device = self.per_mu * mu + part
        if j < self.half:
            return device, j, 1.0
        return self.devices - 1 - device, j - self.half, -1.0

    def kappa(self):
        out = []
        for position in range(self.kappas):
            part, j = divmod(position, self.width)
            if j >= self.half:
                j = self.half + (self.half - (j - self.half)) % self.half
            out.append(self.width * part + j)
        return np.array(out)

    def forward_table(self):
        angle = 2 * np.pi * np.outer(self.kappa(), np.arange(self.tile_cols)) / self.tile_cols
        sine = -np.sin(angle)
        sine[0] = (-1.0) ** np.arange(self.tile_cols)
        return split(np.concatenate([np.cos(angle), sine]))

    def inverse_table(self):
        angle = 2 * np.pi * np.outer(np.arange(self.tile_cols), self.kappa()) / self.tile_cols
        cosine, sine = 2 * np.cos(angle), -2 * np.sin(angle)
        cosine[:, 0] = 1.0
        sine[:, 0] = (-1.0) ** np.arange(self.tile_cols)
        return split(np.concatenate([cosine, sine], axis=1))

    def column_twiddles(self):
        angle = 2 * np.pi * self.kappa() / self.grid
        full = np.broadcast_to(angle[:, None], (self.kappas, self.rows))
        return np.stack([np.cos(full), np.sin(full)]).astype(np.float32)

    def edge_tables(self):
        n, m = self.tile, self.tile // 2
        cells = np.arange(n)
        forward, inverse = np.zeros((2 * n, 2 * n)), np.zeros((2 * n, 2 * n))
        forward[0, :n], forward[n, :n] = 1.0, (-1.0) ** cells
        inverse[:n, 0], inverse[:n, n] = 1.0, (-1.0) ** cells
        for mu in range(1, m):
            angle = 2 * np.pi * cells * mu / n
            forward[mu, :n], forward[n + mu, :n] = np.cos(angle), -np.sin(angle)
            inverse[:n, mu], inverse[:n, n + mu] = 2 * np.cos(angle), -2 * np.sin(angle)
        for nu in range(m):
            angle = 2 * np.pi * cells * (1 + 2 * nu) / (2 * n)
            forward[m + nu, n:], forward[n + m + nu, n:] = np.cos(angle), -np.sin(angle)
            inverse[n:, m + nu], inverse[n:, n + m + nu] = 2 * np.cos(angle), -2 * np.sin(angle)
        return forward.astype(np.float32), inverse.astype(np.float32)

    def row_tables(self):
        n = self.rows
        angle = 2 * np.pi * (np.outer(np.arange(n), np.arange(n)) % n) / n
        both = split(np.concatenate([np.cos(angle), np.sin(angle)], axis=1))
        low = [self.low_part(index) for index in range(self.devices)]
        angle = 2 * np.pi * np.outer(low, np.arange(n)) / self.grid
        return both.reshape(2 * n, 2 * n), np.stack([np.cos(angle), np.sin(angle)]).astype(np.float32)

    def mirror_tables(self):
        pick = np.zeros((self.half + STEP, self.width))
        pick[self.half, 0] = 1.0
        for i in range(self.half):
            pick[i, self.width - i if i else self.half] = 1.0
        n = self.rows
        first, rest = np.zeros((n, n)), np.zeros((n, n))
        for i in range(n):
            first[(n - i) % n, i] = 1.0
            rest[n - 1 - i, i] = 1.0
        return pick.T.astype(jnp.bfloat16), np.stack([first, rest]).astype(jnp.bfloat16)


def transform(points, sign):
    count = len(points)
    if count == 1:
        return points
    even, odd = transform(points[0::2], sign), transform(points[1::2], sign)
    low, high = [], []
    for k in range(count // 2):
        (er, ei), (re, im) = even[k], odd[k]
        if 4 * k == count:
            re, im = (-im, re) if sign > 0 else (im, -re)
        elif 8 * k == count or 8 * k == 3 * count:
            root = math.sqrt(0.5)
            if 8 * k == count:
                re, im = (re - sign * im) * root, (im + sign * re) * root
            else:
                re, im = (-re - sign * im) * root, (sign * re - im) * root
        elif k:
            c, s = math.cos(2 * math.pi * k / count), sign * math.sin(2 * math.pi * k / count)
            re, im = re * c - im * s, im * c + re * s
        low.append((er + re, ei + im))
        high.append((er - re, ei - im))
    return low + high


def dot(a, b):
    return jnp.dot(a, b, preferred_element_type=F32)


def slot_tiles(marks, plan):
    number = marks.astype(jnp.int32) - 1
    shift = plan.tile_cols.bit_length() - 1
    return number & (plan.tile_cols - 1), number >> shift


def slot_mask(tile_row, plan):
    mine = tile_row[:, : plan.rows]
    lane = lax.broadcasted_iota(jnp.int32, mine.shape, 1) // plan.tile
    mask = (mine == lane).astype(F32)
    return jnp.concatenate([mask] * plan.group, axis=1) > 0.5


class Copies:
    def __init__(self, semaphores):
        self.semaphores, self.started = semaphores, []

    def start(self, source, target):
        copy = pltpu.make_async_copy(source, target, self.semaphores.at[len(self.started)])
        copy.start()
        self.started.append(copy)
        return copy

    def wait(self):
        for copy in self.started:
            copy.wait()


def cell_lanes(plan):
    cells, span = plan.tile * plan.tile, plan.group * plan.rows
    cell = lax.broadcasted_iota(jnp.int32, (cells, span), 0)
    lane = lax.broadcasted_iota(jnp.int32, (cells, span), 1)
    differs = (cell & (plan.tile - 1)) - lane // plan.rows
    return jnp.where(cell // plan.tile == (lane & (plan.tile - 1)), differs, -plan.tile)


def spread_lanes(plan, lanes, chunk):
    return jnp.where(lanes == chunk * plan.group, 1.0, 0.0).astype(BF16)


def powers(cosine, sine, count):
    out = [None, (cosine, sine)]
    for k in range(2, count):
        (c, s), (d, t) = out[k // 2], out[k - k // 2]
        out.append((c * d - s * t, s * d + c * t))
    return out


def forward_rows(plan, values_in, marked_in, table_in, twiddle_in, edge_in, out, values, marked, table, twiddle, edge, work, lines, ins, outs):
    tile, rows, group, half = plan.tile, plan.rows, plan.group, plan.half
    slots, cells = values.shape[0], tile * tile
    loads = Copies(ins)
    load_marks = loads.start(marked_in.at[:, cells:], marked)
    load_table = loads.start(table_in, table)
    load_values = loads.start(values_in.at[:, :cells], values)
    load_twiddle = loads.start(twiddle_in, twiddle)
    load_edge = loads.start(edge_in, edge)
    lanes = cell_lanes(plan)
    load_marks.wait()
    marks = marked[...]
    _, tile_row = slot_tiles(marks, plan)
    mask = slot_mask(tile_row, plan)
    tile_col, _ = slot_tiles(marks.T[0:1, :], plan)
    place = lax.broadcasted_iota(jnp.int32, (plan.tile_cols, slots), 0)
    chosen = (place == tile_col).astype(F32).astype(BF16)
    load_table.wait()
    weights = dot(table[0], chosen).astype(BF16)
    weights_low = dot(table[1], chosen).astype(BF16)
    load_values.wait()
    exact = values[...]
    high = exact.astype(BF16)
    low = (exact - high.astype(F32)).astype(BF16)
    for chunk in range(tile // group):
        spread = spread_lanes(plan, lanes, chunk)
        high_part = jnp.where(mask, dot(high, spread), 0.0).astype(BF16)
        low_part = jnp.where(mask, dot(low, spread), 0.0).astype(BF16)
        work[chunk] = (
            dot(weights, high_part) + dot(weights, low_part) + dot(weights_low, high_part)
        )
    load_twiddle.wait()
    load_edge.wait()

    def piece(cell, start, size):
        at = (cell % group) * rows
        return work[cell // group, start : start + size, at : at + rows]

    ends = [piece(cell, 0, 8)[0:1] for cell in range(tile)]
    ends += [piece(cell, plan.kappas, 8)[0:1] for cell in range(tile)]
    shared = jnp.dot(
        edge[...],
        jnp.concatenate(ends, axis=0),
        precision=lax.Precision.HIGHEST,
        preferred_element_type=F32,
    )
    first = lax.broadcasted_iota(jnp.int32, (STEP, rows), 0) == 0
    stores = Copies(outs)
    for start in range(0, plan.kappas, STEP):
        at = slice(start, start + STEP)
        turns = powers(twiddle[0, at], twiddle[1, at], tile)
        points = []
        for cell in range(tile):
            re, im = piece(cell, start, STEP), piece(cell, plan.kappas + start, STEP)
            if cell:
                c, s = turns[cell]
                re, im = re * c + im * s, im * c - re * s
            points.append((re, im))
        for mu, (re, im) in enumerate(transform(points, -1)):
            if start == 0:
                re = jnp.where(first, shared[mu : mu + 1], re)
                im = jnp.where(first, shared[tile + mu : tile + mu + 1], im)
            device, row, sign = plan.place(start, mu)
            lines[device, row : row + STEP] = re.astype(BF16)
            lines[device, half + row : half + row + STEP] = (im * sign).astype(BF16)
            if row + STEP == half:
                stores.start(lines.at[device], out.at[device])
    stores.wait()


def inverse_rows(plan, spectrum_in, marked_in, table_in, twiddle_in, edge_in, out, spectrum, marked, table, twiddle, edge, work, picked, ins, outs):
    tile, rows, group, half = plan.tile, plan.rows, plan.group, plan.half
    slots, cells = marked.shape[0], tile * tile
    loads = Copies(ins)
    load_marks = loads.start(marked_in.at[:, cells:], marked)
    load_edge = loads.start(edge_in, edge)
    load_rows = []
    for row in range(0, half, STEP):
        both_parts = []
        for at in (row, half + row):
            here = pl.ds(at, STEP)
            both_parts.append(loads.start(spectrum_in.at[:, here, :], spectrum.at[:, here, :]))
        load_rows.append(both_parts)
    load_twiddle = loads.start(twiddle_in, twiddle)
    load_table = loads.start(table_in, table)
    lanes = cell_lanes(plan)
    load_marks.wait()
    tile_col, tile_row = slot_tiles(marked[...], plan)
    mask = slot_mask(tile_row, plan)
    place = lax.broadcasted_iota(jnp.int32, (slots, plan.tile_cols), 1)
    chosen = (place == tile_col[:, 0:1]).astype(F32).astype(BF16)
    load_edge.wait()
    load_twiddle.wait()
    first = lax.broadcasted_iota(jnp.int32, (STEP, rows), 0) == 0
    for row in range(0, half, STEP):
        for copy in load_rows[row // STEP]:
            copy.wait()
        if row == 0:
            ends = [spectrum[plan.per_mu * mu, 0:STEP].astype(F32)[0:1] for mu in range(tile)]
            ends += [
                spectrum[plan.per_mu * mu, half : half + STEP].astype(F32)[0:1] for mu in range(tile)
            ]
            shared = jnp.dot(
                edge[...],
                jnp.concatenate(ends, axis=0),
                precision=lax.Precision.HIGHEST,
                preferred_element_type=F32,
            )
        for start in range(0, plan.kappas, STEP):
            if plan.place(start, 0)[1] != row:
                continue
            points = []
            for mu in range(tile):
                device, _, sign = plan.place(start, mu)
                re = spectrum[device, row : row + STEP].astype(F32)
                im = spectrum[device, half + row : half + row + STEP].astype(F32) * sign
                points.append((re, im))
            at = slice(start, start + STEP)
            second = slice(plan.kappas + start, plan.kappas + start + STEP)
            turns = powers(twiddle[0, at], twiddle[1, at], tile)
            for cell, (re, im) in enumerate(transform(points, 1)):
                if cell:
                    c, s = turns[cell]
                    re, im = re * c - im * s, im * c + re * s
                if start == 0:
                    re = jnp.where(first, shared[cell : cell + 1], re)
                    im = jnp.where(first, shared[tile + cell : tile + cell + 1], im)
                here = (cell % group) * rows
                work[cell // group, at, here : here + rows] = re.astype(BF16)
                work[cell // group, second, here : here + rows] = im.astype(BF16)
    load_table.wait()
    weights = dot(chosen, table[0]).astype(BF16)
    weights_low = dot(chosen, table[1]).astype(BF16)
    total = jnp.zeros(picked.shape, F32)
    for chunk in range(tile // group):
        field = dot(weights, work[chunk]) + dot(weights_low, work[chunk])
        field = jnp.where(mask, field, 0.0).astype(BF16)
        total = total + lax.dot_general(
            field,
            spread_lanes(plan, lanes, chunk),
            (((1,), (1,)), ((), ())),
            preferred_element_type=F32,
        )
    picked[...] = total.astype(BF16)
    stores = Copies(outs)
    stores.start(picked, out)
    stores.wait()


def turn_by(point, cosine, sine):
    re, im = point
    return re * cosine - im * sine, im * cosine + re * sine


def columns(plan, origin, spectrum_in, green_in, both_in, twiddle_in, out, spectrum, green, both, twiddle, result, work, rows16, ins, outs):
    loads, stores = Copies(ins), Copies(outs)
    arriving = start_columns(plan, loads, spectrum_in, spectrum, both_in, both, twiddle_in, twiddle)
    load_green = loads.start(green_in, green)
    every_column(
        plan, origin, arriving, spectrum, green, both, twiddle, load_green.wait, stores, out,
        result, work, rows16,
    )
    stores.wait()


def start_columns(plan, loads, spectrum_in, spectrum, both_in, both, twiddle_in, twiddle):
    arriving = []
    for start in range(0, plan.half, STEP):
        for at in (start, plan.half + start):
            here = pl.ds(at, STEP)
            arriving.append(loads.start(spectrum_in.at[:, here, :], spectrum.at[:, here, :]))
        if start == 0:
            arriving.append(loads.start(twiddle_in, twiddle))
            arriving.append(loads.start(both_in, both))
    return arriving


def every_column(plan, origin, arriving, spectrum, green, both, twiddle, need_green, stores, out, result, work, rows16):
    devices, rows, half = plan.devices, plan.rows, plan.half
    outer, inner = plan.factors()
    holds_edge = origin[0] == 1
    tall = 2 * half + STEP
    groups = [(start, half + start, STEP) for start in range(0, half, STEP)]
    groups.insert(1, (2 * half, 2 * half + 8, 8))
    top = (lax.broadcasted_iota(jnp.int32, (STEP, rows), 0) == 0) & holds_edge

    def constant(cell, low, sign):
        angle = 2 * math.pi * cell * low / devices
        return math.cos(angle), sign * math.sin(angle)

    def source(s, start):
        if start == 2 * half:
            shared = spectrum[s, half : half + STEP].astype(F32)
            return jnp.where(top, shared, 0.0)[0:8], jnp.zeros((8, rows), F32)
        re = spectrum[s, start : start + STEP].astype(F32)
        im = spectrum[s, half + start : half + start + STEP].astype(F32)
        return re, (jnp.where(top, 0.0, im) if start == 0 else im)

    arriving = list(arriving)
    for first, second, size in groups:
        at_re, at_im = slice(first, first + size), slice(second, second + size)
        if size == STEP:
            for copy in arriving[: 4 if first == 0 else 2]:
                copy.wait()
            arriving = arriving[4 if first == 0 else 2 :]
        for b in range(inner):
            points = [source(a * inner + b, first) for a in range(outer)]
            for low, point in enumerate(transform(points, -1)):
                if low and b:
                    point = turn_by(point, *constant(b, low, -1))
                work[low * inner + b, at_re], work[low * inner + b, at_im] = point
        for low in range(outer):
            base = low * inner
            points = [(work[base + b, at_re], work[base + b, at_im]) for b in range(inner)]
            for high, point in enumerate(transform(points, -1)):
                c, s = (twiddle[part, base + high : base + high + 1] for part in (0, 1))
                re, im = turn_by(point, c, -s)
                if size == 8:
                    both_parts = jnp.concatenate([re, im], axis=0)
                    rows16[base + high, 2 * half : tall] = both_parts.astype(BF16)
                else:
                    rows16[base + high, at_re] = re.astype(BF16)
                    rows16[base + high, at_im] = im.astype(BF16)
    need_green()
    batch = 4
    spans = [(0, half, 2 * half), (2 * half, 2 * half + 8, tall)]

    def product(values):
        flat = values.reshape(batch * tall, rows)
        twice = jnp.concatenate([flat, flat], axis=1)
        return dot(twice, both[...]).reshape(batch, tall, 2 * rows)

    def middle(i, carry):
        at = pl.ds(i * batch, batch)
        u = product(rows16[at])
        g = green[at]
        parts = []
        for (a, b, c), here in zip(spans, (g[:, :half], g[:, half:])):
            parts.append((u[:, a:b, :rows] + u[:, b:c, rows:]) * here)
            parts.append((u[:, b:c, :rows] - u[:, a:b, rows:]) * here)
        u = product(jnp.concatenate(parts, axis=1).astype(BF16))
        turn_c, turn_s = twiddle[0, at][:, None, :], twiddle[1, at][:, None, :]
        for a, b, c in spans:
            re = u[:, a:b, :rows] - u[:, b:c, rows:]
            im = u[:, b:c, :rows] + u[:, a:b, rows:]
            work[at, a:b], work[at, b:c] = turn_by((re, im), turn_c, turn_s)
        return carry

    lax.fori_loop(0, devices // batch, middle, 0)

    for first, second, size in [groups[1], groups[0], *groups[2:]]:
        at_re, at_im = slice(first, first + size), slice(second, second + size)
        for low in range(outer):
            base = low * inner
            points = [(work[base + high, at_re], work[base + high, at_im]) for high in range(inner)]
            for b, point in enumerate(transform(points, 1)):
                if low and b:
                    point = turn_by(point, *constant(b, low, 1))
                work[base + b, at_re], work[base + b, at_im] = point
        for b in range(inner):
            points = [
                (work[low * inner + b, at_re], work[low * inner + b, at_im])
                for low in range(outer)
            ]
            for a, (re, im) in enumerate(transform(points, 1)):
                s = a * inner + b
                if size == 8:
                    work[s, at_re] = re
                    continue
                if first == 0:
                    im = jnp.where(top, work[s, 2 * half : 2 * half + STEP], im)
                result[s, at_re] = re.astype(BF16)
                result[s, at_im] = im.astype(BF16)
        if size == STEP:
            for at in (first, second):
                here = pl.ds(at, STEP)
                stores.start(result.at[:, here, :], out.at[:, here, :])


def first_columns(plan, origin, follows, spectrum_in, own_in, early_in, late_in, head_in, extra_in, both_in, twiddle_in, out, weights_out, spectrum, green, both, twiddle, result, work, rows16, own, early, late, head, extra, ins, outs):
    half, rows, ahead = plan.half, plan.rows, early.shape[0]
    loads, stores = Copies(ins), Copies(outs)
    arriving = start_columns(plan, loads, spectrum_in, spectrum, both_in, both, twiddle_in, twiddle)
    parts = ((own_in, own), (early_in, early), (late_in, late), (head_in, head), (extra_in, extra))
    parts = [loads.start(source, target) for source, target in parts]

    def need_green():
        for copy in parts:
            copy.wait()
        scale = 0.5 / (plan.grid * plan.grid)
        replaced = lax.broadcasted_iota(jnp.int32, (half, rows), 0) == 0
        replaced = replaced & (follows[0] == 0)
        top = lax.broadcasted_iota(jnp.int32, (8, rows), 0) == 0
        for s in range(plan.devices):
            received = early[s] if s < ahead else late[s - ahead]
            total = own[s] + received.astype(F32)
            total = jnp.where(replaced, jnp.broadcast_to(head[s : s + 1], total.shape), total)
            green[s, 0:half] = total * scale
            second = jnp.broadcast_to(extra[s : s + 1], top.shape)
            green[s, half : half + 8] = jnp.where(top, second, 0.0) * scale
        stores.start(green, weights_out)

    every_column(
        plan, origin, arriving, spectrum, green, both, twiddle, need_green, stores, out,
        result, work, rows16,
    )
    stores.wait()


def mirrored_green(plan, green, pick, turn, early, late, edge, edge_turned, picked):
    devices, rows, half = plan.devices, plan.rows, plan.half
    picked[...] = dot(green[...].astype(BF16), pick[...])
    for m in range(devices):
        block = picked[pl.ds(m, rows, stride=devices), :].T
        turned = dot(block.astype(BF16), turn[0 if m == 0 else 1])
        here, there = plan.place_of(m), plan.place_of((devices - m) % devices)
        if there < early.shape[0]:
            early[there] = turned[0:half].astype(BF16)
        else:
            late[there - early.shape[0]] = turned[0:half].astype(BF16)
        edge[here : here + 1] = block[half : half + 1]
        edge_turned[there : there + 1] = turned[half : half + 1]


def own_green(plan, follows, green, own):
    devices, rows, half = plan.devices, plan.rows, plan.half
    partner = follows[0] == 1
    first = lax.broadcasted_iota(jnp.int32, (half, rows), 0) == 0
    for m in range(devices):
        turned = green[pl.ds(m, rows, stride=devices), :].T
        swap = jnp.broadcast_to(turned[half : half + 1], (half, rows))
        own[plan.place_of(m)] = jnp.where(first & partner, swap, turned[0:half])


def slot_choice(owners, capacity, slots):
    blocks = owners.shape[1]
    across = jnp.broadcast_to(owners[...].astype(F32), (blocks, blocks))
    first = lax.broadcasted_iota(jnp.int32, across.shape, 0)
    second = lax.broadcasted_iota(jnp.int32, across.shape, 1)
    earlier = jnp.where((across.T == across) & (first < second), 1.0, 0.0)
    slot = across[0:1] * capacity + jnp.sum(earlier, axis=0, keepdims=True)
    place = lax.broadcasted_iota(jnp.int32, (slots, blocks), 0)
    return jnp.where(place == slot.astype(jnp.int32), 1.0, 0.0)


def own_lanes(block_size):
    row = lax.broadcasted_iota(jnp.int32, (STEP, STEP * block_size), 0)
    lane = lax.broadcasted_iota(jnp.int32, (STEP, STEP * block_size), 1)
    return row == lane // block_size


def block_rows(stencil, group):
    _, block_size, cells = stencil.shape
    return stencil[group * STEP : (group + 1) * STEP].reshape(STEP * block_size, cells)


def start_blocks(loads, source, target):
    copies = []
    for group in range(source.shape[0] // STEP):
        here = pl.ds(group * STEP, STEP)
        copies.append(loads.start(source.at[here], target.at[here]))
    return copies


def project(values, stencil, chosen, need):
    mine = own_lanes(stencil.shape[1])
    tiles = []
    for group in range(values.shape[0]):
        spread = jnp.where(mine, jnp.broadcast_to(values[group : group + 1], mine.shape), 0.0)
        need(group)
        tiles.append(dot(spread.astype(BF16), block_rows(stencil, group)))
    tiles = jnp.concatenate(tiles, axis=0)
    high = tiles.astype(BF16)
    low = (tiles - high.astype(F32)).astype(BF16)
    return dot(chosen, high) + dot(chosen, low)


def interpolate(returned, stencil, chosen, need):
    mine = own_lanes(stencil.shape[1])
    own = lax.dot_general(
        chosen, returned[...], (((0,), (0,)), ((), ())), preferred_element_type=F32
    ).astype(BF16)
    far = []
    for group in range(stencil.shape[0] // STEP):
        need(group)
        every = lax.dot_general(
            own[group * STEP : (group + 1) * STEP],
            block_rows(stencil, group),
            (((1,), (1,)), ((), ())),
            preferred_element_type=F32,
        )
        far.append(jnp.sum(jnp.where(mine, every, 0.0), axis=0, keepdims=True))
    return jnp.concatenate(far, axis=0)


def first_tiles(capacity, owners_in, tiles_in, values_in, stencil_in, out, owners, tiles, values, stencil, tosend, ins, outs):
    slots, cells = out.shape[0], stencil.shape[2]
    loads, stores = Copies(ins), Copies(outs)
    small = [
        loads.start(owners_in, owners),
        loads.start(tiles_in, tiles),
        loads.start(values_in, values),
    ]
    blocks = start_blocks(loads, stencil_in, stencil)
    for copy in small:
        copy.wait()
    chosen = slot_choice(owners, capacity, slots)
    marks = jnp.sum(chosen * (tiles[...] + 1).astype(F32), axis=1, keepdims=True)
    tosend[:, cells:] = jnp.broadcast_to(marks, (slots, out.shape[1] - cells))
    tosend[:, :cells] = project(
        values[...].astype(F32), stencil, chosen.astype(BF16), lambda group: blocks[group].wait()
    )
    stores.start(tosend, out)
    stores.wait()


def middle_blocks(capacity, owners_in, returned_in, near_in, target_in, stencil_in, potentials, residual, out, owners, returned, near, target, stencil, tosend, ins, outs):
    loads, stores = Copies(ins), Copies(outs)
    first = [loads.start(owners_in, owners), loads.start(returned_in, returned)]
    blocks = start_blocks(loads, stencil_in, stencil)
    later = [loads.start(near_in, near), loads.start(target_in, target)]
    for copy in first:
        copy.wait()
    chosen = slot_choice(owners, capacity, out.shape[0]).astype(BF16)
    far = interpolate(returned, stencil, chosen, lambda group: blocks[group].wait())
    for copy in later:
        copy.wait()
    total = far + near[...]
    potentials[...] = total
    rounded = (total - target[...]).astype(BF16)
    residual[...] = rounded
    tosend[...] = project(rounded.astype(F32), stencil, chosen, lambda group: None)
    stores.start(tosend, out)
    stores.wait()


def last_blocks(capacity, owners_in, returned_in, near_in, stencil_in, gradient, owners, returned, near, stencil, ins):
    loads = Copies(ins)
    first = [loads.start(owners_in, owners), loads.start(returned_in, returned)]
    blocks = start_blocks(loads, stencil_in, stencil)
    last = loads.start(near_in, near)
    for copy in first:
        copy.wait()
    chosen = slot_choice(owners, capacity, returned.shape[0]).astype(BF16)
    far = interpolate(returned, stencil, chosen, lambda group: blocks[group].wait())
    last.wait()
    gradient[...] = far + near[...]


def kernel(body, plan, out_shape, scratch, scalars, operands):
    in_specs = [pl.BlockSpec(memory_space=pltpu.SMEM)] * len(scalars)
    in_specs += [pl.BlockSpec(memory_space=pltpu.VMEM)] * len(operands)
    return pl.pallas_call(
        functools.partial(body, plan),
        out_shape=out_shape,
        in_specs=in_specs,
        out_specs=jax.tree.map(lambda _: pl.BlockSpec(memory_space=pltpu.VMEM), out_shape),
        scratch_shapes=scratch,
        compiler_params=pltpu.CompilerParams(vmem_limit_bytes=WIDE),
    )(*scalars, *operands)


def streamed(
    body, plan, out_shape, out_spaces, scratch, copies, scalars, operands, grant=WIDE
):
    in_specs = [pl.BlockSpec(memory_space=pltpu.SMEM)] * len(scalars)
    in_specs += [pl.BlockSpec(memory_space=pl.ANY)] * len(operands)
    semaphores = [pltpu.SemaphoreType.DMA((count,)) for count in copies]
    return pl.pallas_call(
        functools.partial(body, plan),
        out_shape=out_shape,
        in_specs=in_specs,
        out_specs=jax.tree.map(lambda space: pl.BlockSpec(memory_space=space), out_spaces),
        scratch_shapes=[*scratch, *semaphores],
        compiler_params=pltpu.CompilerParams(vmem_limit_bytes=grant),
    )(*scalars, *operands)


def held(*arrays):
    return [pltpu.VMEM(array.shape, array.dtype) for array in arrays]


def leaving_green(plan, green):
    devices, half, rows = plan.devices, plan.half, plan.rows
    pick, turn = plan.mirror_tables()
    ahead = devices // 2
    early = jax.ShapeDtypeStruct((ahead, half, rows), BF16)
    late = jax.ShapeDtypeStruct((devices - ahead, half, rows), BF16)
    line = jax.ShapeDtypeStruct((devices, rows), F32)
    return kernel(
        mirrored_green,
        plan,
        (early, late, line, line),
        [pltpu.VMEM((plan.grid, half + STEP), F32)],
        [],
        [green, jnp.asarray(pick), jnp.asarray(turn)],
    )


def staying_green(plan, green):
    devices, half, rows, per_mu = plan.devices, plan.half, plan.rows, plan.per_mu
    partner = lax.axis_index(AXES) % per_mu >= per_mu // 2
    return kernel(
        own_green,
        plan,
        jax.ShapeDtypeStruct((devices, half, rows), F32),
        [],
        [partner.astype(jnp.int32).reshape(1)],
        [green],
    )


def swap_mirrored(plan, part):
    return lax.ppermute(part, AXES, [(i, plan.devices - 1 - i) for i in range(plan.devices)])


def swap_edges(plan, edge, edge_turned):
    devices, per_mu, tile = plan.devices, plan.per_mu, plan.tile
    upper = range(tile // 2, tile)
    plain = [(devices // 2, 0)]
    plain += [(per_mu * (m - tile // 2) + per_mu // 2, per_mu * m) for m in upper]
    mirror = [(devices // 2, 0)]
    mirror += [(per_mu * (tile - 1 - m + tile // 2) + per_mu // 2, per_mu * m) for m in upper]
    for i in range(1, devices):
        low = i % per_mu
        if low < per_mu // 2 and (low or i // per_mu < tile // 2):
            mirror.append((devices - i, i))
    return lax.ppermute(edge, AXES, plain), lax.ppermute(edge_turned, AXES, mirror)


def edge_lines(plan, edges, swapped_edges):
    edge, edge_turned = edges
    edge_plain, edge_mirror = swapped_edges
    me = lax.axis_index(AXES)
    mu, part = me // plan.per_mu, me % plan.per_mu
    shared = (part == 0) & (mu >= plan.tile // 2)
    head = jnp.where(shared, edge_plain, edge) + jnp.where(me == 0, edge_turned, edge_mirror)
    return head, edge_plain + edge_mirror


def local(charges, target, stencil, near_matrix, green, block_dest, block_tile, near_offset):
    devices = lax.axis_size(AXES)
    blocks, block_size, cell_count = stencil.shape
    pair_count = near_offset.shape[1]
    capacity = 2 * blocks // devices
    slots = devices * capacity
    plan = Plan(green.shape[0], math.isqrt(cell_count), devices)
    me = lax.axis_index(AXES)
    owners = block_dest.reshape(1, blocks)
    groups = (blocks // STEP, STEP * block_size)
    forward_table = jnp.asarray(plan.forward_table())
    inverse_table = jnp.asarray(plan.inverse_table())
    twiddle = jnp.asarray(plan.column_twiddles())
    edge_forward, edge_inverse = (jnp.asarray(t) for t in plan.edge_tables())
    both, row_twiddle = (jnp.asarray(t) for t in plan.row_tables())
    origin = (me == 0).astype(jnp.int32).reshape(1)
    partner = (me % plan.per_mu >= plan.per_mu // 2).astype(jnp.int32).reshape(1)
    early, late, *edges = leaving_green(plan, green)
    spectrum_shape = jax.ShapeDtypeStruct((devices, plan.width, plan.rows), BF16)
    tall_shape = (devices, 2 * plan.half + STEP, plan.rows)
    half_steps = plan.half // STEP
    green_shape = jax.ShapeDtypeStruct((devices, plan.half + 8, plan.rows), F32)
    column_work = [
        pltpu.VMEM(spectrum_shape.shape, BF16),
        pltpu.VMEM(tall_shape, F32),
        pltpu.VMEM(tall_shape, BF16),
    ]
    work_shape = (plan.tile // plan.group, plan.tile_cols, plan.group * plan.rows)

    def exchange(values):
        return lax.all_to_all(values, AXES, split_axis=0, concat_axis=0, tiled=True)

    def to_columns(arrived, marked, grant):
        return streamed(
            forward_rows,
            plan,
            spectrum_shape,
            pl.ANY,
            [
                pltpu.VMEM((slots, cell_count), F32),
                pltpu.VMEM((slots, 128), F32),
                *held(forward_table, twiddle, edge_forward),
                pltpu.VMEM(work_shape, F32),
                pltpu.VMEM(spectrum_shape.shape, BF16),
            ],
            (5, devices),
            [],
            [arrived, marked, forward_table, twiddle, edge_forward],
            grant,
        )

    def along_columns(spectrum, weights):
        return streamed(
            columns,
            plan,
            spectrum_shape,
            pl.ANY,
            [*held(spectrum, weights, both, row_twiddle), *column_work],
            (2 * half_steps + 3, 2 * half_steps),
            [origin],
            [spectrum, weights, both, row_twiddle],
            NARROW,
        )

    def to_rows(spectrum, marked):
        picked = streamed(
            inverse_rows,
            plan,
            jax.ShapeDtypeStruct((slots, cell_count), BF16),
            pl.ANY,
            [
                pltpu.VMEM(spectrum_shape.shape, BF16),
                pltpu.VMEM((slots, 128), F32),
                *held(inverse_table, twiddle, edge_inverse),
                pltpu.VMEM(work_shape, BF16),
                pltpu.VMEM((slots, cell_count), BF16),
            ],
            (2 * half_steps + 4, 1),
            [],
            [spectrum, marked, inverse_table, twiddle, edge_inverse],
            NARROW,
        )
        return exchange(picked.reshape(devices, capacity, cell_count)).reshape(slots, cell_count)

    couple = near_matrix.reshape(blocks, pair_count, block_size, block_size)
    positions = jnp.arange(blocks, dtype=jnp.int32)[:, None] + REACH + near_offset
    charge_blocks = charges.reshape(blocks, block_size)
    extended = extended_2(charge_blocks, ((AXES, 0),), REACH)
    sources = extended[positions]

    tiles = block_tile.reshape(1, blocks)
    values = charges.reshape(groups)
    outgoing_shape = jax.ShapeDtypeStruct((slots, cell_count + 128), F32)
    outgoing = streamed(
        first_tiles,
        capacity,
        outgoing_shape,
        pl.ANY,
        held(owners, tiles, values, stencil, outgoing_shape),
        (3 + groups[0], 1),
        [],
        [owners, tiles, values, stencil],
    )
    swapped_edges = swap_edges(plan, *edges)
    arrived = exchange(outgoing.reshape(devices, capacity, -1)).reshape(slots, -1)
    early = swap_mirrored(plan, early)
    arrived, late, edges, couple = lax.optimization_barrier((arrived, late, edges, couple))
    late = swap_mirrored(plan, late)
    marked = arrived
    spectrum = to_columns(arrived, marked, WIDE)
    spectrum, early = lax.optimization_barrier((spectrum, early))
    lines = edge_lines(plan, edges, swapped_edges)
    own = staying_green(plan, green)
    spectrum, couple, sources, own = lax.optimization_barrier(
        (exchange(spectrum), couple, sources, own)
    )
    green_parts = [own, early, late, *lines]
    spectrum, weights = streamed(
        first_columns,
        plan,
        (spectrum_shape, green_shape),
        (pl.ANY, pl.ANY),
        [
            *held(spectrum, green_shape, both, row_twiddle),
            *column_work,
            *held(*green_parts),
        ],
        (2 * half_steps + 2 + len(green_parts), 2 * half_steps + 1),
        [origin, partner],
        [spectrum, *green_parts, both, row_twiddle],
    )
    returned = to_rows(exchange(spectrum), marked)
    near = jnp.einsum("bkps,bks->bp", couple, sources, preferred_element_type=F32)
    near, target = near.reshape(groups), target.reshape(groups)
    outgoing_shape = jax.ShapeDtypeStruct((slots, cell_count), F32)
    potentials, residual, outgoing = streamed(
        middle_blocks,
        capacity,
        (
            jax.ShapeDtypeStruct(groups, F32),
            jax.ShapeDtypeStruct(groups, BF16),
            outgoing_shape,
        ),
        (pltpu.VMEM, pltpu.VMEM, pl.ANY),
        held(owners, returned, near, target, stencil, outgoing_shape),
        (4 + groups[0], 1),
        [],
        [owners, returned, near, target, stencil],
    )

    arrived = exchange(outgoing.reshape(devices, capacity, -1)).reshape(slots, -1)
    residual = residual.reshape(blocks, block_size)
    terms = jnp.einsum("bkps,bp->bks", couple, residual, preferred_element_type=F32)
    spectrum = exchange(to_columns(arrived, marked, NARROW))
    spectrum, terms = lax.optimization_barrier((spectrum, terms))
    spectrum = exchange(along_columns(spectrum, weights))
    extended = jnp.zeros((blocks + 2 * REACH, block_size), F32)
    extended = extended.at[positions.reshape(-1)].add(terms.reshape(-1, block_size))
    rims = jnp.concatenate([extended[:REACH], extended[blocks + REACH :]], axis=0)
    neighbour = extended_2(rims, ((AXES, 0),), REACH)
    own_part = extended[REACH : blocks + REACH]
    own_part = own_part.at[:REACH].add(neighbour[:REACH])
    own_part = own_part.at[blocks - REACH :].add(neighbour[3 * REACH :])
    returned, near = to_rows(spectrum, marked), own_part.reshape(groups)
    gradient = streamed(
        last_blocks,
        capacity,
        jax.ShapeDtypeStruct(groups, F32),
        pltpu.VMEM,
        held(owners, returned, near, stencil),
        (3 + groups[0],),
        [],
        [owners, returned, near, stencil],
    )
    return (potentials.reshape(-1), gradient.reshape(-1))


def solution(mesh):
    rows = P(AXES)
    return jax.shard_map(
        local,
        mesh=mesh,
        in_specs=(rows, rows, rows, rows, P(None, AXES), rows, rows, rows),
        out_specs=(rows, rows),
        check_vma=False,
    )
```

time: 272 us -> 245 us (0.901)
  waiting for transfers between devices: 30.1 us -> 70.6 us
  blocking collectives: 41.9 us -> 13.6 us
  local copies, waits for them, and re-layouts: 59.2 us -> 34.3 us
  Pallas kernels: 36.2 us -> 54.1 us
  other arithmetic: 18 us -> 3.29 us
  matrix products: 27.2 us -> 15.3 us
  starting transfers between devices: 55.9 us -> 51.4 us
    pallas_call x0 -> x9, Pallas kernels: none -> 45.6 us  [streamed(): pl.pallas_call(functools.partial(body, plan), out_shape=out_shape, in_spe...]
    all_to_all x2 -> x1, blocking collectives: 41.9 us -> 13.6 us  [exchange(): return lax.all_to_all(values, AXES, split_axis=0, concat_axis=0, tiled=True)]
    pallas_call x8 -> x2, Pallas kernels: 36.2 us -> 8.46 us  [kernel(): pl.pallas_call(functools.partial(body, plan), out_shape=out_shape, in_spe...]
    all_to_all x6 -> x7, waiting for transfers between devices: 30.1 us -> 55.6 us  [exchange(): return lax.all_to_all(values, AXES, split_axis=0, concat_axis=0, tiled=True)]
    ppermute x1, waiting for transfers between devices: 0.01 us -> 14.7 us  [swap_edges(): lax.ppermute(edge, AXES, plain)]
    dot_general x4 -> x0, matrix products: 11.2 us -> none  [the longest x2 6.91 us: interpolate(): jnp.einsum('bpt,bt->bp', stencil, own_tiles, preferred_element_type=F32)]
    unnamed x75 -> x45, local copies, waits for them, and re-layouts: 22.2 us -> 11 us
    reshape x1 -> x5, local copies, waits for them, and re-layouts: 0.69 us -> 4.19 us  [the longest x2 1.34 us: local(): near, target = (near.reshape(groups), target.reshape(groups))]
  transfers between devices with their start and end apart: 14 -> 15, of which waited for: 5 -> 8; matrix products, arithmetic and copies ran while one was open for 28% -> 19% of each run, Pallas kernels for 3% -> 7%
where the time goes in v2:
time: 245 us; the launch traced here: 244 us
  waiting for transfers between devices  70.6 us (29%)
  Pallas kernels  54.1 us (22%)
  starting transfers between devices  51.4 us (21%)
  local copies, waits for them, and re-layouts  34.3 us (14%)
  matrix products  15.3 us (6%)
  blocking collectives  13.6 us (6%)
  other arithmetic  3.29 us (1%)
    all_to_all x7, waiting for transfers between devices, exchange(): return lax.all_to_all(values, AXES, split_axis=0, concat_axis=0, tiled=True)  55.6 us
    pallas_call x9, Pallas kernels, streamed(): pl.pallas_call(functools.partial(body, plan), out_shape=out_shape, in_spe...  45.6 us
    all_to_all x7, starting transfers between devices, exchange(): return lax.all_to_all(values, AXES, split_axis=0, concat_axis=0, tiled=True)  30.4 us
    optimization_barrier x1, local copies, waits for them, and re-layouts, local(): lax.optimization_barrier((exchange(spectrum), couple, sources, own))  15.7 us
    ppermute x1, waiting for transfers between devices, swap_edges(): lax.ppermute(edge, AXES, plain)  14.7 us
    all_to_all x1, blocking collectives, exchange(): return lax.all_to_all(values, AXES, split_axis=0, concat_axis=0, tiled=True)  13.6 us
    unnamed x45, local copies, waits for them, and re-layouts  11 us
    dot_general x1, matrix products, local(): jnp.einsum('bkps,bp->bks', couple, residual, preferred_element_type=F32)  10.7 us
  transfers between devices with their start and end apart: 15, of which 8 were waited for; matrix products, arithmetic and copies ran while one was open for 19% of the time, Pallas kernels for 7%

profile of v2, /device:TPU:0, one launch (start us, length us, event | category | flops | bytes accessed | tf_op | source)
XLA Modules:
  0.0 243.6 jit_solution(11369829319396009203)
XLA Ops:
  2.0 4.1 %shard_map.176 = f32[256,384]{1,0:T(8,128)} custom-call(s32[1,128]{1,0:T(1,128)} %bitcast.47, s32[1,128]{1,0:T(1,128)} %bitcast.51, bf16[8,1024]{1,0:T(8,128)(2,1)} %reshape.184.values_in, bf16[128,64,256]{2,1,0:T(8,128)(2,1)} %stencil_in.5), custom_call_target="tpu_custom_call" | custom-call | tf_op jit(solution)/shard_map/pallas_call | solution.py:681
  6.1 7.3 %all-to-all-start = ((f32[32,8,384]{2,1,0:T(8,128)}), f32[32,8,384]{2,1,0:T(8,128)S(1)}, u32[]{:S(2)}, u32[]{:S(2)}) async-start(f32[32,8,384]{2,1,0:T(8,128)} %bitcast.38), calls=%async_computation | async-start | bytes 786432 | tf_op jit(solution)/shard_map/all_to_all | solution.py:783
  13.4 4.6 %shard_map.177 = (bf16[16,64,128]{2,1,0:T(8,128)(2,1)}, bf16[16,64,128]{2,1,0:T(8,128)(2,1)}, f32[32,128]{1,0:T(8,128)}, f32[32,128]{1,0:T(8,128)}) custom-call(f32[4096,128]{1,0:T(8,128)} %green.3, bf16[128,80]{1,0:T(8,128)(2,1)} %constant.131.clone.pick, bf16[2,128,128]{2,1,0:T(8,128)(2,1)} %constant.132.clone.turn), custom_call_target="tpu_custom_call" | custom-call | tf_op jit(solution)/shard_map/pallas_call | solution.py:665
  18.1 5.3 %collective-permute-start = (bf16[16,64,128]{2,1,0:T(8,128)(2,1)}, bf16[16,64,128]{2,1,0:T(8,128)(2,1)S(1)}, u32[]{:S(2)}, u32[]{:S(2)}) collective-permute-start(bf16[16,64,128]{2,1,0:T(8,128)(2,1)} %get-tuple-element.52), channel_id=1, source_target_pairs={{0,31},{1,30},{2,29},{3,28},{4,27},{5,26},{6,25},{7,24},{8,23},{9,... | collective-permute-start | bytes 786440 | tf_op jit(solution)/shard_map/ppermute | solution.py:726
  23.3 7.8 %copy.19 = bf16[128,4,4096]{0,2,1:T(8,128)(2,1)} copy(bf16[128,4,4096]{2,1,0:T(4,128)(2,1)} %param.24) | data formatting | bytes 8388608 | tf_op args[3]
  33.0 5.4 %shard_map.178 = bf16[32,128,128]{2,1,0:T(8,128)(2,1)} custom-call(f32[256,384]{1,0:T(8,128)} %bitcast.31, f32[256,384]{1,0:T(8,128)} %bitcast.32, bf16[2,256,256]{2,1,0:T(8,128)(2,1)} %constant.124.clone.table_in, f32[2,128,128]{2,1,0:T(8,128)} %constant.126.clone.twiddle_in, f32[32,32]{1,0:T(8,128)} %constant.127.clone.edge_in), custom_call_target="tpu_custom_call" | custom-call | tf_op jit(solution)/shard_map/pallas_call | solution.py:681
  45.3 5.3 %collective-permute-start.1 = (bf16[8,64]{1,0:T(8,128)(2,1)S(1)}, bf16[8,64]{1,0:T(8,128)(2,1)S(1)}, u32[]{:S(2)}, u32[]{:S(2)}) collective-permute-start(bf16[8,64]{1,0:T(8,128)(2,1)S(1)} %slice.77), channel_id=1, source_target_pairs={{0,1},{1,2},{2,3},{3,4},{4,5},{5,6},{6,7},{7,8},{8,9},{9,10},{10,1... | collective-permute-start | bytes 3080 | tf_op jit(solution)/shard_map/ppermute | solution.py:29
  51.0 3.9 %shard_map.179.own_in = f32[32,64,128]{2,1,0:T(8,128)} custom-call(s32[1]{0:T(128)} %bitcast.2.follows, f32[4096,128]{1,0:T(8,128)} %green.3), custom_call_target="tpu_custom_call" | custom-call | tf_op jit(solution)/shard_map/pallas_call | solution.py:665
  59.3 14.7 %collective-permute-done.4 = f32[32,128]{1,0:T(8,128)S(1)} collective-permute-done((f32[32,128]{1,0:T(8,128)S(1)}, f32[32,128]{1,0:T(8,128)S(1)}, u32[]{:S(2)}, u32[]{:S(2)}) %collective-permute-start.4) | collective-permute-done | bytes 16416 | tf_op jit(solution)/shard_map/ppermute | solution.py:740
  76.1 7.4 %shard_map.180 = (bf16[32,128,128]{2,1,0:T(8,128)(2,1)}, f32[32,72,128]{2,1,0:T(8,128)}) custom-call(s32[1]{0:T(128)} %bitcast.1.origin, s32[1]{0:T(128)} %bitcast.2.follows, bf16[32,128,128]{2,1,0:T(8,128)(2,1)} %copy-done.10, f32[32,64,128]{2,1,0:T(8,128)} %shard_map.179.own_in, bf16[16,64,128]{2,1,0:T(8,128)(2,1)} %copy-done.13, ...), custom_call_target="tpu_custom_call" | custom-call | tf_op jit(solution)/shard_map/pallas_call | solution.py:681
  83.5 6.6 %all-to-all-start.2 = ((bf16[32,128,128]{2,1,0:T(8,128)(2,1)}), bf16[32,128,128]{2,1,0:T(8,128)(2,1)S(1)}, u32[]{:S(2)}, u32[]{:S(2)}) async-start(bf16[32,128,128]{2,1,0:T(8,128)(2,1)} %get-tuple-element.61), calls=%async_computation.2 | async-start | bytes 2097152 | tf_op jit(solution)/shard_map/all_to_all | solution.py:783
  90.7 15.7 %copy.25 = bf16[128,4,64,64]{2,3,1,0:T(8,128)(2,1)} copy(bf16[128,4,64,64]{0,3,2,1:T(8,128)(2,1)} %bitcast.37) | data formatting | bytes 8388608 | tf_op jit(solution)/shard_map/optimization_barrier | solution.py:866
  106.4 9.7 %all-to-all-done.2.spectrum_in = bf16[32,128,128]{2,1,0:T(8,128)(2,1)S(1)} async-done(((bf16[32,128,128]{2,1,0:T(8,128)(2,1)}), bf16[32,128,128]{2,1,0:T(8,128)(2,1)S(1)}, u32[]{:S(2)}, u32[]{:S(2)}) %all-to-all-start.2) | async-done | bytes 1048608 | tf_op jit(solution)/shard_map/all_to_all | solution.py:783
  123.5 4.6 %fusion = f32[128,1,64,1]{2,1,3,0:T(1,128)S(1)} fusion(bf16[128,4,64,64]{2,3,1,0:T(8,128)(2,1)} %copy.25, bf16[128,4,64,1]{2,1,0,3:T(4,128)(2,1)S(1)} %bitcast.44), kind=kOutput, calls=%fused_computation.2 | convolution fusion | flops 4194304 | bytes 4292608 | tf_op jit(solution)/shard_map/bkps,bks->bp/dot_general | solution.py:885
  132.4 5.8 %shard_map.182 = (f32[8,1024]{1,0:T(8,128)}, bf16[8,1024]{1,0:T(8,128)(2,1)}, f32[256,256]{1,0:T(8,128)}) custom-call(s32[1,128]{1,0:T(1,128)} %bitcast.48, bf16[256,256]{1,0:T(8,128)(2,1)} %bitcast.40, f32[8,1024]{1,0:T(8,128)} %reshape.191.near_in, f32[8,1024]{1,0:T(8,128)} %reshape.192.target_in, bf16[128,64,256]{2,1,0:T(8,128)(2,1)} %stencil_in.5), custom_call_target="tpu_custom_call" | custom-call | tf_op jit(solution)/shard_map/pallas_call | solution.py:681
  138.2 13.6 %all_to_all.40 = f32[32,8,256]{2,1,0:T(8,128)S(1)} all-to-all(f32[32,8,256]{2,1,0:T(8,128)} %bitcast.42), channel_id=1, replica_groups=mesh['panel'=8,'slab'=4] {'panel','slab'}, dimensions={0} | all-to-all | bytes 524288 | tf_op jit(solution)/shard_map/all_to_all | solution.py:783
  151.7 4.7 %shard_map.183 = bf16[32,128,128]{2,1,0:T(8,128)(2,1)} custom-call(f32[256,256]{1,0:T(8,128)S(1)} %bitcast.36, f32[256,384]{1,0:T(8,128)S(1)} %bitcast.34, bf16[2,256,256]{2,1,0:T(8,128)(2,1)S(1)} %copy-done.5, f32[2,128,128]{2,1,0:T(8,128)S(1)} %copy-done.2, f32[32,32]{1,0:T(8,128)S(1)} %copy-done.9), custom_call_target="tpu_custom_call" | custom-call | tf_op jit(solution)/shard_map/pallas_call | solution.py:681
  160.2 10.7 %fusion.9 = f32[128,1,4,64]{3,1,2,0:T(1,128)} fusion(bf16[128,4,64,64]{2,3,1,0:T(8,128)(2,1)} %copy.25, bf16[128,64,1,1]{1,2,3,0:T(2,128)(2,1)S(1)} %reshape.230), kind=kOutput, calls=%fused_computation.22 | convolution fusion | flops 4194304 | bytes 4341760 | tf_op jit(solution)/shard_map/bkps,bp->bks/dot_general | solution.py:905
  170.8 14.5 %all-to-all-done.5.spectrum_in = bf16[32,128,128]{2,1,0:T(8,128)(2,1)S(1)} async-done(((bf16[32,128,128]{2,1,0:T(8,128)(2,1)}), bf16[32,128,128]{2,1,0:T(8,128)(2,1)S(1)}, u32[]{:S(2)}, u32[]{:S(2)}) %all-to-all-start.5) | async-done | bytes 1048608 | tf_op jit(solution)/shard_map/all_to_all | solution.py:783
  185.3 6.7 %shard_map.184 = bf16[32,128,128]{2,1,0:T(8,128)(2,1)} custom-call(s32[1]{0:T(128)} %bitcast.1.origin, bf16[32,128,128]{2,1,0:T(8,128)(2,1)S(1)} %all-to-all-done.5.spectrum_in, f32[32,72,128]{2,1,0:T(8,128)S(1)} %copy-done.3, bf16[256,256]{1,0:T(8,128)(2,1)S(1)} %copy-done.6, f32[2,32,128]{2,1,0:T(8,128)S(1)} %copy-done.7), custom_call_target="tpu_custom_call" | custom-call | tf_op jit(solution)/shard_map/pallas_call | solution.py:681
  202.0 19.9 %all-to-all-done.6.spectrum_in = bf16[32,128,128]{2,1,0:T(8,128)(2,1)S(1)} async-done(((bf16[32,128,128]{2,1,0:T(8,128)(2,1)}), bf16[32,128,128]{2,1,0:T(8,128)(2,1)S(1)}, u32[]{:S(2)}, u32[]{:S(2)}) %all-to-all-start.6) | async-done | bytes 1048608 | tf_op jit(solution)/shard_map/all_to_all | solution.py:783
  221.9 3.8 %shard_map.185 = bf16[256,256]{1,0:T(8,128)(2,1)} custom-call(bf16[32,128,128]{2,1,0:T(8,128)(2,1)S(1)} %all-to-all-done.6.spectrum_in, f32[256,384]{1,0:T(8,128)S(1)} %bitcast.35, bf16[2,256,256]{2,1,0:T(8,128)(2,1)S(1)} %copy-done.4, f32[2,128,128]{2,1,0:T(8,128)S(1)} %copy-done.2, f32[32,32]{1,0:T(8,128)S(1)} %copy-done.8), custom_call_target="tpu_custom_call" | custom-call | tf_op jit(solution)/shard_map/pallas_call | solution.py:681
  230.1 7.5 %all-to-all-done.7 = bf16[32,8,256]{2,1,0:T(8,128)(2,1)S(1)} async-done(((bf16[32,8,256]{2,1,0:T(8,128)(2,1)}), bf16[32,8,256]{2,1,0:T(8,128)(2,1)S(1)}, u32[]{:S(2)}, u32[]{:S(2)}) %all-to-all-start.7) | async-done | bytes 131104 | tf_op jit(solution)/shard_map/all_to_all | solution.py:783
  238.2 4.0 %shard_map.186 = f32[8,1024]{1,0:T(8,128)} custom-call(s32[1,128]{1,0:T(1,128)} %bitcast.49, bf16[256,256]{1,0:T(8,128)(2,1)} %bitcast.39, f32[8,1024]{1,0:T(8,128)} %reshape.201.near_in, bf16[128,64,256]{2,1,0:T(8,128)(2,1)} %stencil_in.5), custom_call_target="tpu_custom_call" | custom-call | tf_op jit(solution)/shard_map/pallas_call | solution.py:681
  (92 shorter events, 49.1 us)
Async XLA Ops:
  6.1 44.6 %copy-start.20 = (s32[128,4]{0,1:T(4,128)S(1)}, s32[128,4]{0,1:T(4,128)}, u32[]{:S(2)}) copy-start(s32[128,4]{0,1:T(4,128)} %param.28) | copy-start | bytes 6148
  6.1 26.1 %all-to-all-start = ((f32[32,8,384]{2,1,0:T(8,128)}), f32[32,8,384]{2,1,0:T(8,128)S(1)}, u32[]{:S(2)}, u32[]{:S(2)}) async-start(f32[32,8,384]{2,1,0:T(8,128)} %bitcast.38), calls=%async_computation | async-start | bytes 786432 | tf_op jit(solution)/shard_map/all_to_all | solution.py:783
  18.1 20.3 %collective-permute-start = (bf16[16,64,128]{2,1,0:T(8,128)(2,1)}, bf16[16,64,128]{2,1,0:T(8,128)(2,1)S(1)}, u32[]{:S(2)}, u32[]{:S(2)}) collective-permute-start(bf16[16,64,128]{2,1,0:T(8,128)(2,1)} %get-tuple-element.52), channel_id=1, source_target_pairs={{0,31},{1,30},{2,29},{3,28},{4,27},{5,26},{6,25},{7,24},{8,23},{9,... | collective-permute-start | bytes 786440 | tf_op jit(solution)/shard_map/ppermute | solution.py:726
  31.2 58.9 %copy-start.16 = (f32[8192]{0:T(1024)S(1)}, f32[8192]{0:T(1024)}, u32[]{:S(2)}) copy-start(f32[8192]{0:T(1024)} %param.22) | copy-start | bytes 98308
  38.4 36.6 %all-to-all-start.1 = ((bf16[32,128,128]{2,1,0:T(8,128)(2,1)}), bf16[32,128,128]{2,1,0:T(8,128)(2,1)S(1)}, u32[]{:S(2)}, u32[]{:S(2)}) async-start(bf16[32,128,128]{2,1,0:T(8,128)(2,1)} %shard_map.178), calls=%async_computation.1 | async-start | bytes 2097152 | tf_op jit(solution)/shard_map/all_to_all | solution.py:783
  41.2 32.8 %collective-permute-start.4 = (f32[32,128]{1,0:T(8,128)S(1)}, f32[32,128]{1,0:T(8,128)S(1)}, u32[]{:S(2)}, u32[]{:S(2)}) collective-permute-start(f32[32,128]{1,0:T(8,128)S(1)} %copy-done.18), channel_id=1, source_target_pairs={{16,0},{1,16},{3,18},{5,20},{7,22},{9,24},{11,26},{13,28},{15,30}} | collective-permute-start | bytes 49160 | tf_op jit(solution)/shard_map/ppermute | solution.py:740
  42.5 31.9 %collective-permute-start.5 = (f32[32,128]{1,0:T(8,128)S(1)}, f32[32,128]{1,0:T(8,128)S(1)}, u32[]{:S(2)}, u32[]{:S(2)}) collective-permute-start(f32[32,128]{1,0:T(8,128)S(1)} %copy-done.19), channel_id=1, source_target_pairs={{16,0},{31,16},{29,18},{27,20},{25,22},{23,24},{21,26},{19,28},{17... | collective-permute-start | bytes 49160 | tf_op jit(solution)/shard_map/ppermute | solution.py:740
  43.9 14.0 %collective-permute-start.2 = (bf16[8,64]{1,0:T(8,128)(2,1)S(1)}, bf16[8,64]{1,0:T(8,128)(2,1)S(1)}, u32[]{:S(2)}, u32[]{:S(2)}) collective-permute-start(bf16[8,64]{1,0:T(8,128)(2,1)S(1)} %slice.79), channel_id=1, source_target_pairs={{1,0},{2,1},{3,2},{4,3},{5,4},{6,5},{7,6},{8,7},{9,8},{10,9},{11,1... | collective-permute-start | bytes 3080 | tf_op jit(solution)/shard_map/ppermute | solution.py:31
  45.3 12.7 %collective-permute-start.1 = (bf16[8,64]{1,0:T(8,128)(2,1)S(1)}, bf16[8,64]{1,0:T(8,128)(2,1)S(1)}, u32[]{:S(2)}, u32[]{:S(2)}) collective-permute-start(bf16[8,64]{1,0:T(8,128)(2,1)S(1)} %slice.77), channel_id=1, source_target_pairs={{0,1},{1,2},{2,3},{3,4},{4,5},{5,6},{6,7},{7,8},{8,9},{9,10},{10,1... | collective-permute-start | bytes 3080 | tf_op jit(solution)/shard_map/ppermute | solution.py:29
  54.9 20.2 %collective-permute-start.3 = (bf16[16,64,128]{2,1,0:T(8,128)(2,1)S(1)}, bf16[16,64,128]{2,1,0:T(8,128)(2,1)S(1)}, u32[]{:S(2)}, u32[]{:S(2)}) collective-permute-start(bf16[16,64,128]{2,1,0:T(8,128)(2,1)S(1)} %copy-done.21), channel_id=1, source_target_pairs={{0,31},{1,30},{2,29},{3,28},{4,27},{5,26},{6,25},{7,24},{8,23},{9,... | collective-permute-start | bytes 786440 | tf_op jit(solution)/shard_map/ppermute | solution.py:726
  76.1 40.1 %copy-start.8 = (f32[32,32]{1,0:T(8,128)S(1)}, f32[32,32]{1,0:T(8,128)}, u32[]{:S(2)}) copy-start(f32[32,32]{1,0:T(8,128)} %constant.128.clone.edge_in) | copy-start | bytes 12292
  83.5 32.6 %all-to-all-start.2 = ((bf16[32,128,128]{2,1,0:T(8,128)(2,1)}), bf16[32,128,128]{2,1,0:T(8,128)(2,1)S(1)}, u32[]{:S(2)}, u32[]{:S(2)}) async-start(bf16[32,128,128]{2,1,0:T(8,128)(2,1)} %get-tuple-element.61), calls=%async_computation.2 | async-start | bytes 2097152 | tf_op jit(solution)/shard_map/all_to_all | solution.py:783
  106.4 45.3 %copy-start.5 = (bf16[2,256,256]{2,1,0:T(8,128)(2,1)S(1)}, bf16[2,256,256]{2,1,0:T(8,128)(2,1)}, u32[]{:S(2)}) copy-start(bf16[2,256,256]{2,1,0:T(8,128)(2,1)} %constant.124.clone.table_in) | copy-start | bytes 786436
  106.4 45.3 %copy-start.9 = (f32[32,32]{1,0:T(8,128)S(1)}, f32[32,32]{1,0:T(8,128)}, u32[]{:S(2)}) copy-start(f32[32,32]{1,0:T(8,128)} %constant.127.clone.edge_in) | copy-start | bytes 12292
  119.9 11.9 %all-to-all-start.3 = ((bf16[32,8,256]{2,1,0:T(8,128)(2,1)}), bf16[32,8,256]{2,1,0:T(8,128)(2,1)S(1)}, u32[]{:S(2)}, u32[]{:S(2)}) async-start(bf16[32,8,256]{2,1,0:T(8,128)(2,1)} %bitcast.8), calls=%async_computation.3 | async-start | bytes 262144 | tf_op jit(solution)/shard_map/all_to_all | solution.py:783
  132.4 52.9 %copy-start.3 = (f32[32,72,128]{2,1,0:T(8,128)S(1)}, f32[32,72,128]{2,1,0:T(8,128)}, u32[]{:S(2)}) copy-start(f32[32,72,128]{2,1,0:T(8,128)} %get-tuple-element.68.green_in) | copy-start | bytes 3538948
  132.4 52.9 %copy-start.6 = (bf16[256,256]{1,0:T(8,128)(2,1)S(1)}, bf16[256,256]{1,0:T(8,128)(2,1)}, u32[]{:S(2)}) copy-start(bf16[256,256]{1,0:T(8,128)(2,1)} %constant.129.clone.both_in) | copy-start | bytes 393220
  132.4 52.9 %copy-start.7 = (f32[2,32,128]{2,1,0:T(8,128)S(1)}, f32[2,32,128]{2,1,0:T(8,128)}, u32[]{:S(2)}) copy-start(f32[2,32,128]{2,1,0:T(8,128)} %constant.130.clone.twiddle_in) | copy-start | bytes 98308
  156.4 28.9 %all-to-all-start.5 = ((bf16[32,128,128]{2,1,0:T(8,128)(2,1)}), bf16[32,128,128]{2,1,0:T(8,128)(2,1)S(1)}, u32[]{:S(2)}, u32[]{:S(2)}) async-start(bf16[32,128,128]{2,1,0:T(8,128)(2,1)} %shard_map.183), calls=%async_computation.5 | async-start | bytes 2097152 | tf_op jit(solution)/shard_map/all_to_all | solution.py:783
  170.8 71.4 %copy-start.17 = (f32[8,1024]{1,0:T(8,128)S(1)}, f32[8,1024]{1,0:T(8,128)}, u32[]{:S(2)}) copy-start(f32[8,1024]{1,0:T(8,128)} %get-tuple-element.64) | copy-start | bytes 98308
  192.1 29.8 %all-to-all-start.6 = ((bf16[32,128,128]{2,1,0:T(8,128)(2,1)}), bf16[32,128,128]{2,1,0:T(8,128)(2,1)S(1)}, u32[]{:S(2)}, u32[]{:S(2)}) async-start(bf16[32,128,128]{2,1,0:T(8,128)(2,1)} %shard_map.184), calls=%async_computation.6 | async-start | bytes 2097152 | tf_op jit(solution)/shard_map/all_to_all | solution.py:783
  198.5 30.8 %collective-permute-start.6 = (f32[8,64]{1,0:T(8,128)S(1)}, f32[8,64]{1,0:T(8,128)S(1)}, u32[]{:S(2)}, u32[]{:S(2)}) collective-permute-start(f32[8,64]{1,0:T(8,128)S(1)} %get-tuple-element.73), channel_id=1, source_target_pairs={{0,1},{1,2},{2,3},{3,4},{4,5},{5,6},{6,7},{7,8},{8,9},{9,10},{10,1... | collective-permute-start | bytes 6152 | tf_op jit(solution)/shard_map/ppermute | solution.py:29
  200.7 28.6 %collective-permute-start.7 = (f32[8,64]{1,0:T(8,128)S(1)}, f32[8,64]{1,0:T(8,128)S(1)}, u32[]{:S(2)}, u32[]{:S(2)}) collective-permute-start(f32[8,64]{1,0:T(8,128)S(1)} %get-tuple-element.72), channel_id=1, source_target_pairs={{1,0},{2,1},{3,2},{4,3},{5,4},{6,5},{7,6},{8,7},{9,8},{10,9},{11,1... | collective-permute-start | bytes 6152 | tf_op jit(solution)/shard_map/ppermute | solution.py:31
  225.7 11.9 %all-to-all-start.7 = ((bf16[32,8,256]{2,1,0:T(8,128)(2,1)}), bf16[32,8,256]{2,1,0:T(8,128)(2,1)S(1)}, u32[]{:S(2)}, u32[]{:S(2)}) async-start(bf16[32,8,256]{2,1,0:T(8,128)(2,1)} %bitcast.17), calls=%async_computation.7 | async-start | bytes 262144 | tf_op jit(solution)/shard_map/all_to_all | solution.py:783
  (13 other events, 283.1 us)

commit v3 on v2

--- a/solution.py
+++ b/solution.py
@@ -16,6 +16,7 @@
 WIDE = 56 * 1024 * 1024
 NARROW = 24 * 1024 * 1024
 STEP = 16
+LANES = 128
 
 
 def extended_2(cells, sides, width):
@@ -190,6 +191,17 @@
             copy.wait()
 
 
+class Present:
+    def wait(self):
+        pass
+
+
+def bring(loads, source, target):
+    if target is None:
+        return source, Present()
+    return target, loads.start(source, target)
+
+
 def cell_lanes(plan):
     cells, span = plan.tile * plan.tile, plan.group * plan.rows
     cell = lax.broadcasted_iota(jnp.int32, (cells, span), 0)
@@ -210,15 +222,20 @@
     return out
 
 
+def resident_forward_rows(plan, values, marked, table, twiddle, edge, out, work, lines, outs):
+    none = [None] * 5
+    forward_rows(plan, values, marked, table, twiddle, edge, out, *none, work, lines, None, outs)
+
+
 def forward_rows(plan, values_in, marked_in, table_in, twiddle_in, edge_in, out, values, marked, table, twiddle, edge, work, lines, ins, outs):
     tile, rows, group, half = plan.tile, plan.rows, plan.group, plan.half
-    slots, cells = values.shape[0], tile * tile
+    slots, cells = values_in.shape[0], tile * tile
     loads = Copies(ins)
-    load_marks = loads.start(marked_in.at[:, cells:], marked)
-    load_table = loads.start(table_in, table)
-    load_values = loads.start(values_in.at[:, :cells], values)
-    load_twiddle = loads.start(twiddle_in, twiddle)
-    load_edge = loads.start(edge_in, edge)
+    marked, load_marks = bring(loads, marked_in.at[:, cells:], marked)
+    table, load_table = bring(loads, table_in, table)
+    values, load_values = bring(loads, values_in.at[:, :cells], values)
+    twiddle, load_twiddle = bring(loads, twiddle_in, twiddle)
+    edge, load_edge = bring(loads, edge_in, edge)
     lanes = cell_lanes(plan)
     load_marks.wait()
     marks = marked[...]
@@ -280,33 +297,16 @@
     stores.wait()
 
 
-def inverse_rows(plan, spectrum_in, marked_in, table_in, twiddle_in, edge_in, out, spectrum, marked, table, twiddle, edge, work, picked, ins, outs):
+def inverse_rows(plan, spectrum, marked, table, twiddle, edge, out, work, picked, outs):
     tile, rows, group, half = plan.tile, plan.rows, plan.group, plan.half
     slots, cells = marked.shape[0], tile * tile
-    loads = Copies(ins)
-    load_marks = loads.start(marked_in.at[:, cells:], marked)
-    load_edge = loads.start(edge_in, edge)
-    load_rows = []
-    for row in range(0, half, STEP):
-        both_parts = []
-        for at in (row, half + row):
-            here = pl.ds(at, STEP)
-            both_parts.append(loads.start(spectrum_in.at[:, here, :], spectrum.at[:, here, :]))
-        load_rows.append(both_parts)
-    load_twiddle = loads.start(twiddle_in, twiddle)
-    load_table = loads.start(table_in, table)
     lanes = cell_lanes(plan)
-    load_marks.wait()
-    tile_col, tile_row = slot_tiles(marked[...], plan)
+    tile_col, tile_row = slot_tiles(marked[:, cells:], plan)
     mask = slot_mask(tile_row, plan)
     place = lax.broadcasted_iota(jnp.int32, (slots, plan.tile_cols), 1)
     chosen = (place == tile_col[:, 0:1]).astype(F32).astype(BF16)
-    load_edge.wait()
-    load_twiddle.wait()
     first = lax.broadcasted_iota(jnp.int32, (STEP, rows), 0) == 0
     for row in range(0, half, STEP):
-        for copy in load_rows[row // STEP]:
-            copy.wait()
         if row == 0:
             ends = [spectrum[plan.per_mu * mu, 0:STEP].astype(F32)[0:1] for mu in range(tile)]
             ends += [
@@ -340,7 +340,6 @@
                 here = (cell % group) * rows
                 work[cell // group, at, here : here + rows] = re.astype(BF16)
                 work[cell // group, second, here : here + rows] = im.astype(BF16)
-    load_table.wait()
     weights = dot(chosen, table[0]).astype(BF16)
     weights_low = dot(chosen, table[1]).astype(BF16)
     total = jnp.zeros(picked.shape, F32)
@@ -364,12 +363,10 @@
     return re * cosine - im * sine, im * cosine + re * sine
 
 
-def columns(plan, origin, spectrum_in, green_in, both_in, twiddle_in, out, spectrum, green, both, twiddle, result, work, rows16, ins, outs):
-    loads, stores = Copies(ins), Copies(outs)
-    arriving = start_columns(plan, loads, spectrum_in, spectrum, both_in, both, twiddle_in, twiddle)
-    load_green = loads.start(green_in, green)
+def columns(plan, origin, spectrum, green, both, twiddle, out, result, work, rows16, outs):
+    stores = Copies(outs)
     every_column(
-        plan, origin, arriving, spectrum, green, both, twiddle, load_green.wait, stores, out,
+        plan, origin, [], spectrum, green, both, twiddle, lambda: None, stores, out,
         result, work, rows16,
     )
     stores.wait()
@@ -576,11 +573,14 @@
 
 def project(values, stencil, chosen, need):
     mine = own_lanes(stencil.shape[1])
+    each = mine.shape[1] // LANES
     tiles = []
-    for group in range(values.shape[0]):
-        spread = jnp.where(mine, jnp.broadcast_to(values[group : group + 1], mine.shape), 0.0)
+    for group in range(stencil.shape[0] // STEP):
+        rows = [values[i : i + 1] for i in range(group * each, (group + 1) * each)]
+        spread = jnp.concatenate([jnp.broadcast_to(row, (STEP, LANES)) for row in rows], axis=1)
         need(group)
-        tiles.append(dot(spread.astype(BF16), block_rows(stencil, group)))
+        spread = jnp.where(mine, spread, 0.0).astype(BF16)
+        tiles.append(dot(spread, block_rows(stencil, group)))
     tiles = jnp.concatenate(tiles, axis=0)
     high = tiles.astype(BF16)
     low = (tiles - high.astype(F32)).astype(BF16)
@@ -601,7 +601,8 @@
             (((1,), (1,)), ((), ())),
             preferred_element_type=F32,
         )
-        far.append(jnp.sum(jnp.where(mine, every, 0.0), axis=0, keepdims=True))
+        sums = jnp.sum(jnp.where(mine, every, 0.0), axis=0, keepdims=True)
+        far += [sums[:, i : i + LANES] for i in range(0, mine.shape[1], LANES)]
     return jnp.concatenate(far, axis=0)
 
 
@@ -628,12 +629,13 @@
 
 def middle_blocks(capacity, owners_in, returned_in, near_in, target_in, stencil_in, potentials, residual, out, owners, returned, near, target, stencil, tosend, ins, outs):
     loads, stores = Copies(ins), Copies(outs)
-    first = [loads.start(owners_in, owners), loads.start(returned_in, returned)]
+    load_owners = loads.start(owners_in, owners)
+    load_returned = loads.start(returned_in, returned)
     blocks = start_blocks(loads, stencil_in, stencil)
     later = [loads.start(near_in, near), loads.start(target_in, target)]
-    for copy in first:
-        copy.wait()
+    load_owners.wait()
     chosen = slot_choice(owners, capacity, out.shape[0]).astype(BF16)
+    load_returned.wait()
     far = interpolate(returned, stencil, chosen, lambda group: blocks[group].wait())
     for copy in later:
         copy.wait()
@@ -648,12 +650,13 @@
 
 def last_blocks(capacity, owners_in, returned_in, near_in, stencil_in, gradient, owners, returned, near, stencil, ins):
     loads = Copies(ins)
-    first = [loads.start(owners_in, owners), loads.start(returned_in, returned)]
+    load_owners = loads.start(owners_in, owners)
+    load_returned = loads.start(returned_in, returned)
     blocks = start_blocks(loads, stencil_in, stencil)
     last = loads.start(near_in, near)
-    for copy in first:
-        copy.wait()
+    load_owners.wait()
     chosen = slot_choice(owners, capacity, returned.shape[0]).astype(BF16)
+    load_returned.wait()
     far = interpolate(returned, stencil, chosen, lambda group: blocks[group].wait())
     last.wait()
     gradient[...] = far + near[...]
@@ -675,8 +678,9 @@
 def streamed(
     body, plan, out_shape, out_spaces, scratch, copies, scalars, operands, grant=WIDE
 ):
+    space = pl.ANY if grant == WIDE else pltpu.VMEM
     in_specs = [pl.BlockSpec(memory_space=pltpu.SMEM)] * len(scalars)
-    in_specs += [pl.BlockSpec(memory_space=pl.ANY)] * len(operands)
+    in_specs += [pl.BlockSpec(memory_space=space)] * len(operands)
     semaphores = [pltpu.SemaphoreType.DMA((count,)) for count in copies]
     return pl.pallas_call(
         functools.partial(body, plan),
@@ -759,7 +763,8 @@
     plan = Plan(green.shape[0], math.isqrt(cell_count), devices)
     me = lax.axis_index(AXES)
     owners = block_dest.reshape(1, blocks)
-    groups = (blocks // STEP, STEP * block_size)
+    flat = (blocks * block_size // LANES, LANES)
+    steps = blocks // STEP
     forward_table = jnp.asarray(plan.forward_table())
     inverse_table = jnp.asarray(plan.inverse_table())
     twiddle = jnp.asarray(plan.column_twiddles())
@@ -783,21 +788,23 @@
         return lax.all_to_all(values, AXES, split_axis=0, concat_axis=0, tiled=True)
 
     def to_columns(arrived, marked, grant):
+        operands = [arrived, marked, forward_table, twiddle, edge_forward]
+        copied = [pltpu.VMEM((slots, cell_count), F32), pltpu.VMEM((slots, 128), F32)]
+        copied += held(forward_table, twiddle, edge_forward)
+        wide = grant == WIDE
         return streamed(
-            forward_rows,
+            forward_rows if wide else resident_forward_rows,
             plan,
             spectrum_shape,
             pl.ANY,
             [
-                pltpu.VMEM((slots, cell_count), F32),
-                pltpu.VMEM((slots, 128), F32),
-                *held(forward_table, twiddle, edge_forward),
+                *(copied if wide else []),
                 pltpu.VMEM(work_shape, F32),
                 pltpu.VMEM(spectrum_shape.shape, BF16),
             ],
-            (5, devices),
+            (5, devices) if wide else (devices,),
             [],
-            [arrived, marked, forward_table, twiddle, edge_forward],
+            operands,
             grant,
         )
 
@@ -807,8 +814,8 @@
             plan,
             spectrum_shape,
             pl.ANY,
-            [*held(spectrum, weights, both, row_twiddle), *column_work],
-            (2 * half_steps + 3, 2 * half_steps),
+            column_work,
+            (2 * half_steps,),
             [origin],
             [spectrum, weights, both, row_twiddle],
             NARROW,
@@ -820,14 +827,8 @@
             plan,
             jax.ShapeDtypeStruct((slots, cell_count), BF16),
             pl.ANY,
-            [
-                pltpu.VMEM(spectrum_shape.shape, BF16),
-                pltpu.VMEM((slots, 128), F32),
-                *held(inverse_table, twiddle, edge_inverse),
-                pltpu.VMEM(work_shape, BF16),
-                pltpu.VMEM((slots, cell_count), BF16),
-            ],
-            (2 * half_steps + 4, 1),
+            [pltpu.VMEM(work_shape, BF16), pltpu.VMEM((slots, cell_count), BF16)],
+            (1,),
             [],
             [spectrum, marked, inverse_table, twiddle, edge_inverse],
             NARROW,
@@ -837,11 +838,10 @@
     couple = near_matrix.reshape(blocks, pair_count, block_size, block_size)
     positions = jnp.arange(blocks, dtype=jnp.int32)[:, None] + REACH + near_offset
     charge_blocks = charges.reshape(blocks, block_size)
-    extended = extended_2(charge_blocks, ((AXES, 0),), REACH)
-    sources = extended[positions]
+    sources = extended_2(charge_blocks, ((AXES, 0),), REACH)[positions]
 
     tiles = block_tile.reshape(1, blocks)
-    values = charges.reshape(groups)
+    values = charges.reshape(flat)
     outgoing_shape = jax.ShapeDtypeStruct((slots, cell_count + 128), F32)
     outgoing = streamed(
         first_tiles,
@@ -849,7 +849,7 @@
         outgoing_shape,
         pl.ANY,
         held(owners, tiles, values, stencil, outgoing_shape),
-        (3 + groups[0], 1),
+        (3 + steps, 1),
         [],
         [owners, tiles, values, stencil],
     )
@@ -883,19 +883,19 @@
     )
     returned = to_rows(exchange(spectrum), marked)
     near = jnp.einsum("bkps,bks->bp", couple, sources, preferred_element_type=F32)
-    near, target = near.reshape(groups), target.reshape(groups)
+    near, target = near.reshape(flat), target.reshape(flat)
     outgoing_shape = jax.ShapeDtypeStruct((slots, cell_count), F32)
     potentials, residual, outgoing = streamed(
         middle_blocks,
         capacity,
         (
-            jax.ShapeDtypeStruct(groups, F32),
-            jax.ShapeDtypeStruct(groups, BF16),
+            jax.ShapeDtypeStruct(flat, F32),
+            jax.ShapeDtypeStruct(flat, BF16),
             outgoing_shape,
         ),
         (pltpu.VMEM, pltpu.VMEM, pl.ANY),
         held(owners, returned, near, target, stencil, outgoing_shape),
-        (4 + groups[0], 1),
+        (4 + steps, 1),
         [],
         [owners, returned, near, target, stencil],
     )
@@ -913,14 +913,15 @@
     own_part = extended[REACH : blocks + REACH]
     own_part = own_part.at[:REACH].add(neighbour[:REACH])
     own_part = own_part.at[blocks - REACH :].add(neighbour[3 * REACH :])
-    returned, near = to_rows(spectrum, marked), own_part.reshape(groups)
+    returned = to_rows(spectrum, marked)
+    near = own_part.reshape(flat)
     gradient = streamed(
         last_blocks,
         capacity,
-        jax.ShapeDtypeStruct(groups, F32),
+        jax.ShapeDtypeStruct(flat, F32),
         pltpu.VMEM,
         held(owners, returned, near, stencil),
-        (3 + groups[0],),
+        (3 + steps,),
         [],
         [owners, returned, near, stencil],
     )

time: 245 us -> 239 us (0.976)
  Pallas kernels: 54.1 us -> 50.4 us
  local copies, waits for them, and re-layouts: 34.3 us -> 30.9 us
    pallas_call x9, Pallas kernels: 45.6 us -> 41.9 us  [streamed(): pl.pallas_call(functools.partial(body, plan), out_shape=out_shape, in_spe...]
    reshape x5 -> x2, local copies, waits for them, and re-layouts: 4.77 us -> 1.39 us  [the longest x1 0.71 us: local(): near, target = (near.reshape(flat), target.reshape(flat))]
    unnamed x45 -> x41, local copies, waits for them, and re-layouts: 11 us -> 11 us
  transfers between devices with their start and end apart: 15 -> 15, of which waited for: 8 -> 8; matrix products, arithmetic and copies ran while one was open for 19% -> 20% of each run, Pallas kernels for 7% -> 7%
where the time goes in v3:
time: 239 us; the launch traced here: 237 us
  waiting for transfers between devices  71.3 us (30%)
  starting transfers between devices  51.4 us (22%)
  Pallas kernels  50.4 us (21%)
  local copies, waits for them, and re-layouts  30.9 us (13%)
  matrix products  15.3 us (6%)
  blocking collectives  13.6 us (6%)
  other arithmetic  3.3 us (1%)
    all_to_all x7, waiting for transfers between devices, exchange(): return lax.all_to_all(values, AXES, split_axis=0, concat_axis=0, tiled=True)  56.2 us
    pallas_call x9, Pallas kernels, streamed(): pl.pallas_call(functools.partial(body, plan), out_shape=out_shape, in_spe...  41.9 us
    all_to_all x7, starting transfers between devices, exchange(): return lax.all_to_all(values, AXES, split_axis=0, concat_axis=0, tiled=True)  30.4 us
    optimization_barrier x1, local copies, waits for them, and re-layouts, local(): lax.optimization_barrier((exchange(spectrum), couple, sources, own))  15.6 us
    ppermute x1, waiting for transfers between devices, swap_edges(): lax.ppermute(edge, AXES, plain)  14.7 us
    all_to_all x1, blocking collectives, exchange(): return lax.all_to_all(values, AXES, split_axis=0, concat_axis=0, tiled=True)  13.6 us
    unnamed x41, local copies, waits for them, and re-layouts  11 us
    dot_general x1, matrix products, local(): jnp.einsum('bkps,bp->bks', couple, residual, preferred_element_type=F32)  10.7 us
  transfers between devices with their start and end apart: 15, of which 8 were waited for; matrix products, arithmetic and copies ran while one was open for 20% of the time, Pallas kernels for 7%

profile of v3, /device:TPU:0, one launch (start us, length us, event | category | flops | bytes accessed | tf_op | source)
XLA Modules:
  0.0 237.4 jit_solution(17212068571209066249)
XLA Ops:
  0.6 4.2 %shard_map.176 = f32[256,384]{1,0:T(8,128)} custom-call(s32[1,128]{1,0:T(1,128)} %bitcast.46, s32[1,128]{1,0:T(1,128)} %bitcast.50, bf16[64,128]{1,0:T(8,128)(2,1)} %bitcast.42, bf16[128,64,256]{2,1,0:T(8,128)(2,1)} %stencil_in.5), custom_call_target="tpu_custom_call" | custom-call | tf_op jit(solution)/shard_map/pallas_call | solution.py:685
  4.8 7.3 %all-to-all-start = ((f32[32,8,384]{2,1,0:T(8,128)}), f32[32,8,384]{2,1,0:T(8,128)S(1)}, u32[]{:S(2)}, u32[]{:S(2)}) async-start(f32[32,8,384]{2,1,0:T(8,128)} %bitcast.36), calls=%async_computation | async-start | bytes 786432 | tf_op jit(solution)/shard_map/all_to_all | solution.py:788
  12.1 4.6 %shard_map.177 = (bf16[16,64,128]{2,1,0:T(8,128)(2,1)}, bf16[16,64,128]{2,1,0:T(8,128)(2,1)}, f32[32,128]{1,0:T(8,128)}, f32[32,128]{1,0:T(8,128)}) custom-call(f32[4096,128]{1,0:T(8,128)} %green.3, bf16[128,80]{1,0:T(8,128)(2,1)} %constant.131.clone.pick, bf16[2,128,128]{2,1,0:T(8,128)(2,1)} %constant.132.clone.turn), custom_call_target="tpu_custom_call" | custom-call | tf_op jit(solution)/shard_map/pallas_call | solution.py:668
  16.7 5.3 %collective-permute-start = (bf16[16,64,128]{2,1,0:T(8,128)(2,1)}, bf16[16,64,128]{2,1,0:T(8,128)(2,1)S(1)}, u32[]{:S(2)}, u32[]{:S(2)}) collective-permute-start(bf16[16,64,128]{2,1,0:T(8,128)(2,1)} %get-tuple-element.52), channel_id=1, source_target_pairs={{0,31},{1,30},{2,29},{3,28},{4,27},{5,26},{6,25},{7,24},{8,23},{9,... | collective-permute-start | bytes 786440 | tf_op jit(solution)/shard_map/ppermute | solution.py:730
  22.0 7.9 %copy.19 = bf16[128,4,4096]{0,2,1:T(8,128)(2,1)} copy(bf16[128,4,4096]{2,1,0:T(4,128)(2,1)} %param.24) | data formatting | bytes 8388608 | tf_op args[3]
  31.7 5.4 %shard_map.178 = bf16[32,128,128]{2,1,0:T(8,128)(2,1)} custom-call(f32[256,384]{1,0:T(8,128)} %bitcast.29, f32[256,384]{1,0:T(8,128)} %bitcast.30, bf16[2,256,256]{2,1,0:T(8,128)(2,1)} %constant.124.clone.table_in.table, f32[2,128,128]{2,1,0:T(8,128)} %constant.126.clone.twiddle_in.twiddle, f32[32,32]{1,0:T(8,128)} %constant.127.clone.edge_in.edge), custom_call_target="tpu_custom_call" | custom-call | tf_op jit(solution)/shard_map/pallas_call | solution.py:685
  44.0 5.3 %collective-permute-start.1 = (bf16[8,64]{1,0:T(8,128)(2,1)S(1)}, bf16[8,64]{1,0:T(8,128)(2,1)S(1)}, u32[]{:S(2)}, u32[]{:S(2)}) collective-permute-start(bf16[8,64]{1,0:T(8,128)(2,1)S(1)} %slice.77), channel_id=1, source_target_pairs={{0,1},{1,2},{2,3},{3,4},{4,5},{5,6},{6,7},{7,8},{8,9},{9,10},{10,1... | collective-permute-start | bytes 3080 | tf_op jit(solution)/shard_map/ppermute | solution.py:30
  49.7 3.9 %shard_map.179.own_in = f32[32,64,128]{2,1,0:T(8,128)} custom-call(s32[1]{0:T(128)} %bitcast.2.follows, f32[4096,128]{1,0:T(8,128)} %green.3), custom_call_target="tpu_custom_call" | custom-call | tf_op jit(solution)/shard_map/pallas_call | solution.py:668
  58.0 14.7 %collective-permute-done.4 = f32[32,128]{1,0:T(8,128)S(1)} collective-permute-done((f32[32,128]{1,0:T(8,128)S(1)}, f32[32,128]{1,0:T(8,128)S(1)}, u32[]{:S(2)}, u32[]{:S(2)}) %collective-permute-start.4) | collective-permute-done | bytes 16416 | tf_op jit(solution)/shard_map/ppermute | solution.py:744
  74.8 7.4 %shard_map.180 = (bf16[32,128,128]{2,1,0:T(8,128)(2,1)}, f32[32,72,128]{2,1,0:T(8,128)}) custom-call(s32[1]{0:T(128)} %bitcast.1.origin, s32[1]{0:T(128)} %bitcast.2.follows, bf16[32,128,128]{2,1,0:T(8,128)(2,1)} %copy-done.10, f32[32,64,128]{2,1,0:T(8,128)} %shard_map.179.own_in, bf16[16,64,128]{2,1,0:T(8,128)(2,1)} %copy-done.13, ...), custom_call_target="tpu_custom_call" | custom-call | tf_op jit(solution)/shard_map/pallas_call | solution.py:685
  82.2 6.6 %all-to-all-start.2 = ((bf16[32,128,128]{2,1,0:T(8,128)(2,1)}), bf16[32,128,128]{2,1,0:T(8,128)(2,1)S(1)}, u32[]{:S(2)}, u32[]{:S(2)}) async-start(bf16[32,128,128]{2,1,0:T(8,128)(2,1)} %get-tuple-element.61), calls=%async_computation.2 | async-start | bytes 2097152 | tf_op jit(solution)/shard_map/all_to_all | solution.py:788
  88.8 15.6 %copy.25 = bf16[128,4,64,64]{2,3,1,0:T(8,128)(2,1)} copy(bf16[128,4,64,64]{0,3,2,1:T(8,128)(2,1)} %bitcast.35) | data formatting | bytes 8388608 | tf_op jit(solution)/shard_map/optimization_barrier | solution.py:866
  104.4 10.4 %all-to-all-done.2.spectrum = bf16[32,128,128]{2,1,0:T(8,128)(2,1)S(1)} async-done(((bf16[32,128,128]{2,1,0:T(8,128)(2,1)}), bf16[32,128,128]{2,1,0:T(8,128)(2,1)S(1)}, u32[]{:S(2)}, u32[]{:S(2)}) %all-to-all-start.2) | async-done | bytes 1048608 | tf_op jit(solution)/shard_map/all_to_all | solution.py:788
  121.2 4.6 %fusion = f32[128,1,64,1]{2,1,3,0:T(1,128)S(1)} fusion(bf16[128,4,64,64]{2,3,1,0:T(8,128)(2,1)} %copy.25, bf16[128,4,64,1]{2,1,0,3:T(4,128)(2,1)S(1)} %bitcast.41), kind=kOutput, calls=%fused_computation.2 | convolution fusion | flops 4194304 | bytes 4292608 | tf_op jit(solution)/shard_map/bkps,bks->bp/dot_general | solution.py:885
  130.1 5.6 %shard_map.182 = (f32[64,128]{1,0:T(8,128)}, bf16[64,128]{1,0:T(8,128)(2,1)}, f32[256,256]{1,0:T(8,128)}) custom-call(s32[1,128]{1,0:T(1,128)} %bitcast.47, bf16[256,256]{1,0:T(8,128)(2,1)} %bitcast.38, f32[64,128]{1,0:T(8,128)} %reshape.191.near_in, f32[64,128]{1,0:T(8,128)} %bitcast.44, bf16[128,64,256]{2,1,0:T(8,128)(2,1)} %stencil_in.5), custom_call_target="tpu_custom_call" | custom-call | tf_op jit(solution)/shard_map/pallas_call | solution.py:685
  135.8 13.6 %all_to_all.40 = f32[32,8,256]{2,1,0:T(8,128)S(1)} all-to-all(f32[32,8,256]{2,1,0:T(8,128)} %bitcast.40), channel_id=1, replica_groups=mesh['panel'=8,'slab'=4] {'panel','slab'}, dimensions={0} | all-to-all | bytes 524288 | tf_op jit(solution)/shard_map/all_to_all | solution.py:788
  149.3 4.0 %shard_map.183 = bf16[32,128,128]{2,1,0:T(8,128)(2,1)} custom-call(f32[256,256]{1,0:T(8,128)S(1)} %bitcast.34, f32[256,384]{1,0:T(8,128)S(1)} %bitcast.32, bf16[2,256,256]{2,1,0:T(8,128)(2,1)S(1)} %copy-done.5, f32[2,128,128]{2,1,0:T(8,128)S(1)} %copy-done.2, f32[32,32]{1,0:T(8,128)S(1)} %copy-done.9), custom_call_target="tpu_custom_call" | custom-call | tf_op jit(solution)/shard_map/pallas_call | solution.py:685
  157.0 10.7 %fusion.9 = f32[128,1,4,64]{3,1,2,0:T(1,128)} fusion(bf16[128,4,64,64]{2,3,1,0:T(8,128)(2,1)} %copy.25, bf16[128,64,1,1]{1,2,3,0:T(2,128)(2,1)S(1)} %reshape.230), kind=kOutput, calls=%fused_computation.20 | convolution fusion | flops 4194304 | bytes 4341760 | tf_op jit(solution)/shard_map/bkps,bp->bks/dot_general | solution.py:905
  167.7 14.5 %all-to-all-done.5.spectrum = bf16[32,128,128]{2,1,0:T(8,128)(2,1)S(1)} async-done(((bf16[32,128,128]{2,1,0:T(8,128)(2,1)}), bf16[32,128,128]{2,1,0:T(8,128)(2,1)S(1)}, u32[]{:S(2)}, u32[]{:S(2)}) %all-to-all-start.5) | async-done | bytes 1048608 | tf_op jit(solution)/shard_map/all_to_all | solution.py:788
  182.2 6.0 %shard_map.184 = bf16[32,128,128]{2,1,0:T(8,128)(2,1)} custom-call(s32[1]{0:T(128)} %bitcast.1.origin, bf16[32,128,128]{2,1,0:T(8,128)(2,1)S(1)} %all-to-all-done.5.spectrum, f32[32,72,128]{2,1,0:T(8,128)S(1)} %copy-done.3, bf16[256,256]{1,0:T(8,128)(2,1)S(1)} %copy-done.6, f32[2,32,128]{2,1,0:T(8,128)S(1)} %copy-done.7), custom_call_target="tpu_custom_call" | custom-call | tf_op jit(solution)/shard_map/pallas_call | solution.py:685
  198.2 19.9 %all-to-all-done.6.spectrum = bf16[32,128,128]{2,1,0:T(8,128)(2,1)S(1)} async-done(((bf16[32,128,128]{2,1,0:T(8,128)(2,1)}), bf16[32,128,128]{2,1,0:T(8,128)(2,1)S(1)}, u32[]{:S(2)}, u32[]{:S(2)}) %all-to-all-start.6) | async-done | bytes 1048608 | tf_op jit(solution)/shard_map/all_to_all | solution.py:788
  220.8 3.7 %all-to-all-start.7 = ((bf16[32,8,256]{2,1,0:T(8,128)(2,1)}), bf16[32,8,256]{2,1,0:T(8,128)(2,1)S(1)}, u32[]{:S(2)}, u32[]{:S(2)}) async-start(bf16[32,8,256]{2,1,0:T(8,128)(2,1)} %bitcast.20), calls=%async_computation.7 | async-start | bytes 262144 | tf_op jit(solution)/shard_map/all_to_all | solution.py:788
  225.2 7.5 %all-to-all-done.7 = bf16[32,8,256]{2,1,0:T(8,128)(2,1)S(1)} async-done(((bf16[32,8,256]{2,1,0:T(8,128)(2,1)}), bf16[32,8,256]{2,1,0:T(8,128)(2,1)S(1)}, u32[]{:S(2)}, u32[]{:S(2)}) %all-to-all-start.7) | async-done | bytes 131104 | tf_op jit(solution)/shard_map/all_to_all | solution.py:788
  233.3 3.9 %shard_map.186 = f32[64,128]{1,0:T(8,128)} custom-call(s32[1,128]{1,0:T(1,128)} %bitcast.48, bf16[256,256]{1,0:T(8,128)(2,1)} %bitcast.37, f32[64,128]{1,0:T(8,128)} %reshape.201.near_in, bf16[128,64,256]{2,1,0:T(8,128)(2,1)} %stencil_in.5), custom_call_target="tpu_custom_call" | custom-call | tf_op jit(solution)/shard_map/pallas_call | solution.py:685
  (85 shorter events, 43.7 us)
Async XLA Ops:
  4.8 44.5 %copy-start.18 = (s32[128,4]{0,1:T(4,128)S(1)}, s32[128,4]{0,1:T(4,128)}, u32[]{:S(2)}) copy-start(s32[128,4]{0,1:T(4,128)} %param.28) | copy-start | bytes 6148
  4.8 26.1 %all-to-all-start = ((f32[32,8,384]{2,1,0:T(8,128)}), f32[32,8,384]{2,1,0:T(8,128)S(1)}, u32[]{:S(2)}, u32[]{:S(2)}) async-start(f32[32,8,384]{2,1,0:T(8,128)} %bitcast.36), calls=%async_computation | async-start | bytes 786432 | tf_op jit(solution)/shard_map/all_to_all | solution.py:788
  16.7 20.3 %collective-permute-start = (bf16[16,64,128]{2,1,0:T(8,128)(2,1)}, bf16[16,64,128]{2,1,0:T(8,128)(2,1)S(1)}, u32[]{:S(2)}, u32[]{:S(2)}) collective-permute-start(bf16[16,64,128]{2,1,0:T(8,128)(2,1)} %get-tuple-element.52), channel_id=1, source_target_pairs={{0,31},{1,30},{2,29},{3,28},{4,27},{5,26},{6,25},{7,24},{8,23},{9,... | collective-permute-start | bytes 786440 | tf_op jit(solution)/shard_map/ppermute | solution.py:730
  37.1 36.6 %all-to-all-start.1 = ((bf16[32,128,128]{2,1,0:T(8,128)(2,1)}), bf16[32,128,128]{2,1,0:T(8,128)(2,1)S(1)}, u32[]{:S(2)}, u32[]{:S(2)}) async-start(bf16[32,128,128]{2,1,0:T(8,128)(2,1)} %shard_map.178), calls=%async_computation.1 | async-start | bytes 2097152 | tf_op jit(solution)/shard_map/all_to_all | solution.py:788
  39.9 32.8 %collective-permute-start.4 = (f32[32,128]{1,0:T(8,128)S(1)}, f32[32,128]{1,0:T(8,128)S(1)}, u32[]{:S(2)}, u32[]{:S(2)}) collective-permute-start(f32[32,128]{1,0:T(8,128)S(1)} %copy-done.16), channel_id=1, source_target_pairs={{16,0},{1,16},{3,18},{5,20},{7,22},{9,24},{11,26},{13,28},{15,30}} | collective-permute-start | bytes 49160 | tf_op jit(solution)/shard_map/ppermute | solution.py:744
  41.2 31.9 %collective-permute-start.5 = (f32[32,128]{1,0:T(8,128)S(1)}, f32[32,128]{1,0:T(8,128)S(1)}, u32[]{:S(2)}, u32[]{:S(2)}) collective-permute-start(f32[32,128]{1,0:T(8,128)S(1)} %copy-done.17), channel_id=1, source_target_pairs={{16,0},{31,16},{29,18},{27,20},{25,22},{23,24},{21,26},{19,28},{17... | collective-permute-start | bytes 49160 | tf_op jit(solution)/shard_map/ppermute | solution.py:744
  42.6 14.1 %collective-permute-start.2 = (bf16[8,64]{1,0:T(8,128)(2,1)S(1)}, bf16[8,64]{1,0:T(8,128)(2,1)S(1)}, u32[]{:S(2)}, u32[]{:S(2)}) collective-permute-start(bf16[8,64]{1,0:T(8,128)(2,1)S(1)} %slice.79), channel_id=1, source_target_pairs={{1,0},{2,1},{3,2},{4,3},{5,4},{6,5},{7,6},{8,7},{9,8},{10,9},{11,1... | collective-permute-start | bytes 3080 | tf_op jit(solution)/shard_map/ppermute | solution.py:32
  44.0 12.7 %collective-permute-start.1 = (bf16[8,64]{1,0:T(8,128)(2,1)S(1)}, bf16[8,64]{1,0:T(8,128)(2,1)S(1)}, u32[]{:S(2)}, u32[]{:S(2)}) collective-permute-start(bf16[8,64]{1,0:T(8,128)(2,1)S(1)} %slice.77), channel_id=1, source_target_pairs={{0,1},{1,2},{2,3},{3,4},{4,5},{5,6},{6,7},{7,8},{8,9},{9,10},{10,1... | collective-permute-start | bytes 3080 | tf_op jit(solution)/shard_map/ppermute | solution.py:30
  53.5 20.2 %collective-permute-start.3 = (bf16[16,64,128]{2,1,0:T(8,128)(2,1)S(1)}, bf16[16,64,128]{2,1,0:T(8,128)(2,1)S(1)}, u32[]{:S(2)}, u32[]{:S(2)}) collective-permute-start(bf16[16,64,128]{2,1,0:T(8,128)(2,1)S(1)} %copy-done.19), channel_id=1, source_target_pairs={{0,31},{1,30},{2,29},{3,28},{4,27},{5,26},{6,25},{7,24},{8,23},{9,... | collective-permute-start | bytes 786440 | tf_op jit(solution)/shard_map/ppermute | solution.py:730
  74.8 40.1 %copy-start.2 = (f32[2,128,128]{2,1,0:T(8,128)S(1)}, f32[2,128,128]{2,1,0:T(8,128)}, u32[]{:S(2)}) copy-start(f32[2,128,128]{2,1,0:T(8,128)} %constant.126.clone.twiddle_in.twiddle) | copy-start | bytes 393220
  74.8 40.1 %copy-start.4 = (bf16[2,256,256]{2,1,0:T(8,128)(2,1)S(1)}, bf16[2,256,256]{2,1,0:T(8,128)(2,1)}, u32[]{:S(2)}) copy-start(bf16[2,256,256]{2,1,0:T(8,128)(2,1)} %constant.125.clone.table) | copy-start | bytes 786436
  74.8 40.1 %copy-start.8 = (f32[32,32]{1,0:T(8,128)S(1)}, f32[32,32]{1,0:T(8,128)}, u32[]{:S(2)}) copy-start(f32[32,32]{1,0:T(8,128)} %constant.128.clone.edge) | copy-start | bytes 12292
  82.2 32.6 %all-to-all-start.2 = ((bf16[32,128,128]{2,1,0:T(8,128)(2,1)}), bf16[32,128,128]{2,1,0:T(8,128)(2,1)S(1)}, u32[]{:S(2)}, u32[]{:S(2)}) async-start(bf16[32,128,128]{2,1,0:T(8,128)(2,1)} %get-tuple-element.61), calls=%async_computation.2 | async-start | bytes 2097152 | tf_op jit(solution)/shard_map/all_to_all | solution.py:788
  104.4 44.9 %copy-start.5 = (bf16[2,256,256]{2,1,0:T(8,128)(2,1)S(1)}, bf16[2,256,256]{2,1,0:T(8,128)(2,1)}, u32[]{:S(2)}) copy-start(bf16[2,256,256]{2,1,0:T(8,128)(2,1)} %constant.124.clone.table_in.table) | copy-start | bytes 786436
  104.4 44.9 %copy-start.9 = (f32[32,32]{1,0:T(8,128)S(1)}, f32[32,32]{1,0:T(8,128)}, u32[]{:S(2)}) copy-start(f32[32,32]{1,0:T(8,128)} %constant.127.clone.edge_in.edge) | copy-start | bytes 12292
  117.6 11.9 %all-to-all-start.3 = ((bf16[32,8,256]{2,1,0:T(8,128)(2,1)}), bf16[32,8,256]{2,1,0:T(8,128)(2,1)S(1)}, u32[]{:S(2)}, u32[]{:S(2)}) async-start(bf16[32,8,256]{2,1,0:T(8,128)(2,1)} %bitcast.9), calls=%async_computation.3 | async-start | bytes 262144 | tf_op jit(solution)/shard_map/all_to_all | solution.py:788
  130.1 52.1 %copy-start.3 = (f32[32,72,128]{2,1,0:T(8,128)S(1)}, f32[32,72,128]{2,1,0:T(8,128)}, u32[]{:S(2)}) copy-start(f32[32,72,128]{2,1,0:T(8,128)} %get-tuple-element.68.green) | copy-start | bytes 3538948
  130.1 52.1 %copy-start.6 = (bf16[256,256]{1,0:T(8,128)(2,1)S(1)}, bf16[256,256]{1,0:T(8,128)(2,1)}, u32[]{:S(2)}) copy-start(bf16[256,256]{1,0:T(8,128)(2,1)} %constant.129.clone.both_in.both) | copy-start | bytes 393220
  130.1 52.1 %copy-start.7 = (f32[2,32,128]{2,1,0:T(8,128)S(1)}, f32[2,32,128]{2,1,0:T(8,128)}, u32[]{:S(2)}) copy-start(f32[2,32,128]{2,1,0:T(8,128)} %constant.130.clone.twiddle_in.twiddle) | copy-start | bytes 98308
  153.3 28.9 %all-to-all-start.5 = ((bf16[32,128,128]{2,1,0:T(8,128)(2,1)}), bf16[32,128,128]{2,1,0:T(8,128)(2,1)S(1)}, u32[]{:S(2)}, u32[]{:S(2)}) async-start(bf16[32,128,128]{2,1,0:T(8,128)(2,1)} %shard_map.183), calls=%async_computation.5 | async-start | bytes 2097152 | tf_op jit(solution)/shard_map/all_to_all | solution.py:788
  188.2 29.8 %all-to-all-start.6 = ((bf16[32,128,128]{2,1,0:T(8,128)(2,1)}), bf16[32,128,128]{2,1,0:T(8,128)(2,1)S(1)}, u32[]{:S(2)}, u32[]{:S(2)}) async-start(bf16[32,128,128]{2,1,0:T(8,128)(2,1)} %shard_map.184), calls=%async_computation.6 | async-start | bytes 2097152 | tf_op jit(solution)/shard_map/all_to_all | solution.py:788
  194.7 29.8 %collective-permute-start.6 = (f32[8,64]{1,0:T(8,128)S(1)}, f32[8,64]{1,0:T(8,128)S(1)}, u32[]{:S(2)}, u32[]{:S(2)}) collective-permute-start(f32[8,64]{1,0:T(8,128)S(1)} %get-tuple-element.73), channel_id=1, source_target_pairs={{0,1},{1,2},{2,3},{3,4},{4,5},{5,6},{6,7},{7,8},{8,9},{9,10},{10,1... | collective-permute-start | bytes 6152 | tf_op jit(solution)/shard_map/ppermute | solution.py:30
  196.8 27.6 %collective-permute-start.7 = (f32[8,64]{1,0:T(8,128)S(1)}, f32[8,64]{1,0:T(8,128)S(1)}, u32[]{:S(2)}, u32[]{:S(2)}) collective-permute-start(f32[8,64]{1,0:T(8,128)S(1)} %get-tuple-element.72), channel_id=1, source_target_pairs={{1,0},{2,1},{3,2},{4,3},{5,4},{6,5},{7,6},{8,7},{9,8},{10,9},{11,1... | collective-permute-start | bytes 6152 | tf_op jit(solution)/shard_map/ppermute | solution.py:32
  220.8 11.9 %all-to-all-start.7 = ((bf16[32,8,256]{2,1,0:T(8,128)(2,1)}), bf16[32,8,256]{2,1,0:T(8,128)(2,1)S(1)}, u32[]{:S(2)}, u32[]{:S(2)}) async-start(bf16[32,8,256]{2,1,0:T(8,128)(2,1)} %bitcast.20), calls=%async_computation.7 | async-start | bytes 262144 | tf_op jit(solution)/shard_map/all_to_all | solution.py:788
  (11 other events, 203.0 us)

commit v4 on v3

--- a/solution.py
+++ b/solution.py
@@ -455,7 +455,7 @@
             work[at, a:b], work[at, b:c] = turn_by((re, im), turn_c, turn_s)
         return carry
 
-    lax.fori_loop(0, devices // batch, middle, 0)
+    lax.fori_loop(0, devices // batch, middle, 0, unroll=4)
 
     for first, second, size in [groups[1], groups[0], *groups[2:]]:
         at_re, at_im = slice(first, first + size), slice(second, second + size)
@@ -859,7 +859,7 @@
     arrived, late, edges, couple = lax.optimization_barrier((arrived, late, edges, couple))
     late = swap_mirrored(plan, late)
     marked = arrived
-    spectrum = to_columns(arrived, marked, WIDE)
+    spectrum = to_columns(arrived, marked, NARROW)
     spectrum, early = lax.optimization_barrier((spectrum, early))
     lines = edge_lines(plan, edges, swapped_edges)
     own = staying_green(plan, green)

time: 239 us -> 234 us (0.979)
  Pallas kernels: 50.4 us -> 45.6 us
    pallas_call x9, Pallas kernels: 41.9 us -> 37.1 us  [streamed(): pl.pallas_call(functools.partial(body, plan), out_shape=out_shape, in_spe...]
    unnamed x41 -> x37, local copies, waits for them, and re-layouts: 11 us -> 10.3 us
where the time goes in v4:
time: 234 us; the launch traced here: 232 us
  waiting for transfers between devices  71.3 us (30%)
  starting transfers between devices  51.8 us (22%)
  Pallas kernels  45.6 us (19%)
  local copies, waits for them, and re-layouts  30.2 us (13%)
  matrix products  15.3 us (7%)
  blocking collectives  13.6 us (6%)
  other arithmetic  3.3 us (1%)
    all_to_all x7, waiting for transfers between devices, exchange(): return lax.all_to_all(values, AXES, split_axis=0, concat_axis=0, tiled=True)  56.2 us
    pallas_call x9, Pallas kernels, streamed(): pl.pallas_call(functools.partial(body, plan), out_shape=out_shape, in_spe...  37.1 us
    all_to_all x7, starting transfers between devices, exchange(): return lax.all_to_all(values, AXES, split_axis=0, concat_axis=0, tiled=True)  30.8 us
    optimization_barrier x1, local copies, waits for them, and re-layouts, local(): lax.optimization_barrier((exchange(spectrum), couple, sources, own))  15.7 us
    ppermute x1, waiting for transfers between devices, swap_edges(): lax.ppermute(edge, AXES, plain)  14.7 us
    all_to_all x1, blocking collectives, exchange(): return lax.all_to_all(values, AXES, split_axis=0, concat_axis=0, tiled=True)  13.6 us
    dot_general x1, matrix products, local(): jnp.einsum('bkps,bp->bks', couple, residual, preferred_element_type=F32)  10.7 us
    unnamed x37, local copies, waits for them, and re-layouts  10.3 us
  transfers between devices with their start and end apart: 15, of which 8 were waited for; matrix products, arithmetic and copies ran while one was open for 20% of the time, Pallas kernels for 7%

profile of v4, /device:TPU:0, one launch (start us, length us, event | category | flops | bytes accessed | tf_op | source)
XLA Modules:
  0.0 232.3 jit_solution(14784906406825587601)
XLA Ops:
  0.7 4.2 %shard_map.176 = f32[256,384]{1,0:T(8,128)} custom-call(s32[1,128]{1,0:T(1,128)} %bitcast.46, s32[1,128]{1,0:T(1,128)} %bitcast.50, bf16[64,128]{1,0:T(8,128)(2,1)} %bitcast.42, bf16[128,64,256]{2,1,0:T(8,128)(2,1)} %stencil_in.5), custom_call_target="tpu_custom_call" | custom-call | tf_op jit(solution)/shard_map/pallas_call | solution.py:685
  4.9 7.3 %all-to-all-start = ((f32[32,8,384]{2,1,0:T(8,128)}), f32[32,8,384]{2,1,0:T(8,128)S(1)}, u32[]{:S(2)}, u32[]{:S(2)}) async-start(f32[32,8,384]{2,1,0:T(8,128)} %bitcast.36), calls=%async_computation | async-start | bytes 786432 | tf_op jit(solution)/shard_map/all_to_all | solution.py:788
  12.2 4.6 %shard_map.177 = (bf16[16,64,128]{2,1,0:T(8,128)(2,1)}, bf16[16,64,128]{2,1,0:T(8,128)(2,1)}, f32[32,128]{1,0:T(8,128)}, f32[32,128]{1,0:T(8,128)}) custom-call(f32[4096,128]{1,0:T(8,128)} %green.3, bf16[128,80]{1,0:T(8,128)(2,1)} %constant.131.clone.pick, bf16[2,128,128]{2,1,0:T(8,128)(2,1)} %constant.132.clone.turn), custom_call_target="tpu_custom_call" | custom-call | tf_op jit(solution)/shard_map/pallas_call | solution.py:668
  16.8 5.3 %collective-permute-start = (bf16[16,64,128]{2,1,0:T(8,128)(2,1)}, bf16[16,64,128]{2,1,0:T(8,128)(2,1)S(1)}, u32[]{:S(2)}, u32[]{:S(2)}) collective-permute-start(bf16[16,64,128]{2,1,0:T(8,128)(2,1)} %get-tuple-element.52), channel_id=1, source_target_pairs={{0,31},{1,30},{2,29},{3,28},{4,27},{5,26},{6,25},{7,24},{8,23},{9,... | collective-permute-start | bytes 786440 | tf_op jit(solution)/shard_map/ppermute | solution.py:730
  22.1 7.8 %copy.19 = bf16[128,4,4096]{0,2,1:T(8,128)(2,1)} copy(bf16[128,4,4096]{2,1,0:T(4,128)(2,1)} %param.24) | data formatting | bytes 8388608 | tf_op args[3]
  31.0 4.0 %shard_map.178 = bf16[32,128,128]{2,1,0:T(8,128)(2,1)} custom-call(f32[256,384]{1,0:T(8,128)S(1)} %bitcast.29, f32[256,384]{1,0:T(8,128)S(1)} %bitcast.30, bf16[2,256,256]{2,1,0:T(8,128)(2,1)S(1)} %copy-done.3, f32[2,128,128]{2,1,0:T(8,128)S(1)} %copy-done, f32[32,32]{1,0:T(8,128)S(1)} %copy-done.7), custom_call_target="tpu_custom_call" | custom-call | tf_op jit(solution)/shard_map/pallas_call | solution.py:685
  42.3 5.3 %collective-permute-start.1 = (bf16[8,64]{1,0:T(8,128)(2,1)S(1)}, bf16[8,64]{1,0:T(8,128)(2,1)S(1)}, u32[]{:S(2)}, u32[]{:S(2)}) collective-permute-start(bf16[8,64]{1,0:T(8,128)(2,1)S(1)} %slice.77), channel_id=1, source_target_pairs={{0,1},{1,2},{2,3},{3,4},{4,5},{5,6},{6,7},{7,8},{8,9},{9,10},{10,1... | collective-permute-start | bytes 3080 | tf_op jit(solution)/shard_map/ppermute | solution.py:30
  48.0 3.9 %shard_map.179.own_in = f32[32,64,128]{2,1,0:T(8,128)} custom-call(s32[1]{0:T(128)} %bitcast.2.follows, f32[4096,128]{1,0:T(8,128)} %green.3), custom_call_target="tpu_custom_call" | custom-call | tf_op jit(solution)/shard_map/pallas_call | solution.py:668
  56.4 14.7 %collective-permute-done.4 = f32[32,128]{1,0:T(8,128)S(1)} collective-permute-done((f32[32,128]{1,0:T(8,128)S(1)}, f32[32,128]{1,0:T(8,128)S(1)}, u32[]{:S(2)}, u32[]{:S(2)}) %collective-permute-start.4) | collective-permute-done | bytes 16416 | tf_op jit(solution)/shard_map/ppermute | solution.py:744
  73.1 5.7 %shard_map.180 = (bf16[32,128,128]{2,1,0:T(8,128)(2,1)}, f32[32,72,128]{2,1,0:T(8,128)}) custom-call(s32[1]{0:T(128)} %bitcast.1.origin, s32[1]{0:T(128)} %bitcast.2.follows, bf16[32,128,128]{2,1,0:T(8,128)(2,1)} %copy-done.8, f32[32,64,128]{2,1,0:T(8,128)} %shard_map.179.own_in, bf16[16,64,128]{2,1,0:T(8,128)(2,1)} %copy-done.11, ...), custom_call_target="tpu_custom_call" | custom-call | tf_op jit(solution)/shard_map/pallas_call | solution.py:685
  78.8 6.6 %all-to-all-start.2 = ((bf16[32,128,128]{2,1,0:T(8,128)(2,1)}), bf16[32,128,128]{2,1,0:T(8,128)(2,1)S(1)}, u32[]{:S(2)}, u32[]{:S(2)}) async-start(bf16[32,128,128]{2,1,0:T(8,128)(2,1)} %get-tuple-element.61), calls=%async_computation.2 | async-start | bytes 2097152 | tf_op jit(solution)/shard_map/all_to_all | solution.py:788
  85.4 15.7 %copy.25 = bf16[128,4,64,64]{2,3,1,0:T(8,128)(2,1)} copy(bf16[128,4,64,64]{0,3,2,1:T(8,128)(2,1)} %bitcast.35) | data formatting | bytes 8388608 | tf_op jit(solution)/shard_map/optimization_barrier | solution.py:866
  101.1 10.4 %all-to-all-done.2.spectrum = bf16[32,128,128]{2,1,0:T(8,128)(2,1)S(1)} async-done(((bf16[32,128,128]{2,1,0:T(8,128)(2,1)}), bf16[32,128,128]{2,1,0:T(8,128)(2,1)S(1)}, u32[]{:S(2)}, u32[]{:S(2)}) %all-to-all-start.2) | async-done | bytes 1048608 | tf_op jit(solution)/shard_map/all_to_all | solution.py:788
  117.8 4.6 %fusion = f32[128,1,64,1]{2,1,3,0:T(1,128)S(1)} fusion(bf16[128,4,64,64]{2,3,1,0:T(8,128)(2,1)} %copy.25, bf16[128,4,64,1]{2,1,0,3:T(4,128)(2,1)S(1)} %bitcast.41), kind=kOutput, calls=%fused_computation.2 | convolution fusion | flops 4194304 | bytes 4292608 | tf_op jit(solution)/shard_map/bkps,bks->bp/dot_general | solution.py:885
  126.7 5.6 %shard_map.182 = (f32[64,128]{1,0:T(8,128)}, bf16[64,128]{1,0:T(8,128)(2,1)}, f32[256,256]{1,0:T(8,128)}) custom-call(s32[1,128]{1,0:T(1,128)} %bitcast.47, bf16[256,256]{1,0:T(8,128)(2,1)} %bitcast.38, f32[64,128]{1,0:T(8,128)} %reshape.191.near_in, f32[64,128]{1,0:T(8,128)} %bitcast.44, bf16[128,64,256]{2,1,0:T(8,128)(2,1)} %stencil_in.5), custom_call_target="tpu_custom_call" | custom-call | tf_op jit(solution)/shard_map/pallas_call | solution.py:685
  132.3 13.6 %all_to_all.40 = f32[32,8,256]{2,1,0:T(8,128)S(1)} all-to-all(f32[32,8,256]{2,1,0:T(8,128)} %bitcast.40), channel_id=1, replica_groups=mesh['panel'=8,'slab'=4] {'panel','slab'}, dimensions={0} | all-to-all | bytes 524288 | tf_op jit(solution)/shard_map/all_to_all | solution.py:788
  145.9 4.0 %shard_map.183 = bf16[32,128,128]{2,1,0:T(8,128)(2,1)} custom-call(f32[256,256]{1,0:T(8,128)S(1)} %bitcast.34, f32[256,384]{1,0:T(8,128)S(1)} %bitcast.32, bf16[2,256,256]{2,1,0:T(8,128)(2,1)S(1)} %copy-done.3, f32[2,128,128]{2,1,0:T(8,128)S(1)} %copy-done, f32[32,32]{1,0:T(8,128)S(1)} %copy-done.7), custom_call_target="tpu_custom_call" | custom-call | tf_op jit(solution)/shard_map/pallas_call | solution.py:685
  153.6 10.7 %fusion.9 = f32[128,1,4,64]{3,1,2,0:T(1,128)} fusion(bf16[128,4,64,64]{2,3,1,0:T(8,128)(2,1)} %copy.25, bf16[128,64,1,1]{1,2,3,0:T(2,128)(2,1)S(1)} %reshape.230), kind=kOutput, calls=%fused_computation.20 | convolution fusion | flops 4194304 | bytes 4341760 | tf_op jit(solution)/shard_map/bkps,bp->bks/dot_general | solution.py:905
  164.3 14.5 %all-to-all-done.5.spectrum = bf16[32,128,128]{2,1,0:T(8,128)(2,1)S(1)} async-done(((bf16[32,128,128]{2,1,0:T(8,128)(2,1)}), bf16[32,128,128]{2,1,0:T(8,128)(2,1)S(1)}, u32[]{:S(2)}, u32[]{:S(2)}) %all-to-all-start.5) | async-done | bytes 1048608 | tf_op jit(solution)/shard_map/all_to_all | solution.py:788
  178.8 4.3 %shard_map.184 = bf16[32,128,128]{2,1,0:T(8,128)(2,1)} custom-call(s32[1]{0:T(128)} %bitcast.1.origin, bf16[32,128,128]{2,1,0:T(8,128)(2,1)S(1)} %all-to-all-done.5.spectrum, f32[32,72,128]{2,1,0:T(8,128)S(1)} %copy-done.1, bf16[256,256]{1,0:T(8,128)(2,1)S(1)} %copy-done.4, f32[2,32,128]{2,1,0:T(8,128)S(1)} %copy-done.5), custom_call_target="tpu_custom_call" | custom-call | tf_op jit(solution)/shard_map/pallas_call | solution.py:685
  193.0 19.9 %all-to-all-done.6.spectrum = bf16[32,128,128]{2,1,0:T(8,128)(2,1)S(1)} async-done(((bf16[32,128,128]{2,1,0:T(8,128)(2,1)}), bf16[32,128,128]{2,1,0:T(8,128)(2,1)S(1)}, u32[]{:S(2)}, u32[]{:S(2)}) %all-to-all-start.6) | async-done | bytes 1048608 | tf_op jit(solution)/shard_map/all_to_all | solution.py:788
  215.6 3.7 %all-to-all-start.7 = ((bf16[32,8,256]{2,1,0:T(8,128)(2,1)}), bf16[32,8,256]{2,1,0:T(8,128)(2,1)S(1)}, u32[]{:S(2)}, u32[]{:S(2)}) async-start(bf16[32,8,256]{2,1,0:T(8,128)(2,1)} %bitcast.20), calls=%async_computation.7 | async-start | bytes 262144 | tf_op jit(solution)/shard_map/all_to_all | solution.py:788
  220.0 7.5 %all-to-all-done.7 = bf16[32,8,256]{2,1,0:T(8,128)(2,1)S(1)} async-done(((bf16[32,8,256]{2,1,0:T(8,128)(2,1)}), bf16[32,8,256]{2,1,0:T(8,128)(2,1)S(1)}, u32[]{:S(2)}, u32[]{:S(2)}) %all-to-all-start.7) | async-done | bytes 131104 | tf_op jit(solution)/shard_map/all_to_all | solution.py:788
  228.2 3.9 %shard_map.186 = f32[64,128]{1,0:T(8,128)} custom-call(s32[1,128]{1,0:T(1,128)} %bitcast.48, bf16[256,256]{1,0:T(8,128)(2,1)} %bitcast.37, f32[64,128]{1,0:T(8,128)} %reshape.201.near_in, bf16[128,64,256]{2,1,0:T(8,128)(2,1)} %stencil_in.5), custom_call_target="tpu_custom_call" | custom-call | tf_op jit(solution)/shard_map/pallas_call | solution.py:685
  (81 shorter events, 43.4 us)
Async XLA Ops:
  4.9 36.0 %copy-start.13 = (bf16[8192]{0:T(1024)(128)(2,1)S(1)}, bf16[8192]{0:T(1024)(128)(2,1)}, u32[]{:S(2)}) copy-start(bf16[8192]{0:T(1024)(128)(2,1)} %param.21) | copy-start | bytes 49156
  4.9 42.8 %copy-start.16 = (s32[128,4]{0,1:T(4,128)S(1)}, s32[128,4]{0,1:T(4,128)}, u32[]{:S(2)}) copy-start(s32[128,4]{0,1:T(4,128)} %param.28) | copy-start | bytes 6148
  4.9 26.1 %all-to-all-start = ((f32[32,8,384]{2,1,0:T(8,128)}), f32[32,8,384]{2,1,0:T(8,128)S(1)}, u32[]{:S(2)}, u32[]{:S(2)}) async-start(f32[32,8,384]{2,1,0:T(8,128)} %bitcast.36), calls=%async_computation | async-start | bytes 786432 | tf_op jit(solution)/shard_map/all_to_all | solution.py:788
  16.8 35.1 %copy-start.17 = (bf16[16,64,128]{2,1,0:T(8,128)(2,1)S(1)}, bf16[16,64,128]{2,1,0:T(8,128)(2,1)}, u32[]{:S(2)}) copy-start(bf16[16,64,128]{2,1,0:T(8,128)(2,1)} %get-tuple-element.58) | copy-start | bytes 786436
  16.8 18.2 %collective-permute-start = (bf16[16,64,128]{2,1,0:T(8,128)(2,1)}, bf16[16,64,128]{2,1,0:T(8,128)(2,1)S(1)}, u32[]{:S(2)}, u32[]{:S(2)}) collective-permute-start(bf16[16,64,128]{2,1,0:T(8,128)(2,1)} %get-tuple-element.52), channel_id=1, source_target_pairs={{0,31},{1,30},{2,29},{3,28},{4,27},{5,26},{6,25},{7,24},{8,23},{9,... | collective-permute-start | bytes 786440 | tf_op jit(solution)/shard_map/ppermute | solution.py:730
  35.0 37.0 %copy-start.11 = (bf16[16,64,128]{2,1,0:T(8,128)(2,1)}, bf16[16,64,128]{2,1,0:T(8,128)(2,1)S(1)}, u32[]{:S(2)}) copy-start(bf16[16,64,128]{2,1,0:T(8,128)(2,1)S(1)} %collective-permute-done.early_in) | copy-start | bytes 786436
  35.1 37.0 %all-to-all-start.1 = ((bf16[32,128,128]{2,1,0:T(8,128)(2,1)}), bf16[32,128,128]{2,1,0:T(8,128)(2,1)S(1)}, u32[]{:S(2)}, u32[]{:S(2)}) async-start(bf16[32,128,128]{2,1,0:T(8,128)(2,1)} %shard_map.178), calls=%async_computation.1 | async-start | bytes 2097152 | tf_op jit(solution)/shard_map/all_to_all | solution.py:788
  38.2 32.8 %collective-permute-start.4 = (f32[32,128]{1,0:T(8,128)S(1)}, f32[32,128]{1,0:T(8,128)S(1)}, u32[]{:S(2)}, u32[]{:S(2)}) collective-permute-start(f32[32,128]{1,0:T(8,128)S(1)} %copy-done.14), channel_id=1, source_target_pairs={{16,0},{1,16},{3,18},{5,20},{7,22},{9,24},{11,26},{13,28},{15,30}} | collective-permute-start | bytes 49160 | tf_op jit(solution)/shard_map/ppermute | solution.py:744
  39.6 31.9 %collective-permute-start.5 = (f32[32,128]{1,0:T(8,128)S(1)}, f32[32,128]{1,0:T(8,128)S(1)}, u32[]{:S(2)}, u32[]{:S(2)}) collective-permute-start(f32[32,128]{1,0:T(8,128)S(1)} %copy-done.15), channel_id=1, source_target_pairs={{16,0},{31,16},{29,18},{27,20},{25,22},{23,24},{21,26},{19,28},{17... | collective-permute-start | bytes 49160 | tf_op jit(solution)/shard_map/ppermute | solution.py:744
  41.0 14.0 %collective-permute-start.2 = (bf16[8,64]{1,0:T(8,128)(2,1)S(1)}, bf16[8,64]{1,0:T(8,128)(2,1)S(1)}, u32[]{:S(2)}, u32[]{:S(2)}) collective-permute-start(bf16[8,64]{1,0:T(8,128)(2,1)S(1)} %slice.79), channel_id=1, source_target_pairs={{1,0},{2,1},{3,2},{4,3},{5,4},{6,5},{7,6},{8,7},{9,8},{10,9},{11,1... | collective-permute-start | bytes 3080 | tf_op jit(solution)/shard_map/ppermute | solution.py:32
  42.3 12.7 %collective-permute-start.1 = (bf16[8,64]{1,0:T(8,128)(2,1)S(1)}, bf16[8,64]{1,0:T(8,128)(2,1)S(1)}, u32[]{:S(2)}, u32[]{:S(2)}) collective-permute-start(bf16[8,64]{1,0:T(8,128)(2,1)S(1)} %slice.77), channel_id=1, source_target_pairs={{0,1},{1,2},{2,3},{3,4},{4,5},{5,6},{6,7},{7,8},{8,9},{9,10},{10,1... | collective-permute-start | bytes 3080 | tf_op jit(solution)/shard_map/ppermute | solution.py:30
  51.9 20.2 %collective-permute-start.3 = (bf16[16,64,128]{2,1,0:T(8,128)(2,1)S(1)}, bf16[16,64,128]{2,1,0:T(8,128)(2,1)S(1)}, u32[]{:S(2)}, u32[]{:S(2)}) collective-permute-start(bf16[16,64,128]{2,1,0:T(8,128)(2,1)S(1)} %copy-done.17), channel_id=1, source_target_pairs={{0,31},{1,30},{2,29},{3,28},{4,27},{5,26},{6,25},{7,24},{8,23},{9,... | collective-permute-start | bytes 786440 | tf_op jit(solution)/shard_map/ppermute | solution.py:730
  73.1 38.3 %copy-start.2 = (bf16[2,256,256]{2,1,0:T(8,128)(2,1)S(1)}, bf16[2,256,256]{2,1,0:T(8,128)(2,1)}, u32[]{:S(2)}) copy-start(bf16[2,256,256]{2,1,0:T(8,128)(2,1)} %constant.125.clone.table) | copy-start | bytes 786436
  73.1 38.3 %copy-start.6 = (f32[32,32]{1,0:T(8,128)S(1)}, f32[32,32]{1,0:T(8,128)}, u32[]{:S(2)}) copy-start(f32[32,32]{1,0:T(8,128)} %constant.128.clone.edge) | copy-start | bytes 12292
  78.8 32.7 %all-to-all-start.2 = ((bf16[32,128,128]{2,1,0:T(8,128)(2,1)}), bf16[32,128,128]{2,1,0:T(8,128)(2,1)S(1)}, u32[]{:S(2)}, u32[]{:S(2)}) async-start(bf16[32,128,128]{2,1,0:T(8,128)(2,1)} %get-tuple-element.61), calls=%async_computation.2 | async-start | bytes 2097152 | tf_op jit(solution)/shard_map/all_to_all | solution.py:788
  114.2 11.9 %all-to-all-start.3 = ((bf16[32,8,256]{2,1,0:T(8,128)(2,1)}), bf16[32,8,256]{2,1,0:T(8,128)(2,1)S(1)}, u32[]{:S(2)}, u32[]{:S(2)}) async-start(bf16[32,8,256]{2,1,0:T(8,128)(2,1)} %bitcast.9), calls=%async_computation.3 | async-start | bytes 262144 | tf_op jit(solution)/shard_map/all_to_all | solution.py:788
  126.7 52.1 %copy-start.1 = (f32[32,72,128]{2,1,0:T(8,128)S(1)}, f32[32,72,128]{2,1,0:T(8,128)}, u32[]{:S(2)}) copy-start(f32[32,72,128]{2,1,0:T(8,128)} %get-tuple-element.68.green) | copy-start | bytes 3538948
  126.7 52.1 %copy-start.4 = (bf16[256,256]{1,0:T(8,128)(2,1)S(1)}, bf16[256,256]{1,0:T(8,128)(2,1)}, u32[]{:S(2)}) copy-start(bf16[256,256]{1,0:T(8,128)(2,1)} %constant.129.clone.both_in.both) | copy-start | bytes 393220
  126.7 52.1 %copy-start.5 = (f32[2,32,128]{2,1,0:T(8,128)S(1)}, f32[2,32,128]{2,1,0:T(8,128)}, u32[]{:S(2)}) copy-start(f32[2,32,128]{2,1,0:T(8,128)} %constant.130.clone.twiddle_in.twiddle) | copy-start | bytes 98308
  149.9 28.9 %all-to-all-start.5 = ((bf16[32,128,128]{2,1,0:T(8,128)(2,1)}), bf16[32,128,128]{2,1,0:T(8,128)(2,1)S(1)}, u32[]{:S(2)}, u32[]{:S(2)}) async-start(bf16[32,128,128]{2,1,0:T(8,128)(2,1)} %shard_map.183), calls=%async_computation.5 | async-start | bytes 2097152 | tf_op jit(solution)/shard_map/all_to_all | solution.py:788
  183.1 29.8 %all-to-all-start.6 = ((bf16[32,128,128]{2,1,0:T(8,128)(2,1)}), bf16[32,128,128]{2,1,0:T(8,128)(2,1)S(1)}, u32[]{:S(2)}, u32[]{:S(2)}) async-start(bf16[32,128,128]{2,1,0:T(8,128)(2,1)} %shard_map.184), calls=%async_computation.6 | async-start | bytes 2097152 | tf_op jit(solution)/shard_map/all_to_all | solution.py:788
  189.5 29.8 %collective-permute-start.6 = (f32[8,64]{1,0:T(8,128)S(1)}, f32[8,64]{1,0:T(8,128)S(1)}, u32[]{:S(2)}, u32[]{:S(2)}) collective-permute-start(f32[8,64]{1,0:T(8,128)S(1)} %get-tuple-element.73), channel_id=1, source_target_pairs={{0,1},{1,2},{2,3},{3,4},{4,5},{5,6},{6,7},{7,8},{8,9},{9,10},{10,1... | collective-permute-start | bytes 6152 | tf_op jit(solution)/shard_map/ppermute | solution.py:30
  191.7 27.6 %collective-permute-start.7 = (f32[8,64]{1,0:T(8,128)S(1)}, f32[8,64]{1,0:T(8,128)S(1)}, u32[]{:S(2)}, u32[]{:S(2)}) collective-permute-start(f32[8,64]{1,0:T(8,128)S(1)} %get-tuple-element.72), channel_id=1, source_target_pairs={{1,0},{2,1},{3,2},{4,3},{5,4},{6,5},{7,6},{8,7},{9,8},{10,9},{11,1... | collective-permute-start | bytes 6152 | tf_op jit(solution)/shard_map/ppermute | solution.py:32
  215.6 11.9 %all-to-all-start.7 = ((bf16[32,8,256]{2,1,0:T(8,128)(2,1)}), bf16[32,8,256]{2,1,0:T(8,128)(2,1)S(1)}, u32[]{:S(2)}, u32[]{:S(2)}) async-start(bf16[32,8,256]{2,1,0:T(8,128)(2,1)} %bitcast.20), calls=%async_computation.7 | async-start | bytes 262144 | tf_op jit(solution)/shard_map/all_to_all | solution.py:788
  (9 other events, 138.6 us)

commit v5 on v4

--- a/solution.py
+++ b/solution.py
@@ -455,7 +455,7 @@
             work[at, a:b], work[at, b:c] = turn_by((re, im), turn_c, turn_s)
         return carry
 
-    lax.fori_loop(0, devices // batch, middle, 0, unroll=4)
+    lax.fori_loop(0, devices // batch, middle, 0, unroll=8)
 
     for first, second, size in [groups[1], groups[0], *groups[2:]]:
         at_re, at_im = slice(first, first + size), slice(second, second + size)
@@ -486,17 +486,22 @@
                 stores.start(result.at[:, here, :], out.at[:, here, :])
 
 
-def first_columns(plan, origin, follows, spectrum_in, own_in, early_in, late_in, head_in, extra_in, both_in, twiddle_in, out, weights_out, spectrum, green, both, twiddle, result, work, rows16, own, early, late, head, extra, ins, outs):
+def first_columns(plan, origin, follows, shares, spectrum_in, own_in, early_in, late_in, edge_in, turned_in, plain_in, mirror_in, both_in, twiddle_in, out, weights_out, spectrum, green, both, twiddle, result, work, rows16, own, early, late, edge, turned, plain, mirror, ins, outs):
     half, rows, ahead = plan.half, plan.rows, early.shape[0]
     loads, stores = Copies(ins), Copies(outs)
     arriving = start_columns(plan, loads, spectrum_in, spectrum, both_in, both, twiddle_in, twiddle)
-    parts = ((own_in, own), (early_in, early), (late_in, late), (head_in, head), (extra_in, extra))
+    parts = [(own_in, own), (early_in, early), (late_in, late)]
+    parts += [(edge_in, edge), (turned_in, turned), (plain_in, plain), (mirror_in, mirror)]
     parts = [loads.start(source, target) for source, target in parts]
 
     def need_green():
         for copy in parts:
             copy.wait()
         scale = 0.5 / (plan.grid * plan.grid)
+        extra = plain[...] + mirror[...]
+        shared, at_origin = shares[0] == 1, origin[0] == 1
+        head = jnp.where(shared, plain[...], edge[...])
+        head = head + jnp.where(at_origin, turned[...], mirror[...])
         replaced = lax.broadcasted_iota(jnp.int32, (half, rows), 0) == 0
         replaced = replaced & (follows[0] == 0)
         top = lax.broadcasted_iota(jnp.int32, (8, rows), 0) == 0
@@ -744,16 +749,6 @@
     return lax.ppermute(edge, AXES, plain), lax.ppermute(edge_turned, AXES, mirror)
 
 
-def edge_lines(plan, edges, swapped_edges):
-    edge, edge_turned = edges
-    edge_plain, edge_mirror = swapped_edges
-    me = lax.axis_index(AXES)
-    mu, part = me // plan.per_mu, me % plan.per_mu
-    shared = (part == 0) & (mu >= plan.tile // 2)
-    head = jnp.where(shared, edge_plain, edge) + jnp.where(me == 0, edge_turned, edge_mirror)
-    return head, edge_plain + edge_mirror
-
-
 def local(charges, target, stencil, near_matrix, green, block_dest, block_tile, near_offset):
     devices = lax.axis_size(AXES)
     blocks, block_size, cell_count = stencil.shape
@@ -771,6 +766,8 @@
     edge_forward, edge_inverse = (jnp.asarray(t) for t in plan.edge_tables())
     both, row_twiddle = (jnp.asarray(t) for t in plan.row_tables())
     origin = (me == 0).astype(jnp.int32).reshape(1)
+    shares = (me % plan.per_mu == 0) & (me // plan.per_mu >= plan.tile // 2)
+    shares = shares.astype(jnp.int32).reshape(1)
     partner = (me % plan.per_mu >= plan.per_mu // 2).astype(jnp.int32).reshape(1)
     early, late, *edges = leaving_green(plan, green)
     spectrum_shape = jax.ShapeDtypeStruct((devices, plan.width, plan.rows), BF16)
@@ -861,12 +858,11 @@
     marked = arrived
     spectrum = to_columns(arrived, marked, NARROW)
     spectrum, early = lax.optimization_barrier((spectrum, early))
-    lines = edge_lines(plan, edges, swapped_edges)
     own = staying_green(plan, green)
     spectrum, couple, sources, own = lax.optimization_barrier(
         (exchange(spectrum), couple, sources, own)
     )
-    green_parts = [own, early, late, *lines]
+    green_parts = [own, early, late, *edges, *swapped_edges]
     spectrum, weights = streamed(
         first_columns,
         plan,
@@ -878,7 +874,7 @@
             *held(*green_parts),
         ],
         (2 * half_steps + 2 + len(green_parts), 2 * half_steps + 1),
-        [origin, partner],
+        [origin, partner, shares],
         [spectrum, *green_parts, both, row_twiddle],
     )
     returned = to_rows(exchange(spectrum), marked)

time: 234 us -> 233 us (level)
    ppermute x1, waiting for transfers between devices: 14.7 us -> 0.35 us  [swap_edges(): lax.ppermute(edge, AXES, plain)]
    all_to_all x7, waiting for transfers between devices: 56.2 us -> 70.4 us  [exchange(): return lax.all_to_all(values, AXES, split_axis=0, concat_axis=0, tiled=True)]
    unnamed x37 -> x41, local copies, waits for them, and re-layouts: 10.3 us -> 9.97 us
  transfers between devices with their start and end apart: 15 -> 15, of which waited for: 8 -> 9; matrix products, arithmetic and copies ran while one was open for 20% -> 20% of each run, Pallas kernels for 7% -> 7%
where the time goes in v5:
time: 233 us; the launch traced here: 232 us
  waiting for transfers between devices  71.2 us (31%)
  starting transfers between devices  52.9 us (23%)
  Pallas kernels  45.2 us (19%)
  local copies, waits for them, and re-layouts  29.9 us (13%)
  matrix products  15.3 us (7%)
  blocking collectives  13.6 us (6%)
  other arithmetic  2.68 us (1%)
    all_to_all x7, waiting for transfers between devices, exchange(): return lax.all_to_all(values, AXES, split_axis=0, concat_axis=0, tiled=True)  70.4 us
    pallas_call x9, Pallas kernels, streamed(): pl.pallas_call(functools.partial(body, plan), out_shape=out_shape, in_spe...  36.8 us
    all_to_all x7, starting transfers between devices, exchange(): return lax.all_to_all(values, AXES, split_axis=0, concat_axis=0, tiled=True)  31.3 us
    optimization_barrier x1, local copies, waits for them, and re-layouts, local(): lax.optimization_barrier((exchange(spectrum), couple, sources, own))  15.7 us
    all_to_all x1, blocking collectives, exchange(): return lax.all_to_all(values, AXES, split_axis=0, concat_axis=0, tiled=True)  13.6 us
    dot_general x1, matrix products, local(): jnp.einsum('bkps,bp->bks', couple, residual, preferred_element_type=F32)  10.7 us
    unnamed x41, local copies, waits for them, and re-layouts  9.97 us
    ppermute x2, starting transfers between devices, swap_mirrored(): lax.ppermute(part, AXES, [(i, plan.devices - 1 - i) for i in range(plan.d...  8.47 us
  transfers between devices with their start and end apart: 15, of which 9 were waited for; matrix products, arithmetic and copies ran while one was open for 20% of the time, Pallas kernels for 7%

profile of v5, /device:TPU:0, one launch (start us, length us, event | category | flops | bytes accessed | tf_op | source)
XLA Modules:
  0.0 231.9 jit_solution(9343197579263886446)
XLA Ops:
  0.7 4.2 %shard_map.176 = f32[256,384]{1,0:T(8,128)} custom-call(s32[1,128]{1,0:T(1,128)} %bitcast.47, s32[1,128]{1,0:T(1,128)} %bitcast.51, bf16[64,128]{1,0:T(8,128)(2,1)} %bitcast.43, bf16[128,64,256]{2,1,0:T(8,128)(2,1)} %stencil_in.5), custom_call_target="tpu_custom_call" | custom-call | tf_op jit(solution)/shard_map/pallas_call | solution.py:690
  4.9 7.3 %all-to-all-start = ((f32[32,8,384]{2,1,0:T(8,128)}), f32[32,8,384]{2,1,0:T(8,128)S(1)}, u32[]{:S(2)}, u32[]{:S(2)}) async-start(f32[32,8,384]{2,1,0:T(8,128)} %bitcast.37), calls=%async_computation | async-start | bytes 786432 | tf_op jit(solution)/shard_map/all_to_all | solution.py:785
  12.2 4.6 %shard_map.177 = (bf16[16,64,128]{2,1,0:T(8,128)(2,1)}, bf16[16,64,128]{2,1,0:T(8,128)(2,1)}, f32[32,128]{1,0:T(8,128)}, f32[32,128]{1,0:T(8,128)}) custom-call(f32[4096,128]{1,0:T(8,128)} %green.3, bf16[128,80]{1,0:T(8,128)(2,1)} %constant.131.clone.pick, bf16[2,128,128]{2,1,0:T(8,128)(2,1)} %constant.132.clone.turn), custom_call_target="tpu_custom_call" | custom-call | tf_op jit(solution)/shard_map/pallas_call | solution.py:673
  16.8 5.3 %collective-permute-start = (bf16[16,64,128]{2,1,0:T(8,128)(2,1)}, bf16[16,64,128]{2,1,0:T(8,128)(2,1)S(1)}, u32[]{:S(2)}, u32[]{:S(2)}) collective-permute-start(bf16[16,64,128]{2,1,0:T(8,128)(2,1)} %get-tuple-element.52), channel_id=1, source_target_pairs={{0,31},{1,30},{2,29},{3,28},{4,27},{5,26},{6,25},{7,24},{8,23},{9,... | collective-permute-start | bytes 786440 | tf_op jit(solution)/shard_map/ppermute | solution.py:735
  22.1 7.9 %copy.19 = bf16[128,4,4096]{0,2,1:T(8,128)(2,1)} copy(bf16[128,4,4096]{2,1,0:T(4,128)(2,1)} %param.24) | data formatting | bytes 8388608 | tf_op args[3]
  31.0 4.0 %shard_map.178 = bf16[32,128,128]{2,1,0:T(8,128)(2,1)} custom-call(f32[256,384]{1,0:T(8,128)S(1)} %bitcast.30, f32[256,384]{1,0:T(8,128)S(1)} %bitcast.31, bf16[2,256,256]{2,1,0:T(8,128)(2,1)S(1)} %copy-done.3, f32[2,128,128]{2,1,0:T(8,128)S(1)} %copy-done, f32[32,32]{1,0:T(8,128)S(1)} %copy-done.7), custom_call_target="tpu_custom_call" | custom-call | tf_op jit(solution)/shard_map/pallas_call | solution.py:690
  42.3 5.5 %collective-permute-start.1 = (bf16[8,64]{1,0:T(8,128)(2,1)S(1)}, bf16[8,64]{1,0:T(8,128)(2,1)S(1)}, u32[]{:S(2)}, u32[]{:S(2)}) collective-permute-start(bf16[8,64]{1,0:T(8,128)(2,1)S(1)} %slice.77), channel_id=1, source_target_pairs={{0,1},{1,2},{2,3},{3,4},{4,5},{5,6},{6,7},{7,8},{8,9},{9,10},{10,1... | collective-permute-start | bytes 3080 | tf_op jit(solution)/shard_map/ppermute | solution.py:30
  51.4 3.9 %shard_map.179.own_in = f32[32,64,128]{2,1,0:T(8,128)} custom-call(s32[1]{0:T(128)} %bitcast.2.follows, f32[4096,128]{1,0:T(8,128)} %green.3), custom_call_target="tpu_custom_call" | custom-call | tf_op jit(solution)/shard_map/pallas_call | solution.py:673
  56.6 14.1 %all-to-all-done.1.spectrum_in = bf16[32,128,128]{2,1,0:T(8,128)(2,1)S(1)} async-done(((bf16[32,128,128]{2,1,0:T(8,128)(2,1)}), bf16[32,128,128]{2,1,0:T(8,128)(2,1)S(1)}, u32[]{:S(2)}, u32[]{:S(2)}) %all-to-all-start.1) | async-done | bytes 1048608 | tf_op jit(solution)/shard_map/all_to_all | solution.py:785
  72.2 5.6 %shard_map.180 = (bf16[32,128,128]{2,1,0:T(8,128)(2,1)}, f32[32,72,128]{2,1,0:T(8,128)}) custom-call(s32[1]{0:T(128)} %bitcast.1.origin, s32[1]{0:T(128)} %bitcast.2.follows, s32[1]{0:T(128)} %bitcast.3.shares, bf16[32,128,128]{2,1,0:T(8,128)(2,1)} %copy-done.8, f32[32,64,128]{2,1,0:T(8,128)} %shard_map.179.own_in, bf16[16,64,128]{2,1,0:T(8,128)(2,1)} %copy-done.11, ...), custom_call_target="tpu_custom_call" | custom-call | tf_op jit(solution)/shard_map/pallas_call | solution.py:690
  77.7 7.4 %all-to-all-start.2 = ((bf16[32,128,128]{2,1,0:T(8,128)(2,1)}), bf16[32,128,128]{2,1,0:T(8,128)(2,1)S(1)}, u32[]{:S(2)}, u32[]{:S(2)}) async-start(bf16[32,128,128]{2,1,0:T(8,128)(2,1)} %get-tuple-element.61), calls=%async_computation.2 | async-start | bytes 2097152 | tf_op jit(solution)/shard_map/all_to_all | solution.py:785
  85.1 15.7 %copy.25 = bf16[128,4,64,64]{2,3,1,0:T(8,128)(2,1)} copy(bf16[128,4,64,64]{0,3,2,1:T(8,128)(2,1)} %bitcast.36) | data formatting | bytes 8388608 | tf_op jit(solution)/shard_map/optimization_barrier | solution.py:862
  100.8 10.5 %all-to-all-done.2.spectrum = bf16[32,128,128]{2,1,0:T(8,128)(2,1)S(1)} async-done(((bf16[32,128,128]{2,1,0:T(8,128)(2,1)}), bf16[32,128,128]{2,1,0:T(8,128)(2,1)S(1)}, u32[]{:S(2)}, u32[]{:S(2)}) %all-to-all-start.2) | async-done | bytes 1048608 | tf_op jit(solution)/shard_map/all_to_all | solution.py:785
  117.7 4.6 %fusion = f32[128,1,64,1]{2,1,3,0:T(1,128)S(1)} fusion(bf16[128,4,64,64]{2,3,1,0:T(8,128)(2,1)} %copy.25, bf16[128,4,64,1]{2,1,0,3:T(4,128)(2,1)S(1)} %bitcast.42), kind=kOutput, calls=%fused_computation.2 | convolution fusion | flops 4194304 | bytes 4292608 | tf_op jit(solution)/shard_map/bkps,bks->bp/dot_general | solution.py:881
  126.6 5.6 %shard_map.182 = (f32[64,128]{1,0:T(8,128)}, bf16[64,128]{1,0:T(8,128)(2,1)}, f32[256,256]{1,0:T(8,128)}) custom-call(s32[1,128]{1,0:T(1,128)} %bitcast.48, bf16[256,256]{1,0:T(8,128)(2,1)} %bitcast.39, f32[64,128]{1,0:T(8,128)} %reshape.198.near_in, f32[64,128]{1,0:T(8,128)} %bitcast.45, bf16[128,64,256]{2,1,0:T(8,128)(2,1)} %stencil_in.5), custom_call_target="tpu_custom_call" | custom-call | tf_op jit(solution)/shard_map/pallas_call | solution.py:690
  132.2 13.6 %all_to_all.40 = f32[32,8,256]{2,1,0:T(8,128)S(1)} all-to-all(f32[32,8,256]{2,1,0:T(8,128)} %bitcast.41), channel_id=1, replica_groups=mesh['panel'=8,'slab'=4] {'panel','slab'}, dimensions={0} | all-to-all | bytes 524288 | tf_op jit(solution)/shard_map/all_to_all | solution.py:785
  145.8 4.0 %shard_map.183 = bf16[32,128,128]{2,1,0:T(8,128)(2,1)} custom-call(f32[256,256]{1,0:T(8,128)S(1)} %bitcast.35, f32[256,384]{1,0:T(8,128)S(1)} %bitcast.33, bf16[2,256,256]{2,1,0:T(8,128)(2,1)S(1)} %copy-done.3, f32[2,128,128]{2,1,0:T(8,128)S(1)} %copy-done, f32[32,32]{1,0:T(8,128)S(1)} %copy-done.7), custom_call_target="tpu_custom_call" | custom-call | tf_op jit(solution)/shard_map/pallas_call | solution.py:690
  153.2 10.7 %fusion.8 = f32[128,1,4,64]{3,1,2,0:T(1,128)} fusion(bf16[128,4,64,64]{2,3,1,0:T(8,128)(2,1)} %copy.25, bf16[128,64,1,1]{1,2,3,0:T(2,128)(2,1)S(1)} %reshape.239), kind=kOutput, calls=%fused_computation.18 | convolution fusion | flops 4194304 | bytes 4341760 | tf_op jit(solution)/shard_map/bkps,bp->bks/dot_general | solution.py:901
  163.9 14.7 %all-to-all-done.5.spectrum = bf16[32,128,128]{2,1,0:T(8,128)(2,1)S(1)} async-done(((bf16[32,128,128]{2,1,0:T(8,128)(2,1)}), bf16[32,128,128]{2,1,0:T(8,128)(2,1)S(1)}, u32[]{:S(2)}, u32[]{:S(2)}) %all-to-all-start.5) | async-done | bytes 1048608 | tf_op jit(solution)/shard_map/all_to_all | solution.py:785
  178.7 4.1 %shard_map.184 = bf16[32,128,128]{2,1,0:T(8,128)(2,1)} custom-call(s32[1]{0:T(128)} %bitcast.1.origin, bf16[32,128,128]{2,1,0:T(8,128)(2,1)S(1)} %all-to-all-done.5.spectrum, f32[32,72,128]{2,1,0:T(8,128)S(1)} %copy-done.1, bf16[256,256]{1,0:T(8,128)(2,1)S(1)} %copy-done.4, f32[2,32,128]{2,1,0:T(8,128)S(1)} %copy-done.5), custom_call_target="tpu_custom_call" | custom-call | tf_op jit(solution)/shard_map/pallas_call | solution.py:690
  192.9 19.6 %all-to-all-done.6.spectrum = bf16[32,128,128]{2,1,0:T(8,128)(2,1)S(1)} async-done(((bf16[32,128,128]{2,1,0:T(8,128)(2,1)}), bf16[32,128,128]{2,1,0:T(8,128)(2,1)S(1)}, u32[]{:S(2)}, u32[]{:S(2)}) %all-to-all-start.6) | async-done | bytes 1048608 | tf_op jit(solution)/shard_map/all_to_all | solution.py:785
  215.3 3.7 %all-to-all-start.7 = ((bf16[32,8,256]{2,1,0:T(8,128)(2,1)}), bf16[32,8,256]{2,1,0:T(8,128)(2,1)S(1)}, u32[]{:S(2)}, u32[]{:S(2)}) async-start(bf16[32,8,256]{2,1,0:T(8,128)(2,1)} %bitcast.21), calls=%async_computation.7 | async-start | bytes 262144 | tf_op jit(solution)/shard_map/all_to_all | solution.py:785
  219.7 7.5 %all-to-all-done.7 = bf16[32,8,256]{2,1,0:T(8,128)(2,1)S(1)} async-done(((bf16[32,8,256]{2,1,0:T(8,128)(2,1)}), bf16[32,8,256]{2,1,0:T(8,128)(2,1)S(1)}, u32[]{:S(2)}, u32[]{:S(2)}) %all-to-all-start.7) | async-done | bytes 131104 | tf_op jit(solution)/shard_map/all_to_all | solution.py:785
  227.8 3.9 %shard_map.186 = f32[64,128]{1,0:T(8,128)} custom-call(s32[1,128]{1,0:T(1,128)} %bitcast.49, bf16[256,256]{1,0:T(8,128)(2,1)} %bitcast.38, f32[64,128]{1,0:T(8,128)} %reshape.208.near_in, bf16[128,64,256]{2,1,0:T(8,128)(2,1)} %stencil_in.5), custom_call_target="tpu_custom_call" | custom-call | tf_op jit(solution)/shard_map/pallas_call | solution.py:690
  (84 shorter events, 42.8 us)
Async XLA Ops:
  4.9 36.0 %copy-start.13 = (bf16[8192]{0:T(1024)(128)(2,1)S(1)}, bf16[8192]{0:T(1024)(128)(2,1)}, u32[]{:S(2)}) copy-start(bf16[8192]{0:T(1024)(128)(2,1)} %param.21) | copy-start | bytes 49156
  4.9 46.1 %copy-start.18 = (s32[128,4]{0,1:T(4,128)S(1)}, s32[128,4]{0,1:T(4,128)}, u32[]{:S(2)}) copy-start(s32[128,4]{0,1:T(4,128)} %param.28) | copy-start | bytes 6148
  4.9 26.1 %all-to-all-start = ((f32[32,8,384]{2,1,0:T(8,128)}), f32[32,8,384]{2,1,0:T(8,128)S(1)}, u32[]{:S(2)}, u32[]{:S(2)}) async-start(f32[32,8,384]{2,1,0:T(8,128)} %bitcast.37), calls=%async_computation | async-start | bytes 786432 | tf_op jit(solution)/shard_map/all_to_all | solution.py:785
  16.8 31.0 %copy-start.19 = (bf16[16,64,128]{2,1,0:T(8,128)(2,1)S(1)}, bf16[16,64,128]{2,1,0:T(8,128)(2,1)}, u32[]{:S(2)}) copy-start(bf16[16,64,128]{2,1,0:T(8,128)(2,1)} %get-tuple-element.58) | copy-start | bytes 786436
  16.8 18.2 %collective-permute-start = (bf16[16,64,128]{2,1,0:T(8,128)(2,1)}, bf16[16,64,128]{2,1,0:T(8,128)(2,1)S(1)}, u32[]{:S(2)}, u32[]{:S(2)}) collective-permute-start(bf16[16,64,128]{2,1,0:T(8,128)(2,1)} %get-tuple-element.52), channel_id=1, source_target_pairs={{0,31},{1,30},{2,29},{3,28},{4,27},{5,26},{6,25},{7,24},{8,23},{9,... | collective-permute-start | bytes 786440 | tf_op jit(solution)/shard_map/ppermute | solution.py:735
  35.0 36.4 %copy-start.11 = (bf16[16,64,128]{2,1,0:T(8,128)(2,1)}, bf16[16,64,128]{2,1,0:T(8,128)(2,1)S(1)}, u32[]{:S(2)}) copy-start(bf16[16,64,128]{2,1,0:T(8,128)(2,1)S(1)} %collective-permute-done.early_in) | copy-start | bytes 786436
  35.0 35.7 %all-to-all-start.1 = ((bf16[32,128,128]{2,1,0:T(8,128)(2,1)}), bf16[32,128,128]{2,1,0:T(8,128)(2,1)S(1)}, u32[]{:S(2)}, u32[]{:S(2)}) async-start(bf16[32,128,128]{2,1,0:T(8,128)(2,1)} %shard_map.178), calls=%async_computation.1 | async-start | bytes 2097152 | tf_op jit(solution)/shard_map/all_to_all | solution.py:785
  38.2 32.8 %collective-permute-start.4 = (f32[32,128]{1,0:T(8,128)S(1)}, f32[32,128]{1,0:T(8,128)S(1)}, u32[]{:S(2)}, u32[]{:S(2)}) collective-permute-start(f32[32,128]{1,0:T(8,128)S(1)} %copy-done.14), channel_id=1, source_target_pairs={{16,0},{1,16},{3,18},{5,20},{7,22},{9,24},{11,26},{13,28},{15,30}} | collective-permute-start | bytes 49160 | tf_op jit(solution)/shard_map/ppermute | solution.py:749
  39.6 31.9 %collective-permute-start.5 = (f32[32,128]{1,0:T(8,128)S(1)}, f32[32,128]{1,0:T(8,128)S(1)}, u32[]{:S(2)}, u32[]{:S(2)}) collective-permute-start(f32[32,128]{1,0:T(8,128)S(1)} %copy-done.15), channel_id=1, source_target_pairs={{16,0},{31,16},{29,18},{27,20},{25,22},{23,24},{21,26},{19,28},{17... | collective-permute-start | bytes 49160 | tf_op jit(solution)/shard_map/ppermute | solution.py:749
  41.0 14.3 %collective-permute-start.2 = (bf16[8,64]{1,0:T(8,128)(2,1)S(1)}, bf16[8,64]{1,0:T(8,128)(2,1)S(1)}, u32[]{:S(2)}, u32[]{:S(2)}) collective-permute-start(bf16[8,64]{1,0:T(8,128)(2,1)S(1)} %slice.79), channel_id=1, source_target_pairs={{1,0},{2,1},{3,2},{4,3},{5,4},{6,5},{7,6},{8,7},{9,8},{10,9},{11,1... | collective-permute-start | bytes 3080 | tf_op jit(solution)/shard_map/ppermute | solution.py:32
  42.3 12.9 %collective-permute-start.1 = (bf16[8,64]{1,0:T(8,128)(2,1)S(1)}, bf16[8,64]{1,0:T(8,128)(2,1)S(1)}, u32[]{:S(2)}, u32[]{:S(2)}) collective-permute-start(bf16[8,64]{1,0:T(8,128)(2,1)S(1)} %slice.77), channel_id=1, source_target_pairs={{0,1},{1,2},{2,3},{3,4},{4,5},{5,6},{6,7},{7,8},{8,9},{9,10},{10,1... | collective-permute-start | bytes 3080 | tf_op jit(solution)/shard_map/ppermute | solution.py:30
  47.8 23.6 %collective-permute-start.3 = (bf16[16,64,128]{2,1,0:T(8,128)(2,1)S(1)}, bf16[16,64,128]{2,1,0:T(8,128)(2,1)S(1)}, u32[]{:S(2)}, u32[]{:S(2)}) collective-permute-start(bf16[16,64,128]{2,1,0:T(8,128)(2,1)S(1)} %copy-done.19), channel_id=1, source_target_pairs={{0,31},{1,30},{2,29},{3,28},{4,27},{5,26},{6,25},{7,24},{8,23},{9,... | collective-permute-start | bytes 786440 | tf_op jit(solution)/shard_map/ppermute | solution.py:735
  72.2 39.2 %copy-start.2 = (bf16[2,256,256]{2,1,0:T(8,128)(2,1)S(1)}, bf16[2,256,256]{2,1,0:T(8,128)(2,1)}, u32[]{:S(2)}) copy-start(bf16[2,256,256]{2,1,0:T(8,128)(2,1)} %constant.125.clone.table) | copy-start | bytes 786436
  72.2 39.2 %copy-start.6 = (f32[32,32]{1,0:T(8,128)S(1)}, f32[32,32]{1,0:T(8,128)}, u32[]{:S(2)}) copy-start(f32[32,32]{1,0:T(8,128)} %constant.128.clone.edge) | copy-start | bytes 12292
  77.7 33.6 %all-to-all-start.2 = ((bf16[32,128,128]{2,1,0:T(8,128)(2,1)}), bf16[32,128,128]{2,1,0:T(8,128)(2,1)S(1)}, u32[]{:S(2)}, u32[]{:S(2)}) async-start(bf16[32,128,128]{2,1,0:T(8,128)(2,1)} %get-tuple-element.61), calls=%async_computation.2 | async-start | bytes 2097152 | tf_op jit(solution)/shard_map/all_to_all | solution.py:785
  114.1 11.9 %all-to-all-start.3 = ((bf16[32,8,256]{2,1,0:T(8,128)(2,1)}), bf16[32,8,256]{2,1,0:T(8,128)(2,1)S(1)}, u32[]{:S(2)}, u32[]{:S(2)}) async-start(bf16[32,8,256]{2,1,0:T(8,128)(2,1)} %bitcast.10), calls=%async_computation.3 | async-start | bytes 262144 | tf_op jit(solution)/shard_map/all_to_all | solution.py:785
  126.6 52.1 %copy-start.1 = (f32[32,72,128]{2,1,0:T(8,128)S(1)}, f32[32,72,128]{2,1,0:T(8,128)}, u32[]{:S(2)}) copy-start(f32[32,72,128]{2,1,0:T(8,128)} %get-tuple-element.68.green) | copy-start | bytes 3538948
  126.6 52.1 %copy-start.4 = (bf16[256,256]{1,0:T(8,128)(2,1)S(1)}, bf16[256,256]{1,0:T(8,128)(2,1)}, u32[]{:S(2)}) copy-start(bf16[256,256]{1,0:T(8,128)(2,1)} %constant.129.clone.both_in.both) | copy-start | bytes 393220
  126.6 52.1 %copy-start.5 = (f32[2,32,128]{2,1,0:T(8,128)S(1)}, f32[2,32,128]{2,1,0:T(8,128)}, u32[]{:S(2)}) copy-start(f32[2,32,128]{2,1,0:T(8,128)} %constant.130.clone.twiddle_in.twiddle) | copy-start | bytes 98308
  149.8 28.9 %all-to-all-start.5 = ((bf16[32,128,128]{2,1,0:T(8,128)(2,1)}), bf16[32,128,128]{2,1,0:T(8,128)(2,1)S(1)}, u32[]{:S(2)}, u32[]{:S(2)}) async-start(bf16[32,128,128]{2,1,0:T(8,128)(2,1)} %shard_map.183), calls=%async_computation.5 | async-start | bytes 2097152 | tf_op jit(solution)/shard_map/all_to_all | solution.py:785
  182.8 29.8 %all-to-all-start.6 = ((bf16[32,128,128]{2,1,0:T(8,128)(2,1)}), bf16[32,128,128]{2,1,0:T(8,128)(2,1)S(1)}, u32[]{:S(2)}, u32[]{:S(2)}) async-start(bf16[32,128,128]{2,1,0:T(8,128)(2,1)} %shard_map.184), calls=%async_computation.6 | async-start | bytes 2097152 | tf_op jit(solution)/shard_map/all_to_all | solution.py:785
  189.2 29.7 %collective-permute-start.6 = (f32[8,64]{1,0:T(8,128)S(1)}, f32[8,64]{1,0:T(8,128)S(1)}, u32[]{:S(2)}, u32[]{:S(2)}) collective-permute-start(f32[8,64]{1,0:T(8,128)S(1)} %get-tuple-element.73), channel_id=1, source_target_pairs={{0,1},{1,2},{2,3},{3,4},{4,5},{5,6},{6,7},{7,8},{8,9},{9,10},{10,1... | collective-permute-start | bytes 6152 | tf_op jit(solution)/shard_map/ppermute | solution.py:30
  191.4 27.6 %collective-permute-start.7 = (f32[8,64]{1,0:T(8,128)S(1)}, f32[8,64]{1,0:T(8,128)S(1)}, u32[]{:S(2)}, u32[]{:S(2)}) collective-permute-start(f32[8,64]{1,0:T(8,128)S(1)} %get-tuple-element.72), channel_id=1, source_target_pairs={{1,0},{2,1},{3,2},{4,3},{5,4},{6,5},{7,6},{8,7},{9,8},{10,9},{11,1... | collective-permute-start | bytes 6152 | tf_op jit(solution)/shard_map/ppermute | solution.py:32
  215.3 11.9 %all-to-all-start.7 = ((bf16[32,8,256]{2,1,0:T(8,128)(2,1)}), bf16[32,8,256]{2,1,0:T(8,128)(2,1)S(1)}, u32[]{:S(2)}, u32[]{:S(2)}) async-start(bf16[32,8,256]{2,1,0:T(8,128)(2,1)} %bitcast.21), calls=%async_computation.7 | async-start | bytes 262144 | tf_op jit(solution)/shard_map/all_to_all | solution.py:785
  (11 other events, 139.5 us)
